TPU v7x, 32 devices: a whole 2x2x4 slice. The times are simulated.
32 devices in a mesh: grp: 4 (over x, core), col: 4 (over z), dev: 2 (over y).
Axes of the slice: x: 2, y: 2, z: 4, core: 2. Of those that a mesh axis runs over, the one named last changes fastest.
Arguments:
- rho_re: float32 [12288, 512], P(('grp', 'col'), 'dev'), may hold values from -0.078125 to 0.078125
- rho_im: float32 [12288, 512], P(('grp', 'col'), 'dev'), may hold values from -0.078125 to 0.078125
- coulomb: float32 [12288], P(('grp', 'col', 'dev')), may hold values from 0.4 to 1.6
- chi_prev: float32 [2, 4, 4, 768, 12288], P(None, None, 'col', 'dev', 'grp'), may hold values from -0.013671875 to 0.013671875
- source: float32 [12288, 128], P(('grp', 'col', 'dev')), may hold values from -6 to 6
- band_v: int32 [512], P('dev'), may hold values from 0 to 127
- band_c: int32 [512], P('dev'), may hold values from 128 to 255
- band_energy: float32 [256], replicated, may hold values from -2 to 2.5, as said below
- band_occ: float32 [256], replicated, may hold values from 0 to 1, as said below
Outputs:
- screened_re: float32 [12288, 128], P(('grp', 'col', 'dev'))
- screened_im: float32 [12288, 128], P(('grp', 'col', 'dev'))
Inputs may be any that keep to these rules, and one draw needn't show every extreme that they name: `band_v`: the valence bands are the first 128. `band_energy`: the first 128 bands lie below -0.1, the others above 0.2. `band_occ`: the first 128 bands have occupations of 0.7 or more, the others of 0.3 or less.
All inputs are finite; a program needn't handle non-finite values.
Results may differ from a plain program's by a relative error of at most 0.00013.
Values sent between devices are 32-bit elements; how exact they have to be, the bound alone decides.
No kernel may reach another device: no remote copies, remote signals or barrier semaphores. Data moves between devices by JAX's collectives and lax.ppermute only.
A program may use at most 128 MiB of HBM per device.

v0:
```python
import jax
import jax.numpy as jnp
from jax import lax
from jax.sharding import PartitionSpec as P

ITERS = 2


frequency = 0.8
damping = 0.5


def contract(left, right):
    return lax.dot_general(
        left,
        right,
        (((0,), (0,)), ((), ())),
        precision=lax.Precision.HIGHEST,
        preferred_element_type=jnp.float32,
    )


def matmul(left, right):
    return jnp.dot(left, right, precision=lax.Precision.HIGHEST, preferred_element_type=jnp.float32)


def lookup(bands, table):
    band_index = jnp.arange(table.shape[0], dtype=jnp.int32)
    match = bands[:, None] == band_index[None, :]
    return jnp.sum(jnp.where(match, table[None, :], 0.0), axis=1)


def shards(rho_re, rho_im, coulomb, chi_prev, source, band_v, band_c, band_energy, band_occ):
    delta = lookup(band_c, band_energy) - lookup(band_v, band_energy)
    filling = lookup(band_v, band_occ) - lookup(band_c, band_occ)
    weight = filling * 2.0 * delta / (delta * delta + frequency * frequency)
    slab = rho_re.shape[0]
    width = source.shape[1]
    row_block = chi_prev.shape[4]
    my_cols = chi_prev.shape[1] * chi_prev.shape[3]
    previous = chi_prev.reshape(2, my_cols, row_block)
    tile_re = previous[0]
    tile_im = previous[1]
    scale = coulomb[:, None]
    real_part = source
    imag_part = jnp.zeros_like(source)
    for sweep in range(ITERS):
        scaled = jnp.concatenate([scale * real_part, scale * imag_part], axis=1)
        piece = lax.all_gather(scaled, "grp", axis=0, tiled=True)
        swapped = jnp.concatenate([-piece[:, width:], piece[:, :width]], axis=1)
        total = contract(tile_re, piece) + contract(tile_im, swapped)
        slab_scaled = lax.all_gather(scaled, "dev", axis=0, tiled=True)
        slab_re = slab_scaled[:, :width]
        slab_im = slab_scaled[:, width:]
        proj_re = contract(rho_re, slab_re) + contract(rho_im, slab_im)
        proj_im = contract(rho_re, slab_im) - contract(rho_im, slab_re)
        summed = lax.psum(jnp.concatenate([proj_re, proj_im], axis=1), ("grp", "col"))
        weighted = weight[:, None] * summed
        weighted_re = weighted[:, :width]
        weighted_im = weighted[:, width:]
        added_re = -(matmul(rho_re, weighted_re) - matmul(rho_im, weighted_im))
        added_im = -(matmul(rho_re, weighted_im) + matmul(rho_im, weighted_re))
        offset = lax.axis_index("col") * slab
        current = lax.dynamic_slice(total, (offset, 0), (slab, 2 * width))
        total = lax.dynamic_update_slice(
            total, current + jnp.concatenate([added_re, added_im], axis=1), (offset, 0)
        )
        mine = lax.psum_scatter(total, ("col", "dev"), scatter_dimension=0, tiled=True)
        image_re = scale * mine[:, :width]
        image_im = scale * mine[:, width:]
        real_part = real_part + damping * (source + image_re - real_part)
        imag_part = imag_part + damping * (image_im - imag_part)
    return (real_part, imag_part)


def solution(mesh):
    placed = (
        P(("grp", "col"), "dev"),
        P(("grp", "col"), "dev"),
        P(("grp", "col", "dev")),
        P(None, None, "col", "dev", "grp"),
        P(("grp", "col", "dev"), None),
        P("dev"),
        P("dev"),
        P(),
        P(),
    )
    return jax.shard_map(
        shards,
        mesh=mesh,
        in_specs=placed,
        out_specs=(P(("grp", "col", "dev"), None), P(("grp", "col", "dev"), None)),
        check_vma=False,
    )
```

profile of v0, /device:TPU:0, one launch (start us, length us, event | category | flops | bytes accessed | tf_op | source)
XLA Modules:
  0.0 479.5 jit_solution(3537143329620945897)
XLA Ops:
  8.1 0.8 broadcast_multiply_fusion.3
  8.9 1.1 copy.21
  10.7 12.8 %all_gather.13 = f32[768,256]{0,1:T(8,128)S(1)} all-gather(f32[384,256]{0,1:T(8,128)S(1)} %pad_maximum_fusion), channel_id=1, replica_groups=mesh['grp'=4,'col'=4,'dev'=2] {'dev'}, dimensions={0}, use_global_device_ids=true | all-gather | bytes 1179648 | tf_op jit(solution)/shard_map/all_gather | solution.py:52
  27.0 26.2 %fusion.57 = (f32[1,4,1,384,3072]{4,3,2,1,0:T(8,128)}, f32[1,4,1,384,3072]{4,3,2,1,0:T(8,128)}) fusion(f32[2,4,1,384,3072]{4,3,2,1,0:T(8,128)} %param.12), kind=kLoop, calls=%fused_computation.92 | loop fusion | bytes 75497472 | tf_op jit(solution)/shard_map/slice | solution.py:43
  53.6 65.9 %all-reduce.3.cloned.1.call-done = f32[256,256]{0,1:T(8,128)} async-done(((f32[256,256]{0,1:T(8,128)}), f32[256,256]{0,1:T(8,128)}) %all-reduce.3.cloned.1.call-update) | async-done | bytes 262160 | tf_op jit(solution)/shard_map/psum | solution.py:57
  119.5 1.0 broadcast_multiply_fusion.1
  120.4 0.9 fusion.49
  121.4 0.9 fusion.53
  122.3 0.9 fusion.11
  123.2 0.9 fusion.13
  124.2 1.6 slice_negate_fusion.1
  126.1 19.4 %fusion.58 = f32[256,3072]{1,0:T(8,128)S(1)} fusion(f32[1536,256]{0,1:T(8,128)S(1)} %copy-done.3, f32[1536,3072]{1,0:T(8,128)} %bitcast.48), kind=kOutput, calls=%fused_computation.93 | convolution fusion | flops 14495514624 | bytes 23592960 | tf_op jit(solution)/shard_map/dot_general | solution.py:14
  145.5 16.8 %convolution_add_fusion.1 = f32[256,3072]{1,0:T(8,128)S(1)} fusion(f32[256,3072]{1,0:T(8,128)S(1)} %fusion.58, f32[1536,3072]{1,0:T(8,128)S(1)} %bitcast.47, f32[1536,128]{0,1:T(8,128)S(1)} %get-tuple-element.15, f32[1536,128]{0,1:T(8,128)S(1)} %get-tuple-element.14), kind=kOutput, calls=%fused_computation.1 | convolution fusion | flops 14496694272 | bytes 26738688 | tf_op jit(solution)/shard_map/dot_general | solution.py:14
  162.3 1.6 copy.26
  164.0 1.1 fusion.18
  165.1 74.9 %reduce-scatter.3.cloned.1.call-done = f32[384,256]{0,1:T(8,128)} async-done(((f32[3072,256]{0,1:T(8,128)}), f32[384,256]{0,1:T(8,128)}) %reduce-scatter.3.cloned.1.call-update) | async-done | bytes 393232 | tf_op jit(solution)/shard_map/reduce_scatter | solution.py:68
  240.0 1.1 fusion.42
  241.1 10.8 %all_gather.15 = f32[768,256]{0,1:T(8,128)S(1)} all-gather(f32[384,256]{0,1:T(8,128)S(1)} %pad_maximum_fusion.1), channel_id=1, replica_groups=mesh['grp'=4,'col'=4,'dev'=2] {'dev'}, dimensions={0}, use_global_device_ids=true | all-gather | bytes 1179648 | tf_op jit(solution)/shard_map/all_gather | solution.py:52
  255.5 90.7 %all-reduce.5.cloned.1.call-done = f32[256,256]{0,1:T(8,128)} async-done(((f32[256,256]{0,1:T(8,128)}), f32[256,256]{0,1:T(8,128)}) %all-reduce.5.cloned.1.call-update) | async-done | bytes 262160 | tf_op jit(solution)/shard_map/psum | solution.py:57
  346.2 1.0 broadcast_multiply_fusion
  347.2 0.9 fusion.43
  348.1 0.9 fusion.47
  349.0 0.9 fusion.7
  350.0 0.9 fusion.9
  350.9 21.6 %fusion.59 = f32[256,3072]{1,0:T(8,128)S(1)} fusion(f32[1536,256]{0,1:T(8,128)} %all-gather.5.cloned.1.call-done, f32[1536,3072]{1,0:T(8,128)} %bitcast.49), kind=kOutput, calls=%fused_computation.94 | convolution fusion | flops 14495514624 | bytes 23592960 | tf_op jit(solution)/shard_map/dot_general | solution.py:14
  372.7 19.4 %convolution_add_fusion = f32[256,3072]{1,0:T(8,128)S(1)} fusion(f32[256,3072]{1,0:T(8,128)S(1)} %fusion.59, f32[1536,3072]{1,0:T(8,128)} %bitcast.46, f32[1536,128]{0,1:T(8,128)S(1)} %get-tuple-element.13, f32[1536,128]{0,1:T(8,128)S(1)} %get-tuple-element.12), kind=kOutput, calls=%fused_computation | convolution fusion | flops 14496694272 | bytes 26738688 | tf_op jit(solution)/shard_map/dot_general | solution.py:14
  392.1 1.6 copy.28
  393.7 1.1 fusion.19
  394.8 74.8 %reduce-scatter.5.cloned.1.call-done = f32[384,256]{0,1:T(8,128)} async-done(((f32[3072,256]{0,1:T(8,128)}), f32[384,256]{0,1:T(8,128)}) %reduce-scatter.5.cloned.1.call-update) | async-done | bytes 393232 | tf_op jit(solution)/shard_map/reduce_scatter | solution.py:68
  469.7 1.1 fusion.36
  470.8 0.8 copy.24
  471.6 0.8 copy.23
  (57 shorter events, 8.6 us)
Async XLA Ops:
  8.0 15.5 %copy-start = (f32[768,256]{1,0:T(8,128)S(1)}, f32[768,256]{1,0:T(8,128)}, u32[]{:S(2)}) copy-start(f32[768,256]{1,0:T(8,128)} %param.9) | copy-start | bytes 2359300
  8.0 16.5 %copy-start.2 = (f32[768,256]{1,0:T(8,128)S(1)}, f32[768,256]{1,0:T(8,128)}, u32[]{:S(2)}) copy-start(f32[768,256]{1,0:T(8,128)} %param.10) | copy-start | bytes 2359300
  8.0 111.4 %all-reduce.3.cloned.1.call-start = ((), (), s32[]{:S(2)}) async-start(), calls=%async_computation.3 | async-start | bytes 524288 | tf_op jit(solution)/shard_map/psum | solution.py:57
  10.7 14.9 %copy-start.5 = (f32[384,256]{0,1:T(8,128)}, f32[384,256]{0,1:T(8,128)S(1)}, u32[]{:S(2)}) copy-start(f32[384,256]{0,1:T(8,128)S(1)} %pad_maximum_fusion) | copy-start | bytes 1179652
  26.3 97.8 %all-gather.3.cloned.1.call-start = ((), (), s32[]{:S(2)}) async-start(), calls=%async_computation.2 | async-start | bytes 1966080 | tf_op jit(solution)/shard_map/all_gather | solution.py:49
  26.9 26.3 %copy-start.9 = (s32[256]{0:T(256)S(1)}, s32[256]{0:T(256)}, u32[]{:S(2)}) copy-start(s32[256]{0:T(256)} %param.15) | copy-start | bytes 3076
  26.9 26.3 %copy-start.10 = (f32[256]{0:T(256)S(1)}, f32[256]{0:T(256)}, u32[]{:S(2)}) copy-start(f32[256]{0:T(256)} %param.17) | copy-start | bytes 3076
  26.9 26.3 %copy-start.11 = (s32[256]{0:T(256)S(1)}, s32[256]{0:T(256)}, u32[]{:S(2)}) copy-start(s32[256]{0:T(256)} %param.14) | copy-start | bytes 3076
  27.0 26.3 %copy-start.12 = (f32[256]{0:T(256)S(1)}, f32[256]{0:T(256)}, u32[]{:S(2)}) copy-start(f32[256]{0:T(256)} %param.16) | copy-start | bytes 3076
  27.0 213.0 %reduce-scatter.3.cloned.1.call-start = ((), (), s32[]{:S(2)}) async-start(), calls=%async_computation.4 | async-start | bytes 3538944 | tf_op jit(solution)/shard_map/reduce_scatter | solution.py:68
  124.2 1.9 copy-start.3
  126.1 19.4 %copy-start.1 = (f32[1,4,1,384,3072]{4,3,2,1,0:T(8,128)S(1)}, f32[1,4,1,384,3072]{4,3,2,1,0:T(8,128)}, u32[]{:S(2)}) copy-start(f32[1,4,1,384,3072]{4,3,2,1,0:T(8,128)} %get-tuple-element.10) | copy-start | bytes 56623108
  164.0 76.0 %copy-start.8 = (f32[384]{0:T(512)S(1)}, f32[384]{0:T(512)}, u32[]{:S(2)}) copy-start(f32[384]{0:T(512)} %param.11) | copy-start | bytes 4612
  165.0 181.2 %all-reduce.5.cloned.1.call-start = ((), (), s32[]{:S(2)}) async-start(), calls=%async_computation.6 | async-start | bytes 524288 | tf_op jit(solution)/shard_map/psum | solution.py:57
  241.1 13.0 %copy-start.6 = (f32[384,256]{0,1:T(8,128)}, f32[384,256]{0,1:T(8,128)S(1)}, u32[]{:S(2)}) copy-start(f32[384,256]{0,1:T(8,128)S(1)} %pad_maximum_fusion.1) | copy-start | bytes 1179652
  254.9 96.1 %all-gather.5.cloned.1.call-start = ((), (), s32[]{:S(2)}) async-start(), calls=%async_computation.5 | async-start | bytes 1966080 | tf_op jit(solution)/shard_map/all_gather | solution.py:49
  255.5 214.2 %reduce-scatter.5.cloned.1.call-start = ((), (), s32[]{:S(2)}) async-start(), calls=%async_computation.7 | async-start | bytes 3538944 | tf_op jit(solution)/shard_map/reduce_scatter | solution.py:68
  350.9 21.7 %copy-start.4 = (f32[1536,256]{0,1:T(8,128)S(1)}, f32[1536,256]{0,1:T(8,128)}, u32[]{:S(2)}) copy-start(f32[1536,256]{0,1:T(8,128)} %all-gather.5.cloned.1.call-done) | copy-start | bytes 4718596
  393.7 75.9 %copy-start.7 = (f32[384,256]{0,1:T(8,128)S(1)}, f32[384,256]{0,1:T(8,128)}, u32[]{:S(2)}) copy-start(f32[384,256]{0,1:T(8,128)} %reduce-scatter.3.cloned.1.call-done) | copy-start | bytes 1179652
Sparse Core Ops, SparseCore 0:
  26.5 92.9 all-reduce.2
  165.2 74.7 reduce-scatter.2
  255.0 91.1 all-reduce.4
  394.9 74.6 reduce-scatter.4
Sparse Core Ops, SparseCore 1:
  28.4 21.2 all-gather.2
  256.9 19.4 all-gather.4
where the time goes:
time: 480 us
  waiting for transfers between devices  308 us (64%)
  matrix products  88.8 us (18%)
  local copies, waits for them, and re-layouts  32.5 us (7%)
  blocking collectives  23.6 us (5%)
  between operations  15.6 us (3%)
  other arithmetic  11.3 us (2%)
    psum x2, waiting for transfers between devices, shards(): lax.psum(jnp.concatenate([proj_re, proj_im], axis=1), ('grp', 'col'))  157 us
    reduce_scatter x2, waiting for transfers between devices, shards(): lax.psum_scatter(total, ('col', 'dev'), scatter_dimension=0, tiled=True)  150 us
    dot_general x12, matrix products, contract(): lax.dot_general(left, right, (((0,), (0,)), ((), ())), precision=lax.Prec...  81.5 us
    slice x1, local copies, waits for them, and re-layouts, shards(): tile_im = previous[1]  26.2 us
    all_gather x2, blocking collectives, shards(): slab_scaled = lax.all_gather(scaled, 'dev', axis=0, tiled=True)  23.6 us
  transfers between devices with their start and end apart: 6, of which 4 were waited for; matrix products, arithmetic and copies ran while one was open for 7% of the time, Pallas kernels for 0%

commit v1 on v0

--- a/solution.py
+++ b/solution.py
@@ -1,6 +1,10 @@
+import functools
+
 import jax
 import jax.numpy as jnp
 from jax import lax
+from jax.experimental import pallas as pl
+from jax.experimental.pallas import tpu as pltpu
 from jax.sharding import PartitionSpec as P
 
 ITERS = 2
@@ -8,6 +12,19 @@
 
 frequency = 0.8
 damping = 0.5
+MIB = 1 << 20
+
+
+def lookup(bands, table):
+    band_index = jnp.arange(table.shape[0], dtype=jnp.int32)
+    match = bands[None, :] == band_index[:, None]
+    return jnp.sum(jnp.where(match, table[:, None], 0.0), axis=0)
+
+
+def pair_weight(band_v, band_c, band_energy, band_occ):
+    delta = lookup(band_c, band_energy) - lookup(band_v, band_energy)
+    filling = lookup(band_v, band_occ) - lookup(band_c, band_occ)
+    return filling * 2.0 * delta / (delta * delta + frequency * frequency)
 
 
 def contract(left, right):
@@ -24,23 +41,13 @@
     return jnp.dot(left, right, precision=lax.Precision.HIGHEST, preferred_element_type=jnp.float32)
 
 
-def lookup(bands, table):
-    band_index = jnp.arange(table.shape[0], dtype=jnp.int32)
-    match = bands[:, None] == band_index[None, :]
-    return jnp.sum(jnp.where(match, table[None, :], 0.0), axis=1)
-
-
-def shards(rho_re, rho_im, coulomb, chi_prev, source, band_v, band_c, band_energy, band_occ):
-    delta = lookup(band_c, band_energy) - lookup(band_v, band_energy)
-    filling = lookup(band_v, band_occ) - lookup(band_c, band_occ)
-    weight = filling * 2.0 * delta / (delta * delta + frequency * frequency)
+def general(rho_re, rho_im, coulomb, chi_prev, source, band_v, band_c, band_energy, band_occ):
+    weight = pair_weight(band_v, band_c, band_energy, band_occ)
     slab = rho_re.shape[0]
     width = source.shape[1]
     row_block = chi_prev.shape[4]
     my_cols = chi_prev.shape[1] * chi_prev.shape[3]
     previous = chi_prev.reshape(2, my_cols, row_block)
-    tile_re = previous[0]
-    tile_im = previous[1]
     scale = coulomb[:, None]
     real_part = source
     imag_part = jnp.zeros_like(source)
@@ -48,7 +55,7 @@
         scaled = jnp.concatenate([scale * real_part, scale * imag_part], axis=1)
         piece = lax.all_gather(scaled, "grp", axis=0, tiled=True)
         swapped = jnp.concatenate([-piece[:, width:], piece[:, :width]], axis=1)
-        total = contract(tile_re, piece) + contract(tile_im, swapped)
+        total = contract(previous[0], piece) + contract(previous[1], swapped)
         slab_scaled = lax.all_gather(scaled, "dev", axis=0, tiled=True)
         slab_re = slab_scaled[:, :width]
         slab_im = slab_scaled[:, width:]
@@ -73,6 +80,326 @@
     return (real_part, imag_part)
 
 
+def split(value):
+    high = value.astype(jnp.bfloat16)
+    return high, (value - high.astype(jnp.float32)).astype(jnp.bfloat16)
+
+
+def dot(left, right):
+    return jnp.dot(left, right, preferred_element_type=jnp.float32)
+
+
+def dot_nt(left, right):
+    return lax.dot_general(
+        left, right, (((1,), (1,)), ((), ())), preferred_element_type=jnp.float32
+    )
+
+
+def dot3(stacked, rows, right, product=dot):
+    high, low = split(right)
+    both = product(stacked, high)
+    return both[:rows] + both[rows:] + product(stacked[:rows], low)
+
+
+def stack(value):
+    high, low = split(value)
+    return jnp.concatenate([high, low], axis=0)
+
+
+def call(kernel, name, scalars, grid, in_specs, out_specs, out_shape, scratch, cost, *operands):
+    return pl.pallas_call(
+        kernel,
+        name=name,
+        grid_spec=pltpu.PrefetchScalarGridSpec(
+            num_scalar_prefetch=1,
+            grid=grid,
+            in_specs=in_specs,
+            out_specs=out_specs,
+            scratch_shapes=scratch,
+        ),
+        out_shape=out_shape,
+        cost_estimate=pl.CostEstimate(flops=cost[0], bytes_accessed=cost[1], transcendentals=0),
+        compiler_params=pltpu.CompilerParams(
+            vmem_limit_bytes=36 * MIB, dimension_semantics=("arbitrary",) * len(grid)
+        ),
+    )(scalars, *operands)
+
+
+def whole(*shape):
+    return pl.BlockSpec(shape, lambda *_: (0,) * len(shape))
+
+
+def shaped(*shape):
+    return jax.ShapeDtypeStruct(shape, jnp.float32)
+
+
+def apply_block(panel, rows, width, chi, out, start=None):
+    depth = chi.shape[1] * chi.shape[2]
+    part_re = dot3(panel[...], rows, chi[0].reshape(depth, chi.shape[3]))
+    part_im = dot3(panel[...], rows, chi[1].reshape(depth, chi.shape[3]))
+    if rows == 2 * width:
+        image_re = part_re[:width] - part_im[width:]
+        image_im = part_re[width:] + part_im[:width]
+    else:
+        image_re = part_re
+        image_im = part_im
+    if start is not None:
+        image_re = start[:width] + image_re
+        image_im = start[width:] + image_im
+    out[:width] = image_re
+    out[width:] = image_im
+
+
+def fill_panel(panel, core, near, far):
+    rows, half = near.shape
+    for piece, place in ((near, core), (far, 1 - core)):
+        high, low = split(piece[...])
+        at = pl.ds(pl.multiple_of(place * half, half), half)
+        panel[:rows, at] = high
+        panel[rows:, at] = low
+
+
+def begin_kernel(scalars, source, coulomb, bare, scaled):
+    turned = source[...].T
+    bare[...] = turned
+    scaled[...] = turned * coulomb[...]
+
+
+def local_kernel(width, scalars, near, far, chi, out, panel):
+    @pl.when(pl.program_id(0) == 0)
+    def _():
+        fill_panel(panel, scalars[1], near, far)
+
+    apply_block(panel, near.shape[0], width, chi, out)
+
+
+def half_kernel(width, scalars, near, far, chi, start, *rest):
+    *outs, panel = rest
+    step = pl.program_id(0)
+
+    @pl.when(step == 0)
+    def _():
+        fill_panel(panel, scalars[1], near, far)
+
+    for index, out in enumerate(outs):
+
+        @pl.when(step == index)
+        def _():
+            apply_block(panel, near.shape[0], width, chi, out, start)
+
+
+def slab_kernel(width, scalars, near, far, chi, start, *rest):
+    *outs, panel, full = rest
+    step = pl.program_id(0)
+    half = near.shape[1]
+
+    @pl.when(step == 0)
+    def _():
+        fill_panel(panel, scalars[1], near, far)
+
+    apply_block(panel, near.shape[0], width, chi, full, start)
+    for index in range(len(outs) // 2):
+
+        @pl.when(step == index)
+        def _():
+            for place, out in zip((1 - scalars[3], scalars[3]), outs[2 * index : 2 * index + 2]):
+                out[...] = full[:, pl.ds(pl.multiple_of(place * half, half), half)]
+
+
+def project_kernel(width, scalars, near, far, rho_re, rho_im, keep, send, full):
+    rows, half = near.shape
+    dev, core = scalars[3], scalars[1]
+    total_re = total_im = None
+    for piece, place in ((near, dev), (far, 1 - dev)):
+        at = pl.ds(pl.multiple_of(place * half, half), half)
+        panel = stack(piece[...])
+        by_re = dot3(panel, rows, rho_re[at])
+        by_im = dot3(panel, rows, rho_im[at])
+        total_re = by_re if total_re is None else total_re + by_re
+        total_im = by_im if total_im is None else total_im + by_im
+    if rows == 2 * width:
+        full[:width] = total_re[:width] + total_im[width:]
+        full[width:] = total_re[width:] - total_im[:width]
+    else:
+        full[:width] = total_re
+        full[width:] = -total_im
+    keep[...] = full[pl.ds(pl.multiple_of(core * width, width), width)]
+    send[...] = full[pl.ds(pl.multiple_of((1 - core) * width, width), width)]
+
+
+def spread_kernel(width, scalars, near, far, weight, rho_re, rho_im, first, second, first_out, second_out, full):
+    half = first.shape[1]
+    dev, core = scalars[3], scalars[1]
+    full[pl.ds(pl.multiple_of(core * width, width), width)] = weight[...] * near[...]
+    full[pl.ds(pl.multiple_of((1 - core) * width, width), width)] = weight[...] * far[...]
+    panel = stack(full[...])
+    for place, given, out in ((1 - dev, first, first_out), (dev, second, second_out)):
+        at = pl.ds(pl.multiple_of(place * half, half), half)
+        by_re = dot3(panel, 2 * width, rho_re[at], dot_nt)
+        by_im = dot3(panel, 2 * width, rho_im[at], dot_nt)
+        out[:width] = given[:width] - (by_re[:width] - by_im[width:])
+        out[width:] = given[width:] - (by_re[width:] + by_im[:width])
+
+
+def end_kernel(width, scalars, own, by_dev, by_near, by_far, iterate, bare, coulomb, out_re, out_im):
+    image = coulomb[...] * (own[...] + by_dev[...] + by_near[...] + by_far[...])
+    real_part = iterate[:width]
+    imag_part = iterate[width:]
+    real_part = real_part + damping * (bare[...] + image[:width] - real_part)
+    imag_part = imag_part + damping * (image[width:] - imag_part)
+    out_re[...] = real_part.T
+    out_im[...] = imag_part.T
+
+
+def exchange(value, axis, flip):
+    size = lax.axis_size(axis)
+    return lax.ppermute(value, axis, [(i, i ^ flip) for i in range(size)])
+
+
+def exchanged(rho_re, rho_im, coulomb, chi_prev, source, band_v, band_c, band_energy, band_occ):
+    weight = pair_weight(band_v, band_c, band_energy, band_occ)[None, :]
+    half, width = source.shape
+    pairs = rho_re.shape[1]
+    slab = 2 * half
+    panel_rows = 2 * width
+    parts = chi_prev.shape[0]
+    row_block = chi_prev.shape[4]
+    n_slab = row_block // slab
+    last = n_slab - 1
+    grp = lax.axis_index("grp")
+    scalars = jnp.stack([grp // 2, grp % 2, lax.axis_index("col"), lax.axis_index("dev")]).astype(jnp.int32)
+    scale = coulomb[None, :]
+
+    bare, scaled = call(
+        begin_kernel, "begin", scalars, (1,),
+        [whole(half, width), whole(1, half)],
+        [whole(width, half)] * 2,
+        [shaped(width, half)] * 2,
+        [], (0, 12 * half * width),
+        source, scale,
+    )
+
+    def chi_block(columns, pair, place):
+        return pl.BlockSpec((parts, 2, None, half, columns), lambda i, s: (0, pair(s), 0, 0, place(i, s)))
+
+    def products(blocks, rows, columns):
+        flops = 3 * 2 * 2 * blocks * rows * slab * columns
+        return flops, 4 * blocks * columns * (parts * slab + panel_rows)
+
+    here = lambda s: s[0]
+    there = lambda s: 1 - s[0]
+
+    def image(scaled):
+        rows = scaled.shape[0]
+        from_x = exchange(scaled, "grp", 2)
+        from_core = exchange(scaled, "grp", 1)
+        from_dev = exchange(scaled, "dev", 1)
+        panel = pltpu.VMEM((2 * rows, slab), jnp.bfloat16)
+        pieces = [whole(rows, half)] * 2
+
+        start = call(
+            functools.partial(local_kernel, width), "near_half", scalars, (n_slab,),
+            pieces + [chi_block(slab, here, lambda i, s: s[2] ^ (last - i))],
+            pl.BlockSpec((None, panel_rows, slab), lambda i, s: (i, 0, 0)),
+            shaped(n_slab, panel_rows, slab),
+            [panel], products(n_slab, rows, slab),
+            scaled, from_core, chi_prev,
+        )
+
+        keep, send = call(
+            functools.partial(project_kernel, width), "project", scalars, (1,),
+            pieces + [whole(slab, pairs)] * 2,
+            [whole(width, pairs)] * 2,
+            [shaped(width, pairs)] * 2,
+            [pltpu.VMEM((panel_rows, pairs), jnp.float32)],
+            (3 * 4 * rows * slab * pairs, 8 * slab * pairs),
+            scaled, from_dev, rho_re, rho_im,
+        )
+        total = keep + exchange(send, "grp", 1)
+        total = total + exchange(total, "grp", 2)
+        total = total + exchange(total, "col", 1)
+        total = total + exchange(total, "col", 2)
+        other = exchange(total, "grp", 1)
+
+        from_x_core = exchange(from_x, "grp", 1)
+
+        def by_halves(places):
+            def at(i, s):
+                where = [2 * (s[2] ^ j) + (1 - s[3] if sent else s[3]) for j, sent in places]
+                found = where[-1]
+                for index in range(len(places) - 2, -1, -1):
+                    found = jnp.where(i == index, where[index], found)
+                return found
+
+            def begun(i, s):
+                row, col = last - places[-1][0], (1 - s[3] if places[-1][1] else s[3])
+                for index in range(len(places) - 2, -1, -1):
+                    j, sent = places[index]
+                    row = jnp.where(i == index, last - j, row)
+                    col = jnp.where(i == index, 1 - s[3] if sent else s[3], col)
+                return row, 0, col
+
+            return call(
+                functools.partial(half_kernel, width), f"far_half_{len(places)}", scalars, (len(places),),
+                pieces + [chi_block(half, there, at), pl.BlockSpec((None, panel_rows, half), begun)],
+                [whole(panel_rows, half)] * len(places),
+                [shaped(panel_rows, half)] * len(places),
+                [panel], products(len(places), rows, half),
+                from_x, from_x_core, chi_prev, start,
+            )
+
+        def by_slabs(first, count):
+            return call(
+                functools.partial(slab_kernel, width), f"far_slab_{count}", scalars, (count,),
+                pieces + [
+                    chi_block(slab, there, lambda i, s: s[2] ^ (first - i)),
+                    pl.BlockSpec((None, panel_rows, slab), lambda i, s: (last - first + i, 0, 0)),
+                ],
+                [whole(panel_rows, half)] * (2 * count),
+                [shaped(panel_rows, half)] * (2 * count),
+                [panel, pltpu.VMEM((panel_rows, slab), jnp.float32)],
+                products(count, rows, slab),
+                from_x, from_x_core, chi_prev, start,
+            )
+
+        (send3,) = by_halves([(3, True)])
+        got3 = exchange(send3, "dev", 1)
+        send2, keep2, keep3 = by_halves([(2, True), (2, False), (3, False)])
+        got2 = exchange(send2, "dev", 1)
+        send1, keep1, send0, keep0 = by_slabs(1, 2)
+        got1 = exchange(send1, "dev", 1)
+        send0, keep0 = call(
+            functools.partial(spread_kernel, width), "spread", scalars, (1,),
+            [whole(width, pairs)] * 2 + [whole(1, pairs)] + [whole(slab, pairs)] * 2 + [whole(panel_rows, half)] * 2,
+            [whole(panel_rows, half)] * 2,
+            [shaped(panel_rows, half)] * 2,
+            [pltpu.VMEM((panel_rows, pairs), jnp.float32)],
+            (3 * 4 * panel_rows * slab * pairs, 8 * slab * pairs),
+            total, other, weight, rho_re, rho_im, send0, keep0,
+        )
+        got0 = exchange(send0, "dev", 1)
+        across = exchange(keep3 + got3, "col", 1)
+        far = exchange(keep2 + got2 + across, "col", 2)
+        near = exchange(keep1 + got1, "col", 1)
+        return keep0, got0, near, far
+
+    own, by_dev, by_near, by_far = image(scaled)
+    pulled = scale * (own + by_dev + by_near + by_far)
+    real_part = bare + damping * (bare + pulled[:width] - bare)
+    imag_part = damping * pulled[width:]
+    iterate = jnp.concatenate([real_part, imag_part], axis=0)
+    for sweep in range(1, ITERS):
+        own, by_dev, by_near, by_far = image(scale * iterate)
+    return call(
+        functools.partial(end_kernel, width), "end", scalars, (1,),
+        [whole(panel_rows, half)] * 5 + [whole(width, half), whole(1, half)],
+        [whole(half, width)] * 2,
+        [shaped(half, width)] * 2,
+        [], (0, 4 * 8 * half * panel_rows),
+        own, by_dev, by_near, by_far, iterate, bare, scale,
+    )
+
+
 def solution(mesh):
     placed = (
         P(("grp", "col"), "dev"),
@@ -85,6 +412,14 @@
         P(),
         P(),
     )
+
+    def shards(*blocks):
+        half, width = blocks[4].shape
+        pairs = blocks[0].shape[1]
+        paired = mesh.shape["grp"] == 4 and mesh.shape["col"] == 4 and mesh.shape["dev"] == 2
+        tiled = half % 128 == 0 and width % 128 == 0 and pairs % 128 == 0
+        return (exchanged if paired and tiled and ITERS == 2 else general)(*blocks)
+
     return jax.shard_map(
         shards,
         mesh=mesh,

time: 480 us -> 164 us (0.34)
  waiting for transfers between devices: 308 us -> 66 us
  matrix products: 88.8 us -> 0 us
  Pallas kernels: 0 us -> 61.6 us
  starting transfers between devices: 0.25 us -> 29.5 us
  local copies, waits for them, and re-layouts: 32.5 us -> 3.92 us
  blocking collectives: 23.6 us -> 0 us
  between operations: 15.6 us -> 1.02 us
  other arithmetic: 11.3 us -> 0.87 us
    psum x2 -> x0, waiting for transfers between devices: 157 us -> none  [shards(): lax.psum(jnp.concatenate([proj_re, proj_im], axis=1), ('grp', 'col'))]
    reduce_scatter x2 -> x0, waiting for transfers between devices: 150 us -> none  [shards(): lax.psum_scatter(total, ('col', 'dev'), scatter_dimension=0, tiled=True)]
    dot_general x20 -> x0, matrix products: 88.8 us -> none  [the longest x12 81.5 us: contract(): lax.dot_general(left, right, (((0,), (0,)), ((), ())), precision=lax.Prec...]
    ppermute x0 -> x32, waiting for transfers between devices: none -> 66 us  [exchange(): return lax.ppermute(value, axis, [(i, i ^ flip) for i in range(size)])]
    pallas_call x0 -> x14, Pallas kernels: none -> 61.6 us  [call(): pl.pallas_call(kernel, name=name, grid_spec=pltpu.PrefetchScalarGridSpec(...]
    ppermute x0 -> x32, starting transfers between devices: none -> 29.5 us  [exchange(): return lax.ppermute(value, axis, [(i, i ^ flip) for i in range(size)])]
    slice x1 -> x0, local copies, waits for them, and re-layouts: 26.2 us -> none  [shards(): tile_im = previous[1]]
    all_gather x2 -> x0, blocking collectives: 23.6 us -> none  [shards(): slab_scaled = lax.all_gather(scaled, 'dev', axis=0, tiled=True)]
  transfers between devices with their start and end apart: 6 -> 32, of which waited for: 4 -> 12; matrix products, arithmetic and copies ran while one was open for 7% -> 0% of each run, Pallas kernels for 0% -> 36%
where the time goes in v1:
time: 164 us; the launch traced here: 163 us
  waiting for transfers between devices  66 us (40%)
  Pallas kernels  61.6 us (38%)
  starting transfers between devices  29.5 us (18%)
  local copies, waits for them, and re-layouts  3.92 us (2%)
    ppermute x32, waiting for transfers between devices, exchange(): return lax.ppermute(value, axis, [(i, i ^ flip) for i in range(size)])  66 us
    pallas_call x14, Pallas kernels, call(): pl.pallas_call(kernel, name=name, grid_spec=pltpu.PrefetchScalarGridSpec(...  61.6 us
    ppermute x32, starting transfers between devices, exchange(): return lax.ppermute(value, axis, [(i, i ^ flip) for i in range(size)])  29.5 us
  transfers between devices with their start and end apart: 32, of which 12 were waited for; matrix products, arithmetic and copies ran while one was open for 0% of the time, Pallas kernels for 36%

profile of v1, /device:TPU:0, one launch (start us, length us, event | category | flops | bytes accessed | tf_op | source)
XLA Modules:
  0.0 162.9 jit_solution(18173353863083234192)
XLA Ops:
  3.0 3.0 %collective-permute-start = (f32[128,384]{1,0:T(8,128)S(1)}, f32[128,384]{1,0:T(8,128)S(1)}, u32[]{:S(2)}, u32[]{:S(2)}) collective-permute-start(f32[128,384]{1,0:T(8,128)S(1)} %get-tuple-element.27.near), channel_id=1, source_target_pairs={{0,1},{1,0},{2,3},{3,2},{4,5},{5,4},{6,7},{7,6},{8,9},{9,8},{10,11... | collective-permute-start | bytes 589832 | tf_op jit(solution)/shard_map/ppermute | solution.py:256
  6.0 1.5 collective-permute-start.6
  7.5 3.4 %collective-permute-done.far = f32[128,384]{1,0:T(8,128)S(1)} collective-permute-done((f32[128,384]{1,0:T(8,128)S(1)}, f32[128,384]{1,0:T(8,128)S(1)}, u32[]{:S(2)}, u32[]{:S(2)}) %collective-permute-start) | collective-permute-done | bytes 196640 | tf_op jit(solution)/shard_map/ppermute | solution.py:256
  15.0 9.2 %near_half.2.start = f32[4,256,768]{2,1,0:T(8,128)S(1)} custom-call(s32[4]{0:T(128)S(1)} %pad_add_fusion.scalars, f32[128,384]{1,0:T(8,128)S(1)} %get-tuple-element.27.near, f32[128,384]{1,0:T(8,128)S(1)} %collective-permute-done.8.far, f32[2,4,1,384,3072]{4,3,2,1,0:T(8,128)} %chi.15), custom_call_target="tpu_custom_call" | custom-call | flops 3623878656 | bytes 22020096 | tf_op jit(solution)/shard_map/near_half/pallas_call | solution.py:110
  24.2 1.8 %collective-permute-start.2 = (f32[128,256]{1,0:T(8,128)S(1)}, f32[128,256]{1,0:T(8,128)S(1)}, u32[]{:S(2)}, u32[]{:S(2)}) collective-permute-start(f32[128,256]{1,0:T(8,128)S(1)} %add.85), channel_id=1, source_target_pairs={{0,16},{8,24},{16,0},{24,8},{1,17},{9,25},{17,1},{25,9},{2,18},{10... | collective-permute-start | bytes 393224 | tf_op jit(solution)/shard_map/ppermute | solution.py:256
  26.0 3.1 %far_half_1.2 = f32[256,384]{1,0:T(8,128)S(1)} custom-call(s32[4]{0:T(128)S(1)} %pad_add_fusion.scalars, f32[128,384]{1,0:T(8,128)S(1)} %collective-permute-done.6.near, f32[128,384]{1,0:T(8,128)S(1)} %collective-permute-done.7.far, f32[2,4,1,384,3072]{4,3,2,1,0:T(8,128)} %chi.15, f32[4,256,768]{2,1,0:T(8,128)S(1)} %near_half.2.start), custom_call_target="tpu_custom_call" | custom-call | flops 452984832 | bytes 2752512 | tf_op jit(solution)/shard_map/far_half_1/pallas_call | solution.py:110
  29.1 1.6 collective-permute-start.13
  30.7 1.6 %collective-permute-start.3 = (f32[128,256]{1,0:T(8,128)S(1)}, f32[128,256]{1,0:T(8,128)S(1)}, u32[]{:S(2)}, u32[]{:S(2)}) collective-permute-start(f32[128,256]{1,0:T(8,128)S(1)} %add.86), channel_id=1, source_target_pairs={{0,2},{2,0},{4,6},{6,4},{1,3},{3,1},{5,7},{7,5},{8,10},{10,8},{12,... | collective-permute-start | bytes 393224 | tf_op jit(solution)/shard_map/ppermute | solution.py:256
  32.4 5.6 %far_slab_2.2 = (f32[256,384]{1,0:T(8,128)S(1)}, f32[256,384]{1,0:T(8,128)S(1)}, f32[256,384]{1,0:T(8,128)S(1)}, f32[256,384]{1,0:T(8,128)S(1)}) custom-call(s32[4]{0:T(128)S(1)} %pad_add_fusion.scalars, f32[128,384]{1,0:T(8,128)S(1)} %collective-permute-done.6.near, f32[128,384]{1,0:T(8,128)S(1)} %collective-permute-done.7.far, ...), custom_call_target="tpu_custom_call" | custom-call | flops 1811939328 | bytes 11010048 | tf_op jit(solution)/shard_map/far_slab_2/pallas_call | solution.py:110
  38.9 5.7 %far_half_3.2 = (f32[256,384]{1,0:T(8,128)S(1)}, f32[256,384]{1,0:T(8,128)S(1)}, f32[256,384]{1,0:T(8,128)S(1)}) custom-call(s32[4]{0:T(128)S(1)} %pad_add_fusion.scalars, f32[128,384]{1,0:T(8,128)S(1)} %collective-permute-done.6.near, f32[128,384]{1,0:T(8,128)S(1)} %collective-permute-done.7.far, f32[2,4,1,384,3072]{4,3,2,1,0:T(8,128)} %chi.15, ...), custom_call_target="tpu_custom_call" | custom-call | flops 1358954496 | bytes 8257536 | tf_op jit(solution)/shard_map/far_half_3/pallas_call | solution.py:110
  45.9 2.7 %collective-permute-start.4 = (f32[128,256]{1,0:T(8,128)S(1)}, f32[128,256]{1,0:T(8,128)S(1)}, u32[]{:S(2)}, u32[]{:S(2)}) collective-permute-start(f32[128,256]{1,0:T(8,128)S(1)} %add.87), channel_id=1, source_target_pairs={{0,4},{2,6},{4,0},{6,2},{1,5},{3,7},{5,1},{7,3},{8,12},{10,14},{12... | collective-permute-start | bytes 393224 | tf_op jit(solution)/shard_map/ppermute | solution.py:256
  49.4 4.3 %collective-permute-done.4 = f32[128,256]{1,0:T(8,128)S(1)} collective-permute-done((f32[128,256]{1,0:T(8,128)S(1)}, f32[128,256]{1,0:T(8,128)S(1)}, u32[]{:S(2)}, u32[]{:S(2)}) %collective-permute-start.4) | collective-permute-done | bytes 131104 | tf_op jit(solution)/shard_map/ppermute | solution.py:256
  55.2 1.6 spread.2
  57.3 4.4 %collective-permute-done.14 = f32[256,384]{1,0:T(8,128)S(1)} collective-permute-done((f32[256,384]{1,0:T(8,128)S(1)}, f32[256,384]{1,0:T(8,128)S(1)}, u32[]{:S(2)}, u32[]{:S(2)}) %collective-permute-start.14) | collective-permute-done | bytes 393248 | tf_op jit(solution)/shard_map/ppermute | solution.py:256
  61.8 11.6 %collective-permute-done.11 = f32[256,384]{1,0:T(8,128)S(1)} collective-permute-done((f32[256,384]{1,0:T(8,128)S(1)}, f32[256,384]{1,0:T(8,128)S(1)}, u32[]{:S(2)}, u32[]{:S(2)}) %collective-permute-start.11) | collective-permute-done | bytes 393248 | tf_op jit(solution)/shard_map/ppermute | solution.py:256
  73.5 6.9 %collective-permute-done.15 = f32[256,384]{1,0:T(8,128)S(1)} collective-permute-done((f32[256,384]{1,0:T(8,128)S(1)}, f32[256,384]{1,0:T(8,128)S(1)}, u32[]{:S(2)}, u32[]{:S(2)}) %collective-permute-start.15) | collective-permute-done | bytes 393248 | tf_op jit(solution)/shard_map/ppermute | solution.py:256
  81.1 1.5 collective-permute-start.22
  82.6 6.3 %collective-permute-done.16.far = f32[256,384]{1,0:T(8,128)S(1)} collective-permute-done((f32[256,384]{1,0:T(8,128)S(1)}, f32[256,384]{1,0:T(8,128)S(1)}, u32[]{:S(2)}, u32[]{:S(2)}) %collective-permute-start.16) | collective-permute-done | bytes 393248 | tf_op jit(solution)/shard_map/ppermute | solution.py:256
  88.8 1.6 project.3
  92.4 11.8 %near_half.3.start = f32[4,256,768]{2,1,0:T(8,128)S(1)} custom-call(s32[4]{0:T(128)S(1)} %pad_add_fusion.scalars, f32[256,384]{1,0:T(8,128)S(1)} %get-tuple-element.55.near, f32[256,384]{1,0:T(8,128)S(1)} %collective-permute-done.24.far, f32[2,4,1,384,3072]{4,3,2,1,0:T(8,128)} %chi.15), custom_call_target="tpu_custom_call" | custom-call | flops 7247757312 | bytes 22020096 | tf_op jit(solution)/shard_map/near_half/pallas_call | solution.py:110
  104.3 3.8 %far_half_1.3 = f32[256,384]{1,0:T(8,128)S(1)} custom-call(s32[4]{0:T(128)S(1)} %pad_add_fusion.scalars, f32[256,384]{1,0:T(8,128)S(1)} %collective-permute-done.22.near, f32[256,384]{1,0:T(8,128)S(1)} %collective-permute-done.23.far, f32[2,4,1,384,3072]{4,3,2,1,0:T(8,128)} %chi.15, f32[4,256,768]{2,1,0:T(8,128)S(1)} %near_half.3.start), custom_call_target="tpu_custom_call" | custom-call | flops 905969664 | bytes 2752512 | tf_op jit(solution)/shard_map/far_half_1/pallas_call | solution.py:110
  108.1 1.6 collective-permute-start.29
  109.7 7.4 %far_slab_2.3 = (f32[256,384]{1,0:T(8,128)S(1)}, f32[256,384]{1,0:T(8,128)S(1)}, f32[256,384]{1,0:T(8,128)S(1)}, f32[256,384]{1,0:T(8,128)S(1)}) custom-call(s32[4]{0:T(128)S(1)} %pad_add_fusion.scalars, f32[256,384]{1,0:T(8,128)S(1)} %collective-permute-done.22.near, f32[256,384]{1,0:T(8,128)S(1)} %collective-permute-done.23.far, ...), custom_call_target="tpu_custom_call" | custom-call | flops 3623878656 | bytes 11010048 | tf_op jit(solution)/shard_map/far_slab_2/pallas_call | solution.py:110
  117.7 7.0 %far_half_3.3 = (f32[256,384]{1,0:T(8,128)S(1)}, f32[256,384]{1,0:T(8,128)S(1)}, f32[256,384]{1,0:T(8,128)S(1)}) custom-call(s32[4]{0:T(128)S(1)} %pad_add_fusion.scalars, f32[256,384]{1,0:T(8,128)S(1)} %collective-permute-done.22.near, f32[256,384]{1,0:T(8,128)S(1)} %collective-permute-done.23.far, f32[2,4,1,384,3072]{4,3,2,1,0:T(8,128)} %chi.15, ...), custom_call_target="tpu_custom_call" | custom-call | flops 2717908992 | bytes 8257536 | tf_op jit(solution)/shard_map/far_half_3/pallas_call | solution.py:110
  124.7 1.6 collective-permute-start.28
  126.3 2.0 %collective-permute-start.30 = (f32[256,384]{1,0:T(8,128)S(1)}, f32[256,384]{1,0:T(8,128)S(1)}, u32[]{:S(2)}, u32[]{:S(2)}) collective-permute-start(f32[256,384]{1,0:T(8,128)S(1)} %add.107), channel_id=1, source_target_pairs={{0,2},{2,0},{4,6},{6,4},{1,3},{3,1},{5,7},{7,5},{8,10},{10,8},{12,... | collective-permute-start | bytes 1179656 | tf_op jit(solution)/shard_map/ppermute | solution.py:256
  128.4 10.0 %collective-permute-done.20 = f32[128,256]{1,0:T(8,128)S(1)} collective-permute-done((f32[128,256]{1,0:T(8,128)S(1)}, f32[128,256]{1,0:T(8,128)S(1)}, u32[]{:S(2)}, u32[]{:S(2)}) %collective-permute-start.20) | collective-permute-done | bytes 131104 | tf_op jit(solution)/shard_map/ppermute | solution.py:256
  139.8 1.6 spread.3
  142.0 1.8 %collective-permute-start.27 = (f32[256,384]{1,0:T(8,128)S(1)}, f32[256,384]{1,0:T(8,128)S(1)}, u32[]{:S(2)}, u32[]{:S(2)}) collective-permute-start(f32[256,384]{1,0:T(8,128)S(1)} %add.105), channel_id=1, source_target_pairs={{0,2},{2,0},{4,6},{6,4},{1,3},{3,1},{5,7},{7,5},{8,10},{10,8},{12,... | collective-permute-start | bytes 1179656 | tf_op jit(solution)/shard_map/ppermute | solution.py:256
  143.9 1.7 %collective-permute-start.31 = (f32[256,384]{1,0:T(8,128)S(1)}, f32[256,384]{1,0:T(8,128)S(1)}, u32[]{:S(2)}, u32[]{:S(2)}) collective-permute-start(f32[256,384]{1,0:T(8,128)S(1)} %add_add_fusion), channel_id=1, source_target_pairs={{0,4},{2,6},{4,0},{6,2},{1,5},{3,7},{5,1},{7,3},{8,12},{10,14},{12... | collective-permute-start | bytes 1179656 | tf_op jit(solution)/shard_map/ppermute | solution.py:256
  145.7 7.0 %collective-permute-done.25.by_dev = f32[256,384]{1,0:T(8,128)S(1)} collective-permute-done((f32[256,384]{1,0:T(8,128)S(1)}, f32[256,384]{1,0:T(8,128)S(1)}, u32[]{:S(2)}, u32[]{:S(2)}) %collective-permute-start.25) | collective-permute-done | bytes 393248 | tf_op jit(solution)/shard_map/ppermute | solution.py:256
  152.6 8.8 %collective-permute-done.27.by_near = f32[256,384]{1,0:T(8,128)S(1)} collective-permute-done((f32[256,384]{1,0:T(8,128)S(1)}, f32[256,384]{1,0:T(8,128)S(1)}, u32[]{:S(2)}, u32[]{:S(2)}) %collective-permute-start.27) | collective-permute-done | bytes 393248 | tf_op jit(solution)/shard_map/ppermute | solution.py:256
  (87 shorter events, 18.6 us)
Async XLA Ops:
  3.0 7.9 %collective-permute-start = (f32[128,384]{1,0:T(8,128)S(1)}, f32[128,384]{1,0:T(8,128)S(1)}, u32[]{:S(2)}, u32[]{:S(2)}) collective-permute-start(f32[128,384]{1,0:T(8,128)S(1)} %get-tuple-element.27.near), channel_id=1, source_target_pairs={{0,1},{1,0},{2,3},{3,2},{4,5},{5,4},{6,7},{7,6},{8,9},{9,8},{10,11... | collective-permute-start | bytes 589832 | tf_op jit(solution)/shard_map/ppermute | solution.py:256
  6.0 8.4 %collective-permute-start.6 = (f32[128,384]{1,0:T(8,128)S(1)}, f32[128,384]{1,0:T(8,128)S(1)}, u32[]{:S(2)}, u32[]{:S(2)}) collective-permute-start(f32[128,384]{1,0:T(8,128)S(1)} %get-tuple-element.27.near), channel_id=1, source_target_pairs={{0,16},{8,24},{16,0},{24,8},{1,17},{9,25},{17,1},{25,9},{2,18},{10... | collective-permute-start | bytes 589832 | tf_op jit(solution)/shard_map/ppermute | solution.py:256
  7.5 7.4 %collective-permute-start.8 = (f32[128,384]{1,0:T(8,128)S(1)}, f32[128,384]{1,0:T(8,128)S(1)}, u32[]{:S(2)}, u32[]{:S(2)}) collective-permute-start(f32[128,384]{1,0:T(8,128)S(1)} %get-tuple-element.27.near), channel_id=1, source_target_pairs={{0,8},{8,0},{16,24},{24,16},{1,9},{9,1},{17,25},{25,17},{2,10},{10... | collective-permute-start | bytes 589832 | tf_op jit(solution)/shard_map/ppermute | solution.py:256
  14.4 9.8 %collective-permute-start.1 = (f32[128,256]{1,0:T(8,128)S(1)}, f32[128,256]{1,0:T(8,128)S(1)}, u32[]{:S(2)}, u32[]{:S(2)}) collective-permute-start(f32[128,256]{1,0:T(8,128)S(1)} %get-tuple-element.29), channel_id=1, source_target_pairs={{0,8},{8,0},{16,24},{24,16},{1,9},{9,1},{17,25},{25,17},{2,10},{10... | collective-permute-start | bytes 393224 | tf_op jit(solution)/shard_map/ppermute | solution.py:256
  14.5 11.5 %collective-permute-start.7 = (f32[128,384]{1,0:T(8,128)S(1)}, f32[128,384]{1,0:T(8,128)S(1)}, u32[]{:S(2)}, u32[]{:S(2)}) collective-permute-start(f32[128,384]{1,0:T(8,128)S(1)} %collective-permute-done.6.near), channel_id=1, source_target_pairs={{0,8},{8,0},{16,24},{24,16},{1,9},{9,1},{17,25},{25,17},{2,10},{10... | collective-permute-start | bytes 589832 | tf_op jit(solution)/shard_map/ppermute | solution.py:256
  24.2 6.5 %collective-permute-start.2 = (f32[128,256]{1,0:T(8,128)S(1)}, f32[128,256]{1,0:T(8,128)S(1)}, u32[]{:S(2)}, u32[]{:S(2)}) collective-permute-start(f32[128,256]{1,0:T(8,128)S(1)} %add.85), channel_id=1, source_target_pairs={{0,16},{8,24},{16,0},{24,8},{1,17},{9,25},{17,1},{25,9},{2,18},{10... | collective-permute-start | bytes 393224 | tf_op jit(solution)/shard_map/ppermute | solution.py:256
  29.1 19.4 %collective-permute-start.13 = (f32[256,384]{1,0:T(8,128)S(1)}, f32[256,384]{1,0:T(8,128)S(1)}, u32[]{:S(2)}, u32[]{:S(2)}) collective-permute-start(f32[256,384]{1,0:T(8,128)S(1)} %far_half_1.2), channel_id=1, source_target_pairs={{0,1},{1,0},{2,3},{3,2},{4,5},{5,4},{6,7},{7,6},{8,9},{9,8},{10,11... | collective-permute-start | bytes 1179656 | tf_op jit(solution)/shard_map/ppermute | solution.py:256
  30.7 15.1 %collective-permute-start.3 = (f32[128,256]{1,0:T(8,128)S(1)}, f32[128,256]{1,0:T(8,128)S(1)}, u32[]{:S(2)}, u32[]{:S(2)}) collective-permute-start(f32[128,256]{1,0:T(8,128)S(1)} %add.86), channel_id=1, source_target_pairs={{0,2},{2,0},{4,6},{6,4},{1,3},{3,1},{5,7},{7,5},{8,10},{10,8},{12,... | collective-permute-start | bytes 393224 | tf_op jit(solution)/shard_map/ppermute | solution.py:256
  38.0 15.8 %collective-permute-start.10 = (f32[256,384]{1,0:T(8,128)S(1)}, f32[256,384]{1,0:T(8,128)S(1)}, u32[]{:S(2)}, u32[]{:S(2)}) collective-permute-start(f32[256,384]{1,0:T(8,128)S(1)} %get-tuple-element.35), channel_id=1, source_target_pairs={{0,1},{1,0},{2,3},{3,2},{4,5},{5,4},{6,7},{7,6},{8,9},{9,8},{10,11... | collective-permute-start | bytes 1179656 | tf_op jit(solution)/shard_map/ppermute | solution.py:256
  44.6 12.7 %collective-permute-start.12 = (f32[256,384]{1,0:T(8,128)S(1)}, f32[256,384]{1,0:T(8,128)S(1)}, u32[]{:S(2)}, u32[]{:S(2)}) collective-permute-start(f32[256,384]{1,0:T(8,128)S(1)} %get-tuple-element.37), channel_id=1, source_target_pairs={{0,1},{1,0},{2,3},{3,2},{4,5},{5,4},{6,7},{7,6},{8,9},{9,8},{10,11... | collective-permute-start | bytes 1179656 | tf_op jit(solution)/shard_map/ppermute | solution.py:256
  45.9 7.8 %collective-permute-start.4 = (f32[128,256]{1,0:T(8,128)S(1)}, f32[128,256]{1,0:T(8,128)S(1)}, u32[]{:S(2)}, u32[]{:S(2)}) collective-permute-start(f32[128,256]{1,0:T(8,128)S(1)} %add.87), channel_id=1, source_target_pairs={{0,4},{2,6},{4,0},{6,2},{1,5},{3,7},{5,1},{7,3},{8,12},{10,14},{12... | collective-permute-start | bytes 393224 | tf_op jit(solution)/shard_map/ppermute | solution.py:256
  48.6 13.1 %collective-permute-start.14 = (f32[256,384]{1,0:T(8,128)S(1)}, f32[256,384]{1,0:T(8,128)S(1)}, u32[]{:S(2)}, u32[]{:S(2)}) collective-permute-start(f32[256,384]{1,0:T(8,128)S(1)} %add.96), channel_id=1, source_target_pairs={{0,2},{2,0},{4,6},{6,4},{1,3},{3,1},{5,7},{7,5},{8,10},{10,8},{12,... | collective-permute-start | bytes 1179656 | tf_op jit(solution)/shard_map/ppermute | solution.py:256
  53.7 1.4 collective-permute-start.5
  53.9 19.6 %collective-permute-start.11 = (f32[256,384]{1,0:T(8,128)S(1)}, f32[256,384]{1,0:T(8,128)S(1)}, u32[]{:S(2)}, u32[]{:S(2)}) collective-permute-start(f32[256,384]{1,0:T(8,128)S(1)} %add.93), channel_id=1, source_target_pairs={{0,2},{2,0},{4,6},{6,4},{1,3},{3,1},{5,7},{7,5},{8,10},{10,8},{12,... | collective-permute-start | bytes 1179656 | tf_op jit(solution)/shard_map/ppermute | solution.py:256
  56.7 16.7 %collective-permute-start.9 = (f32[256,384]{1,0:T(8,128)S(1)}, f32[256,384]{1,0:T(8,128)S(1)}, u32[]{:S(2)}, u32[]{:S(2)}) collective-permute-start(f32[256,384]{1,0:T(8,128)S(1)} %get-tuple-element.33), channel_id=1, source_target_pairs={{0,1},{1,0},{2,3},{3,2},{4,5},{5,4},{6,7},{7,6},{8,9},{9,8},{10,11... | collective-permute-start | bytes 1179656 | tf_op jit(solution)/shard_map/ppermute | solution.py:256
  61.7 18.6 %collective-permute-start.15 = (f32[256,384]{1,0:T(8,128)S(1)}, f32[256,384]{1,0:T(8,128)S(1)}, u32[]{:S(2)}, u32[]{:S(2)}) collective-permute-start(f32[256,384]{1,0:T(8,128)S(1)} %add_add_fusion.1), channel_id=1, source_target_pairs={{0,4},{2,6},{4,0},{6,2},{1,5},{3,7},{5,1},{7,3},{8,12},{10,14},{12... | collective-permute-start | bytes 1179656 | tf_op jit(solution)/shard_map/ppermute | solution.py:256
  80.5 8.3 %collective-permute-start.16 = (f32[256,384]{1,0:T(8,128)S(1)}, f32[256,384]{1,0:T(8,128)S(1)}, u32[]{:S(2)}, u32[]{:S(2)}) collective-permute-start(f32[256,384]{1,0:T(8,128)S(1)} %get-tuple-element.55.near), channel_id=1, source_target_pairs={{0,1},{1,0},{2,3},{3,2},{4,5},{5,4},{6,7},{7,6},{8,9},{9,8},{10,11... | collective-permute-start | bytes 1179656 | tf_op jit(solution)/shard_map/ppermute | solution.py:256
  81.1 9.4 %collective-permute-start.22 = (f32[256,384]{1,0:T(8,128)S(1)}, f32[256,384]{1,0:T(8,128)S(1)}, u32[]{:S(2)}, u32[]{:S(2)}) collective-permute-start(f32[256,384]{1,0:T(8,128)S(1)} %get-tuple-element.55.near), channel_id=1, source_target_pairs={{0,16},{8,24},{16,0},{24,8},{1,17},{9,25},{17,1},{25,9},{2,18},{10... | collective-permute-start | bytes 1179656 | tf_op jit(solution)/shard_map/ppermute | solution.py:256
  82.6 9.8 %collective-permute-start.24 = (f32[256,384]{1,0:T(8,128)S(1)}, f32[256,384]{1,0:T(8,128)S(1)}, u32[]{:S(2)}, u32[]{:S(2)}) collective-permute-start(f32[256,384]{1,0:T(8,128)S(1)} %get-tuple-element.55.near), channel_id=1, source_target_pairs={{0,8},{8,0},{16,24},{24,16},{1,9},{9,1},{17,25},{25,17},{2,10},{10... | collective-permute-start | bytes 1179656 | tf_op jit(solution)/shard_map/ppermute | solution.py:256
  90.4 1.4 collective-permute-start.17
  90.5 13.8 %collective-permute-start.23 = (f32[256,384]{1,0:T(8,128)S(1)}, f32[256,384]{1,0:T(8,128)S(1)}, u32[]{:S(2)}, u32[]{:S(2)}) collective-permute-start(f32[256,384]{1,0:T(8,128)S(1)} %collective-permute-done.22.near), channel_id=1, source_target_pairs={{0,8},{8,0},{16,24},{24,16},{1,9},{9,1},{17,25},{25,17},{2,10},{10... | collective-permute-start | bytes 1179656 | tf_op jit(solution)/shard_map/ppermute | solution.py:256
  91.9 12.3 %collective-permute-start.18 = (f32[128,256]{1,0:T(8,128)S(1)}, f32[128,256]{1,0:T(8,128)S(1)}, u32[]{:S(2)}, u32[]{:S(2)}) collective-permute-start(f32[128,256]{1,0:T(8,128)S(1)} %add.101), channel_id=1, source_target_pairs={{0,16},{8,24},{16,0},{24,8},{1,17},{9,25},{17,1},{25,9},{2,18},{10... | collective-permute-start | bytes 393224 | tf_op jit(solution)/shard_map/ppermute | solution.py:256
  104.2 24.1 %collective-permute-start.19 = (f32[128,256]{1,0:T(8,128)S(1)}, f32[128,256]{1,0:T(8,128)S(1)}, u32[]{:S(2)}, u32[]{:S(2)}) collective-permute-start(f32[128,256]{1,0:T(8,128)S(1)} %add.102), channel_id=1, source_target_pairs={{0,2},{2,0},{4,6},{6,4},{1,3},{3,1},{5,7},{7,5},{8,10},{10,8},{12,... | collective-permute-start | bytes 393224 | tf_op jit(solution)/shard_map/ppermute | solution.py:256
  108.1 18.2 %collective-permute-start.29 = (f32[256,384]{1,0:T(8,128)S(1)}, f32[256,384]{1,0:T(8,128)S(1)}, u32[]{:S(2)}, u32[]{:S(2)}) collective-permute-start(f32[256,384]{1,0:T(8,128)S(1)} %far_half_1.3), channel_id=1, source_target_pairs={{0,1},{1,0},{2,3},{3,2},{4,5},{5,4},{6,7},{7,6},{8,9},{9,8},{10,11... | collective-permute-start | bytes 1179656 | tf_op jit(solution)/shard_map/ppermute | solution.py:256
  117.1 24.9 %collective-permute-start.26 = (f32[256,384]{1,0:T(8,128)S(1)}, f32[256,384]{1,0:T(8,128)S(1)}, u32[]{:S(2)}, u32[]{:S(2)}) collective-permute-start(f32[256,384]{1,0:T(8,128)S(1)} %get-tuple-element.46), channel_id=1, source_target_pairs={{0,1},{1,0},{2,3},{3,2},{4,5},{5,4},{6,7},{7,6},{8,9},{9,8},{10,11... | collective-permute-start | bytes 1179656 | tf_op jit(solution)/shard_map/ppermute | solution.py:256
  124.7 19.2 %collective-permute-start.28 = (f32[256,384]{1,0:T(8,128)S(1)}, f32[256,384]{1,0:T(8,128)S(1)}, u32[]{:S(2)}, u32[]{:S(2)}) collective-permute-start(f32[256,384]{1,0:T(8,128)S(1)} %get-tuple-element.48), channel_id=1, source_target_pairs={{0,1},{1,0},{2,3},{3,2},{4,5},{5,4},{6,7},{7,6},{8,9},{9,8},{10,11... | collective-permute-start | bytes 1179656 | tf_op jit(solution)/shard_map/ppermute | solution.py:256
  126.3 17.5 %collective-permute-start.30 = (f32[256,384]{1,0:T(8,128)S(1)}, f32[256,384]{1,0:T(8,128)S(1)}, u32[]{:S(2)}, u32[]{:S(2)}) collective-permute-start(f32[256,384]{1,0:T(8,128)S(1)} %add.107), channel_id=1, source_target_pairs={{0,2},{2,0},{4,6},{6,4},{1,3},{3,1},{5,7},{7,5},{8,10},{10,8},{12,... | collective-permute-start | bytes 1179656 | tf_op jit(solution)/shard_map/ppermute | solution.py:256
  128.3 10.1 %collective-permute-start.20 = (f32[128,256]{1,0:T(8,128)S(1)}, f32[128,256]{1,0:T(8,128)S(1)}, u32[]{:S(2)}, u32[]{:S(2)}) collective-permute-start(f32[128,256]{1,0:T(8,128)S(1)} %add.103), channel_id=1, source_target_pairs={{0,4},{2,6},{4,0},{6,2},{1,5},{3,7},{5,1},{7,3},{8,12},{10,14},{12... | collective-permute-start | bytes 393224 | tf_op jit(solution)/shard_map/ppermute | solution.py:256
  138.4 1.4 collective-permute-start.21
  141.4 11.2 %collective-permute-start.25 = (f32[256,384]{1,0:T(8,128)S(1)}, f32[256,384]{1,0:T(8,128)S(1)}, u32[]{:S(2)}, u32[]{:S(2)}) collective-permute-start(f32[256,384]{1,0:T(8,128)S(1)} %get-tuple-element.44), channel_id=1, source_target_pairs={{0,1},{1,0},{2,3},{3,2},{4,5},{5,4},{6,7},{7,6},{8,9},{9,8},{10,11... | collective-permute-start | bytes 1179656 | tf_op jit(solution)/shard_map/ppermute | solution.py:256
  142.0 19.4 %collective-permute-start.27 = (f32[256,384]{1,0:T(8,128)S(1)}, f32[256,384]{1,0:T(8,128)S(1)}, u32[]{:S(2)}, u32[]{:S(2)}) collective-permute-start(f32[256,384]{1,0:T(8,128)S(1)} %add.105), channel_id=1, source_target_pairs={{0,2},{2,0},{4,6},{6,4},{1,3},{3,1},{5,7},{7,5},{8,10},{10,8},{12,... | collective-permute-start | bytes 1179656 | tf_op jit(solution)/shard_map/ppermute | solution.py:256
  143.9 17.5 %collective-permute-start.31 = (f32[256,384]{1,0:T(8,128)S(1)}, f32[256,384]{1,0:T(8,128)S(1)}, u32[]{:S(2)}, u32[]{:S(2)}) collective-permute-start(f32[256,384]{1,0:T(8,128)S(1)} %add_add_fusion), channel_id=1, source_target_pairs={{0,4},{2,6},{4,0},{6,2},{1,5},{3,7},{5,1},{7,3},{8,12},{10,14},{12... | collective-permute-start | bytes 1179656 | tf_op jit(solution)/shard_map/ppermute | solution.py:256
  (10 other events, 122.5 us)

commit v2 on v0

--- a/solution.py
+++ b/solution.py
@@ -1,6 +1,10 @@
+import functools
+
 import jax
 import jax.numpy as jnp
 from jax import lax
+from jax.experimental import pallas as pl
+from jax.experimental.pallas import tpu as pltpu
 from jax.sharding import PartitionSpec as P
 
 ITERS = 2
@@ -8,6 +12,23 @@
 
 frequency = 0.8
 damping = 0.5
+MIB = 1 << 20
+DEPTH = 4
+LIMIT = 8
+HURRY = 64
+AHEAD = 3
+
+
+def lookup(bands, table):
+    band_index = jnp.arange(table.shape[0], dtype=jnp.int32)
+    match = bands[None, :] == band_index[:, None]
+    return jnp.sum(jnp.where(match, table[:, None], 0.0), axis=0)
+
+
+def pair_weight(band_v, band_c, band_energy, band_occ):
+    delta = lookup(band_c, band_energy) - lookup(band_v, band_energy)
+    filling = lookup(band_v, band_occ) - lookup(band_c, band_occ)
+    return filling * 2.0 * delta / (delta * delta + frequency * frequency)
 
 
 def contract(left, right):
@@ -24,23 +45,13 @@
     return jnp.dot(left, right, precision=lax.Precision.HIGHEST, preferred_element_type=jnp.float32)
 
 
-def lookup(bands, table):
-    band_index = jnp.arange(table.shape[0], dtype=jnp.int32)
-    match = bands[:, None] == band_index[None, :]
-    return jnp.sum(jnp.where(match, table[None, :], 0.0), axis=1)
-
-
-def shards(rho_re, rho_im, coulomb, chi_prev, source, band_v, band_c, band_energy, band_occ):
-    delta = lookup(band_c, band_energy) - lookup(band_v, band_energy)
-    filling = lookup(band_v, band_occ) - lookup(band_c, band_occ)
-    weight = filling * 2.0 * delta / (delta * delta + frequency * frequency)
+def general(rho_re, rho_im, coulomb, chi_prev, source, band_v, band_c, band_energy, band_occ):
+    weight = pair_weight(band_v, band_c, band_energy, band_occ)
     slab = rho_re.shape[0]
     width = source.shape[1]
     row_block = chi_prev.shape[4]
     my_cols = chi_prev.shape[1] * chi_prev.shape[3]
     previous = chi_prev.reshape(2, my_cols, row_block)
-    tile_re = previous[0]
-    tile_im = previous[1]
     scale = coulomb[:, None]
     real_part = source
     imag_part = jnp.zeros_like(source)
@@ -48,7 +59,7 @@
         scaled = jnp.concatenate([scale * real_part, scale * imag_part], axis=1)
         piece = lax.all_gather(scaled, "grp", axis=0, tiled=True)
         swapped = jnp.concatenate([-piece[:, width:], piece[:, :width]], axis=1)
-        total = contract(tile_re, piece) + contract(tile_im, swapped)
+        total = contract(previous[0], piece) + contract(previous[1], swapped)
         slab_scaled = lax.all_gather(scaled, "dev", axis=0, tiled=True)
         slab_re = slab_scaled[:, :width]
         slab_im = slab_scaled[:, width:]
@@ -73,6 +84,387 @@
     return (real_part, imag_part)
 
 
+def split(value):
+    high = value.astype(jnp.bfloat16)
+    return high, (value - high.astype(jnp.float32)).astype(jnp.bfloat16)
+
+
+def dot(left, right):
+    return jnp.dot(left, right, preferred_element_type=jnp.float32)
+
+
+def dot_nt(left, right):
+    return lax.dot_general(
+        left, right, (((1,), (1,)), ((), ())), preferred_element_type=jnp.float32
+    )
+
+
+def dot3(stacked, rows, right, product=dot):
+    high, low = split(right)
+    both = product(stacked, high)
+    return both[:rows] + both[rows:] + product(stacked[:rows], low)
+
+
+def stack(value):
+    high, low = split(value)
+    return jnp.concatenate([high, low], axis=0)
+
+
+def small(kernel, name, scalars, out_shape, scratch, cost, *operands, chi=None, limit=LIMIT):
+    vmem = pl.BlockSpec(memory_space=pltpu.VMEM)
+    in_specs = [pl.BlockSpec(memory_space=pltpu.SMEM)] + [vmem] * len(operands)
+    if chi is not None:
+        in_specs.append(pl.BlockSpec(memory_space=pl.ANY))
+        operands += (chi,)
+    return pl.pallas_call(
+        kernel,
+        name=name,
+        in_specs=in_specs,
+        out_specs=[vmem] * len(out_shape),
+        out_shape=out_shape,
+        scratch_shapes=scratch,
+        cost_estimate=pl.CostEstimate(flops=cost[0] // HURRY, bytes_accessed=cost[1] // HURRY, transcendentals=0),
+        compiler_params=pltpu.CompilerParams(vmem_limit_bytes=limit * MIB),
+    )(scalars, *operands)
+
+
+def shaped(*shape):
+    return jax.ShapeDtypeStruct(shape, jnp.float32)
+
+
+def product3(stacked, rows, high, low):
+    both = dot(stacked, high)
+    return both[:rows] + both[rows:] + dot(stacked[:rows], low)
+
+
+def fill_panel(panel, core, near, far, width):
+    rows, half = near.shape
+    for piece, place in ((near, core), (far, 1 - core)):
+        at = pl.ds(pl.multiple_of(place * half, half), half)
+        high, low = split(piece[...])
+        panel[0, :rows, at] = high
+        panel[0, rows:, at] = low
+        if rows == 2 * width:
+            panel[1, :width, at] = -high[width:]
+            panel[1, width:rows, at] = high[:width]
+            panel[1, rows : rows + width, at] = -low[width:]
+            panel[1, rows + width :, at] = low[:width]
+
+
+def add_product(total, width, panel, part, block, first):
+    if panel.shape[0] == 2:
+        rows, stacked, at = 2 * width, panel[part], slice(None)
+    else:
+        rows, stacked, at = width, panel[0], slice(part * width, (part + 1) * width)
+    product = product3(stacked, rows, *split(block))
+    total[at] = product if first else total[at] + product
+
+
+def fetch(scalars, chi, targets, sems, jobs):
+    slab = targets[0].shape[-1]
+    queue = []
+    for (j, far), target in zip(jobs, targets):
+        pair = 1 - scalars[0] if far else scalars[0]
+        at = pl.ds(pl.multiple_of((scalars[2] ^ j) * slab, slab), slab)
+        for part in range(2):
+            source = chi.at[part, pl.ds(2 * pair, 2), 0, :, at]
+            queue.append(pltpu.make_async_copy(source, target.at[part], sems.at[len(queue)]))
+    for copy in queue[:DEPTH]:
+        copy.start()
+
+    def arrived(index):
+        queue[index].wait()
+        if index + DEPTH < len(queue):
+            queue[index + DEPTH].start()
+
+    return arrived
+
+
+def begin_kernel(scalars, source, coulomb, bare, scaled):
+    turned = source[...].T
+    bare[...] = turned
+    scaled[...] = turned * coulomb[...]
+
+
+def each_block(count, chi, buffers, sems, place, use):
+    slots, slab = buffers.shape[0], buffers.shape[-1]
+
+    def copy(t):
+        part, pair, row = place(t)
+        at = pl.ds(pl.multiple_of(row * slab, slab), slab)
+        slot = lax.rem(t, slots)
+        return pltpu.make_async_copy(chi.at[part, pl.ds(2 * pair, 2), 0, :, at], buffers.at[slot], sems.at[slot])
+
+    def step(t, carry):
+        copy(t).wait()
+
+        @pl.when((t == 0) & (count > 1))
+        def _():
+            copy(t + 1).start()
+
+        @pl.when(t + 2 < count)
+        def _():
+            copy(t + 2).start()
+
+        use(t, buffers[lax.rem(t, slots)].reshape(slab, slab))
+        return carry
+
+    return copy, step
+
+
+def first_kernel(width, jobs, scalars, near, far, chi, out, *rest):
+    *blocks, panel, sems = rest
+    slab = 2 * near.shape[1]
+    arrived = fetch(scalars, chi, blocks, sems, jobs)
+    fill_panel(panel, scalars[1], near, far, width)
+    for part in range(2):
+        arrived(part)
+        first = part == 0 or panel.shape[0] == 1
+        add_product(out.at[0], width, panel, part, blocks[0][part].reshape(slab, slab), first)
+    for index in range(2, 2 * len(jobs)):
+        arrived(index)
+
+
+def near_kernel(width, scalars, near, far, *rest):
+    *blocks, out, panel = rest
+    slab = 2 * near.shape[1]
+    fill_panel(panel, scalars[1], near, far, width)
+    for index, block in enumerate(blocks):
+        for part in range(2):
+            first = part == 0 or panel.shape[0] == 1
+            add_product(out.at[index], width, panel, part, block[part].reshape(slab, slab), first)
+
+
+def halves_out(scalars, full, send, keep):
+    half = send.shape[1]
+    for place, out in ((1 - scalars[3], send), (scalars[3], keep)):
+        out[...] = full[:, pl.ds(pl.multiple_of(place * half, half), half)]
+
+
+def far_kernel(width, begun, scalars, near, far, start, block, send, keep, panel, full):
+    slab = 2 * near.shape[1]
+    full[...] = start[begun]
+    fill_panel(panel, scalars[1], near, far, width)
+    for part in range(2):
+        add_product(full, width, panel, part, block[part].reshape(slab, slab), False)
+    halves_out(scalars, full, send, keep)
+
+
+def held_kernel(width, scalars, near, near_far, far, far_far, near_block, far_block, send, keep, panel, full):
+    slab = 2 * near.shape[1]
+    for side, pieces in enumerate(((near, near_far), (far, far_far))):
+        fill_panel(panel.at[side], scalars[1], *pieces, width)
+    for side, block in enumerate((near_block, far_block)):
+        for part in range(2):
+            first = side == 0 and (part == 0 or panel.shape[1] == 1)
+            add_product(full, width, panel.at[side], part, block[part].reshape(slab, slab), first)
+    halves_out(scalars, full, send, keep)
+
+
+def both_kernel(width, jobs, scalars, near, near_far, far, far_far, chi, *rest):
+    count = len(jobs) // 2
+    outs, blocks, (panel, full, sems) = rest[: 2 * count], rest[2 * count : 4 * count], rest[4 * count :]
+    slab = 2 * near.shape[1]
+    arrived = fetch(scalars, chi, blocks, sems, jobs)
+    fill_panel(panel.at[0], scalars[1], near, near_far, width)
+    fill_panel(panel.at[1], scalars[1], far, far_far, width)
+    for index, block in enumerate(blocks):
+        side = index % 2
+        for part in range(2):
+            arrived(2 * index + part)
+            first = side == 0 and (part == 0 or panel.shape[1] == 1)
+            add_product(full, width, panel.at[side], part, block[part].reshape(slab, slab), first)
+        if side == 1:
+            halves_out(scalars, full, outs[index - 1], outs[index])
+
+
+def project_kernel(width, scalars, near, far, rho_re, rho_im, keep, send, full):
+    rows, half = near.shape
+    dev, core = scalars[3], scalars[1]
+    total_re = total_im = None
+    for piece, place in ((near, dev), (far, 1 - dev)):
+        at = pl.ds(pl.multiple_of(place * half, half), half)
+        panel = stack(piece[...])
+        by_re = dot3(panel, rows, rho_re[at])
+        by_im = dot3(panel, rows, rho_im[at])
+        total_re = by_re if total_re is None else total_re + by_re
+        total_im = by_im if total_im is None else total_im + by_im
+    if rows == 2 * width:
+        full[:width] = total_re[:width] + total_im[width:]
+        full[width:] = total_re[width:] - total_im[:width]
+    else:
+        full[:width] = total_re
+        full[width:] = -total_im
+    keep[...] = full[pl.ds(pl.multiple_of(core * width, width), width)]
+    send[...] = full[pl.ds(pl.multiple_of((1 - core) * width, width), width)]
+
+
+def spread_kernel(width, scalars, near, far, weight, rho_re, rho_im, first, second, first_out, second_out, full):
+    half = first.shape[1]
+    dev, core = scalars[3], scalars[1]
+    full[pl.ds(pl.multiple_of(core * width, width), width)] = weight[...] * near[...]
+    full[pl.ds(pl.multiple_of((1 - core) * width, width), width)] = weight[...] * far[...]
+    panel = stack(full[...])
+    for place, given, out in ((1 - dev, first, first_out), (dev, second, second_out)):
+        at = pl.ds(pl.multiple_of(place * half, half), half)
+        by_re = dot3(panel, 2 * width, rho_re[at], dot_nt)
+        by_im = dot3(panel, 2 * width, rho_im[at], dot_nt)
+        out[:width] = given[:width] - (by_re[:width] - by_im[width:])
+        out[width:] = given[width:] - (by_re[width:] + by_im[:width])
+
+
+def end_kernel(width, scalars, own, by_dev, by_near, by_far, iterate, bare, coulomb, out_re, out_im):
+    image = coulomb[...] * (own[...] + by_dev[...] + by_near[...] + by_far[...])
+    real_part = iterate[:width]
+    imag_part = iterate[width:]
+    real_part = real_part + damping * (bare[...] + image[:width] - real_part)
+    imag_part = imag_part + damping * (image[width:] - imag_part)
+    out_re[...] = real_part.T
+    out_im[...] = imag_part.T
+
+
+def after(value, *earlier):
+    return lax.optimization_barrier((value, *earlier))[0]
+
+
+def exchange(value, axis, flip):
+    size = lax.axis_size(axis)
+    return lax.ppermute(value, axis, [(i, i ^ flip) for i in range(size)])
+
+
+def exchanged(rho_re, rho_im, coulomb, chi_prev, source, band_v, band_c, band_energy, band_occ):
+    weight = pair_weight(band_v, band_c, band_energy, band_occ)[None, :]
+    half, width = source.shape
+    pairs = rho_re.shape[1]
+    slab = 2 * half
+    panel_rows = 2 * width
+    parts = chi_prev.shape[0]
+    row_block = chi_prev.shape[4]
+    n_slab = row_block // slab
+    last = n_slab - 1
+    grp = lax.axis_index("grp")
+    scalars = jnp.stack([grp // 2, grp % 2, lax.axis_index("col"), lax.axis_index("dev")]).astype(jnp.int32)
+    scale = coulomb[None, :]
+
+    bare, scaled = small(
+        begin_kernel, "begin", scalars, [shaped(width, half)] * 2, [], (0, 12 * half * width), source, scale
+    )
+
+    def products(blocks, rows):
+        flops = 3 * 2 * 2 * blocks * rows * slab * slab
+        return flops, 4 * blocks * slab * (parts * slab + panel_rows)
+
+    block_shape = (parts, 2, half, slab)
+
+    def image(scaled, blocks):
+        rows = scaled.shape[0]
+        from_x = exchange(scaled, "grp", 2)
+        from_core = exchange(scaled, "grp", 1)
+        from_dev = exchange(scaled, "dev", 1)
+        panel_shape = (rows // width, 2 * rows, slab)
+        panel = pltpu.VMEM(panel_shape, jnp.bfloat16)
+        full = pltpu.VMEM((panel_rows, slab), jnp.float32)
+        fresh = not blocks
+
+        if fresh:
+            jobs = [(last, False), (last, True)]
+            start, *brought = small(
+                functools.partial(first_kernel, width, jobs), "first_near", scalars,
+                [shaped(1, panel_rows, slab)] + [shaped(*block_shape)] * 2,
+                [panel, pltpu.SemaphoreType.DMA((4,))], products(1, rows), scaled, from_core, chi=chi_prev,
+            )
+            blocks.update(zip(jobs, brought))
+        else:
+            (start,) = small(
+                functools.partial(near_kernel, width), "near_half", scalars, [shaped(AHEAD, panel_rows, slab)],
+                [panel], products(AHEAD, rows), scaled, from_core, *[blocks[last - i, False] for i in range(AHEAD)],
+            )
+
+        from_x = after(from_x, start)
+        from_x_core = exchange(from_x, "grp", 1)
+        def far_slab(j, *earlier):
+            return small(
+                functools.partial(far_kernel, width, last - j), f"far_slab_{j}", scalars,
+                [shaped(panel_rows, half)] * 2, [panel, full], products(1, rows),
+                from_x, after(from_x_core, *earlier), start, blocks[j, True],
+            )
+
+        def held_slab(j, *earlier):
+            return small(
+                functools.partial(held_kernel, width), f"held_slab_{j}", scalars,
+                [shaped(panel_rows, half)] * 2, [pltpu.VMEM((2, *panel_shape), jnp.bfloat16), full],
+                products(2, rows),
+                scaled, from_core, from_x, after(from_x_core, *earlier), blocks[j, False], blocks[j, True],
+            )
+
+        def both_slabs(*slabs, earlier):
+            count = len(slabs)
+            jobs = [(j, far) for j in slabs for far in (False, True)]
+            outs = small(
+                functools.partial(both_kernel, width, jobs), f"both_slabs_{count}", scalars,
+                [shaped(panel_rows, half)] * (2 * count) + [shaped(*block_shape)] * (2 * count),
+                [pltpu.VMEM((2, *panel_shape), jnp.bfloat16), full, pltpu.SemaphoreType.DMA((4 * count,))],
+                products(2 * count, rows), scaled, from_core, from_x, after(from_x_core, *earlier), chi=chi_prev,
+            )
+            blocks.update(zip(jobs, outs[2 * count :]))
+            return outs[: 2 * count]
+
+        def slab_of(j, *earlier):
+            if fresh:
+                return both_slabs(j, earlier=earlier)
+            return (far_slab if last - j < AHEAD else held_slab)(j, *earlier)
+
+        send3, keep3 = far_slab(3, start, from_dev)
+        got3 = exchange(send3, "dev", 1)
+        keep, send = small(
+            functools.partial(project_kernel, width), "project", scalars, [shaped(width, pairs)] * 2,
+            [pltpu.VMEM((panel_rows, pairs), jnp.float32)],
+            (3 * 4 * rows * slab * pairs, 8 * slab * pairs),
+            scaled, after(from_dev, start, *(() if fresh else (send3,))), rho_re, rho_im,
+        )
+        total = keep + exchange(after(send, send3), "grp", 1)
+        from_z = exchange(total, "grp", 2)
+        send2, keep2 = slab_of(2, send3, keep)
+        got2 = exchange(send2, "dev", 1)
+        total = total + after(from_z, send2)
+        from_z = exchange(total, "col", 1)
+        sum3 = keep3 + got3
+        across = exchange(sum3, "col", 1)
+        send1, keep1 = slab_of(1, send2, total, sum3)
+        got1 = exchange(send1, "dev", 1)
+        total = total + after(from_z, send1)
+        from_z = exchange(total, "col", 2)
+        sum2 = keep2 + got2 + across
+        far = exchange(sum2, "col", 2)
+        send0, keep0 = slab_of(0, send1, total, sum2)
+        total = total + after(from_z, send0)
+        other = exchange(total, "grp", 1)
+        sum1 = keep1 + got1
+        near = exchange(sum1, "col", 1)
+        send0, keep0 = small(
+            functools.partial(spread_kernel, width), "spread", scalars, [shaped(panel_rows, half)] * 2,
+            [pltpu.VMEM((panel_rows, pairs), jnp.float32)],
+            (3 * 4 * panel_rows * slab * pairs, 8 * slab * pairs),
+            total, after(other, sum1), weight, rho_re, rho_im, send0, keep0,
+        )
+        got0 = exchange(send0, "dev", 1)
+        return keep0, got0, near, far
+
+    blocks = {}
+    own, by_dev, by_near, by_far = image(scaled, blocks)
+    pulled = scale * (own + by_dev + by_near + by_far)
+    real_part = bare + damping * (bare + pulled[:width] - bare)
+    imag_part = damping * pulled[width:]
+    iterate = jnp.concatenate([real_part, imag_part], axis=0)
+    for sweep in range(1, ITERS):
+        own, by_dev, by_near, by_far = image(scale * iterate, blocks)
+    return small(
+        functools.partial(end_kernel, width), "end", scalars, [shaped(half, width)] * 2,
+        [], (0, 4 * 8 * half * panel_rows),
+        own, by_dev, by_near, by_far, iterate, bare, scale,
+    )
+
+
 def solution(mesh):
     placed = (
         P(("grp", "col"), "dev"),
@@ -85,6 +477,14 @@
         P(),
         P(),
     )
+
+    def shards(*blocks):
+        half, width = blocks[4].shape
+        pairs = blocks[0].shape[1]
+        paired = mesh.shape["grp"] == 4 and mesh.shape["col"] == 4 and mesh.shape["dev"] == 2
+        tiled = half % 128 == 0 and width % 128 == 0 and pairs % 128 == 0
+        return (exchanged if paired and tiled and ITERS == 2 else general)(*blocks)
+
     return jax.shard_map(
         shards,
         mesh=mesh,

time: 480 us -> 142 us (0.30)
  waiting for transfers between devices: 308 us -> 52.8 us
  matrix products: 88.8 us -> 0 us
  Pallas kernels: 0 us -> 52.7 us
  starting transfers between devices: 0.25 us -> 32.7 us
  local copies, waits for them, and re-layouts: 32.5 us -> 1.66 us
  blocking collectives: 23.6 us -> 0 us
  between operations: 15.6 us -> 1.02 us
  other arithmetic: 11.3 us -> 0.84 us
    psum x2 -> x0, waiting for transfers between devices: 157 us -> none  [shards(): lax.psum(jnp.concatenate([proj_re, proj_im], axis=1), ('grp', 'col'))]
    reduce_scatter x2 -> x0, waiting for transfers between devices: 150 us -> none  [shards(): lax.psum_scatter(total, ('col', 'dev'), scatter_dimension=0, tiled=True)]
    dot_general x20 -> x0, matrix products: 88.8 us -> none  [the longest x12 81.5 us: contract(): lax.dot_general(left, right, (((0,), (0,)), ((), ())), precision=lax.Prec...]
    ppermute x0 -> x32, waiting for transfers between devices: none -> 52.8 us  [exchange(): return lax.ppermute(value, axis, [(i, i ^ flip) for i in range(size)])]
    pallas_call x0 -> x16, Pallas kernels: none -> 52.7 us  [small(): pl.pallas_call(kernel, name=name, in_specs=in_specs, out_specs=[vmem] * l...]
    ppermute x0 -> x32, starting transfers between devices: none -> 32.7 us  [exchange(): return lax.ppermute(value, axis, [(i, i ^ flip) for i in range(size)])]
    slice x1 -> x0, local copies, waits for them, and re-layouts: 26.2 us -> none  [shards(): tile_im = previous[1]]
    all_gather x2 -> x0, blocking collectives: 23.6 us -> none  [shards(): slab_scaled = lax.all_gather(scaled, 'dev', axis=0, tiled=True)]
  transfers between devices with their start and end apart: 6 -> 32, of which waited for: 4 -> 15; matrix products, arithmetic and copies ran while one was open for 7% -> 0% of each run, Pallas kernels for 0% -> 32%
where the time goes in v2:
time: 142 us
  waiting for transfers between devices  52.8 us (37%)
  Pallas kernels  52.7 us (37%)
  starting transfers between devices  32.7 us (23%)
  local copies, waits for them, and re-layouts  1.66 us (1%)
    ppermute x32, waiting for transfers between devices, exchange(): return lax.ppermute(value, axis, [(i, i ^ flip) for i in range(size)])  52.8 us
    pallas_call x16, Pallas kernels, small(): pl.pallas_call(kernel, name=name, in_specs=in_specs, out_specs=[vmem] * l...  52.7 us
    ppermute x32, starting transfers between devices, exchange(): return lax.ppermute(value, axis, [(i, i ^ flip) for i in range(size)])  32.7 us
  transfers between devices with their start and end apart: 32, of which 15 were waited for; matrix products, arithmetic and copies ran while one was open for 0% of the time, Pallas kernels for 32%

profile of v2, /device:TPU:0, one launch (start us, length us, event | category | flops | bytes accessed | tf_op | source)
XLA Modules:
  0.0 141.7 jit_solution(15884118327707596639)
XLA Ops:
  3.5 2.6 %collective-permute-start.2 = (f32[128,384]{1,0:T(8,128)S(1)}, f32[128,384]{1,0:T(8,128)S(1)}, u32[]{:S(2)}, u32[]{:S(2)}) collective-permute-start(f32[128,384]{1,0:T(8,128)S(1)} %get-tuple-element.60.near), channel_id=1, source_target_pairs={{0,16},{8,24},{16,0},{24,8},{1,17},{9,25},{17,1},{25,9},{2,18},{10... | collective-permute-start | bytes 589832 | tf_op jit(solution)/shard_map/ppermute | solution.py:332
  7.6 4.4 %first_near.1 = (f32[1,256,768]{2,1,0:T(8,128)S(1)}, f32[2,2,384,768]{3,2,1,0:T(8,128)S(1)}, f32[2,2,384,768]{3,2,1,0:T(8,128)S(1)}) custom-call(s32[4]{0:T(128)S(1)} %pad_add_fusion.scalars, f32[128,384]{1,0:T(8,128)S(1)} %get-tuple-element.60.near, f32[128,384]{1,0:T(8,128)S(1)} %collective-permute-done.1.far.near_far, f32[2,4,1,384,3072]{4,3,2,1,0:T(8,128)} %chi.7), custom_call_target="tpu_custom_call" | custom-call | flops 14155776 | bytes 86016 | tf_op jit(solution)/shard_map/first_near/pallas_call | solution.py:119
  13.5 2.0 %far_slab_3.2 = (f32[256,384]{1,0:T(8,128)S(1)}, f32[256,384]{1,0:T(8,128)S(1)}) custom-call(s32[4]{0:T(128)S(1)} %pad_add_fusion.scalars, f32[128,384]{1,0:T(8,128)S(1)} %collective-permute-done.2.near.far, f32[128,384]{1,0:T(8,128)S(1)} %collective-permute-done.3.far.far_far, f32[1,256,768]{2,1,0:T(8,128)S(1)} %get-tuple-element.61.start, ...), custom_call_target="tpu_custom_call" | custom-call | flops 14155776 | bytes 86016 | tf_op jit(solution)/shard_map/far_slab_3/pallas_call | solution.py:119
  18.2 5.5 %both_slabs_1.3 = (f32[256,384]{1,0:T(8,128)S(1)}, f32[256,384]{1,0:T(8,128)S(1)}, f32[2,2,384,768]{3,2,1,0:T(8,128)S(1)}, f32[2,2,384,768]{3,2,1,0:T(8,128)S(1)}) custom-call(s32[4]{0:T(128)S(1)} %pad_add_fusion.scalars, f32[128,384]{1,0:T(8,128)S(1)} %get-tuple-element.60.near, f32[128,384]{1,0:T(8,128)S(1)} %collective-permute-done.1.far.near_far, ...), custom_call_target="tpu_custom_call" | custom-call | flops 28311552 | bytes 172032 | tf_op jit(solution)/shard_map/both_slabs_1/pallas_call | solution.py:119
  24.5 2.3 %collective-permute-done.7 = f32[256,384]{1,0:T(8,128)S(1)} collective-permute-done((f32[256,384]{1,0:T(8,128)S(1)}, f32[256,384]{1,0:T(8,128)S(1)}, u32[]{:S(2)}, u32[]{:S(2)}) %collective-permute-start.7) | collective-permute-done | bytes 393248 | tf_op jit(solution)/shard_map/ppermute | solution.py:332
  26.9 1.6 %collective-permute-start.10 = (f32[256,384]{1,0:T(8,128)S(1)}, f32[256,384]{1,0:T(8,128)S(1)}, u32[]{:S(2)}, u32[]{:S(2)}) collective-permute-start(f32[256,384]{1,0:T(8,128)S(1)} %add.87), channel_id=1, source_target_pairs={{0,2},{2,0},{4,6},{6,4},{1,3},{3,1},{5,7},{7,5},{8,10},{10,8},{12,... | collective-permute-start | bytes 1179656 | tf_op jit(solution)/shard_map/ppermute | solution.py:332
  29.8 3.7 %collective-permute-done.5 = f32[128,256]{1,0:T(8,128)S(1)} collective-permute-done((f32[128,256]{1,0:T(8,128)S(1)}, f32[128,256]{1,0:T(8,128)S(1)}, u32[]{:S(2)}, u32[]{:S(2)}) %collective-permute-start.5) | collective-permute-done | bytes 131104 | tf_op jit(solution)/shard_map/ppermute | solution.py:332
  34.3 5.5 %both_slabs_1.4 = (f32[256,384]{1,0:T(8,128)S(1)}, f32[256,384]{1,0:T(8,128)S(1)}, f32[2,2,384,768]{3,2,1,0:T(8,128)S(1)}, f32[2,2,384,768]{3,2,1,0:T(8,128)S(1)}) custom-call(s32[4]{0:T(128)S(1)} %pad_add_fusion.scalars, f32[128,384]{1,0:T(8,128)S(1)} %get-tuple-element.60.near, f32[128,384]{1,0:T(8,128)S(1)} %collective-permute-done.1.far.near_far, ...), custom_call_target="tpu_custom_call" | custom-call | flops 28311552 | bytes 172032 | tf_op jit(solution)/shard_map/both_slabs_1/pallas_call | solution.py:119
  39.7 1.8 %collective-permute-start.12 = (f32[256,384]{1,0:T(8,128)S(1)}, f32[256,384]{1,0:T(8,128)S(1)}, u32[]{:S(2)}, u32[]{:S(2)}) collective-permute-start(f32[256,384]{1,0:T(8,128)S(1)} %get-tuple-element.75), channel_id=1, source_target_pairs={{0,1},{1,0},{2,3},{3,2},{4,5},{5,4},{6,7},{7,6},{8,9},{9,8},{10,11... | collective-permute-start | bytes 1179656 | tf_op jit(solution)/shard_map/ppermute | solution.py:332
  41.5 2.6 %collective-permute-start.8 = (f32[128,256]{1,0:T(8,128)S(1)}, f32[128,256]{1,0:T(8,128)S(1)}, u32[]{:S(2)}, u32[]{:S(2)}) collective-permute-start(f32[128,256]{1,0:T(8,128)S(1)} %add.88), channel_id=1, source_target_pairs={{0,4},{2,6},{4,0},{6,2},{1,5},{3,7},{5,1},{7,3},{8,12},{10,14},{12... | collective-permute-start | bytes 393224 | tf_op jit(solution)/shard_map/ppermute | solution.py:332
  44.2 5.6 %both_slabs_1.5 = (f32[256,384]{1,0:T(8,128)S(1)}, f32[256,384]{1,0:T(8,128)S(1)}, f32[2,2,384,768]{3,2,1,0:T(8,128)S(1)}, f32[2,2,384,768]{3,2,1,0:T(8,128)S(1)}) custom-call(s32[4]{0:T(128)S(1)} %pad_add_fusion.scalars, f32[128,384]{1,0:T(8,128)S(1)} %get-tuple-element.60.near, f32[128,384]{1,0:T(8,128)S(1)} %collective-permute-done.1.far.near_far, ...), custom_call_target="tpu_custom_call" | custom-call | flops 28311552 | bytes 172032 | tf_op jit(solution)/shard_map/both_slabs_1/pallas_call | solution.py:119
  50.5 2.6 %collective-permute-start.14 = (f32[256,384]{1,0:T(8,128)S(1)}, f32[256,384]{1,0:T(8,128)S(1)}, u32[]{:S(2)}, u32[]{:S(2)}) collective-permute-start(f32[256,384]{1,0:T(8,128)S(1)} %add.92), channel_id=1, source_target_pairs={{0,2},{2,0},{4,6},{6,4},{1,3},{3,1},{5,7},{7,5},{8,10},{10,8},{12,... | collective-permute-start | bytes 1179656 | tf_op jit(solution)/shard_map/ppermute | solution.py:332
  55.3 12.6 %collective-permute-done.14 = f32[256,384]{1,0:T(8,128)S(1)} collective-permute-done((f32[256,384]{1,0:T(8,128)S(1)}, f32[256,384]{1,0:T(8,128)S(1)}, u32[]{:S(2)}, u32[]{:S(2)}) %collective-permute-start.14) | collective-permute-done | bytes 393248 | tf_op jit(solution)/shard_map/ppermute | solution.py:332
  67.9 2.9 %collective-permute-done.15 = f32[256,384]{1,0:T(8,128)S(1)} collective-permute-done((f32[256,384]{1,0:T(8,128)S(1)}, f32[256,384]{1,0:T(8,128)S(1)}, u32[]{:S(2)}, u32[]{:S(2)}) %collective-permute-start.15) | collective-permute-done | bytes 393248 | tf_op jit(solution)/shard_map/ppermute | solution.py:332
  71.1 1.9 %collective-permute-start.18 = (f32[256,384]{1,0:T(8,128)S(1)}, f32[256,384]{1,0:T(8,128)S(1)}, u32[]{:S(2)}, u32[]{:S(2)}) collective-permute-start(f32[256,384]{1,0:T(8,128)S(1)} %get-tuple-element.121.near), channel_id=1, source_target_pairs={{0,16},{8,24},{16,0},{24,8},{1,17},{9,25},{17,1},{25,9},{2,18},{10... | collective-permute-start | bytes 1179656 | tf_op jit(solution)/shard_map/ppermute | solution.py:332
  73.0 7.0 %near_half.1.start = f32[3,256,768]{2,1,0:T(8,128)S(1)} custom-call(s32[4]{0:T(128)S(1)} %pad_add_fusion.scalars, f32[256,384]{1,0:T(8,128)S(1)} %get-tuple-element.121.near, f32[256,384]{1,0:T(8,128)S(1)} %collective-permute-done.17.far.near_far, f32[2,2,384,768]{3,2,1,0:T(8,128)S(1)} %get-tuple-element.86.rest_0_, ...), custom_call_target="tpu_custom_call" | custom-call | flops 84934656 | bytes 258048 | tf_op jit(solution)/shard_map/near_half/pallas_call | solution.py:119
  80.0 2.7 %collective-permute-done.18.near.far = f32[256,384]{1,0:T(8,128)S(1)} collective-permute-done((f32[256,384]{1,0:T(8,128)S(1)}, f32[256,384]{1,0:T(8,128)S(1)}, u32[]{:S(2)}, u32[]{:S(2)}) %collective-permute-start.18) | collective-permute-done | bytes 393248 | tf_op jit(solution)/shard_map/ppermute | solution.py:332
  84.4 3.1 %far_slab_3.3 = (f32[256,384]{1,0:T(8,128)S(1)}, f32[256,384]{1,0:T(8,128)S(1)}) custom-call(s32[4]{0:T(128)S(1)} %pad_add_fusion.scalars, f32[256,384]{1,0:T(8,128)S(1)} %collective-permute-done.18.near.far, f32[256,384]{1,0:T(8,128)S(1)} %collective-permute-done.19.far.far_far, f32[3,256,768]{2,1,0:T(8,128)S(1)} %near_half.1.start, ...), custom_call_target="tpu_custom_call" | custom-call | flops 28311552 | bytes 86016 | tf_op jit(solution)/shard_map/far_slab_3/pallas_call | solution.py:119
  88.0 1.6 %project.3 = (f32[128,256]{1,0:T(8,128)S(1)}, f32[128,256]{1,0:T(8,128)S(1)}) custom-call(s32[4]{0:T(128)S(1)} %pad_add_fusion.scalars, f32[256,384]{1,0:T(8,128)S(1)} %get-tuple-element.121.near, f32[256,384]{1,0:T(8,128)S(1)} %collective-permute-done.16.far, f32[768,256]{1,0:T(8,128)S(1)} %copy-done, f32[768,256]{1,0:T(8,128)S(1)} %copy-done.1), custom_call_target="tpu_custom_call" | custom-call | flops 9437184 | bytes 24576 | tf_op jit(solution)/shard_map/project/pallas_call | solution.py:119
  89.7 3.1 %far_slab_2.1 = (f32[256,384]{1,0:T(8,128)S(1)}, f32[256,384]{1,0:T(8,128)S(1)}) custom-call(s32[4]{0:T(128)S(1)} %pad_add_fusion.scalars, f32[256,384]{1,0:T(8,128)S(1)} %collective-permute-done.18.near.far, f32[256,384]{1,0:T(8,128)S(1)} %collective-permute-done.19.far.far_far, f32[3,256,768]{2,1,0:T(8,128)S(1)} %near_half.1.start, ...), custom_call_target="tpu_custom_call" | custom-call | flops 28311552 | bytes 86016 | tf_op jit(solution)/shard_map/far_slab_2/pallas_call | solution.py:119
  92.7 1.7 %collective-permute-start.25 = (f32[256,384]{1,0:T(8,128)S(1)}, f32[256,384]{1,0:T(8,128)S(1)}, u32[]{:S(2)}, u32[]{:S(2)}) collective-permute-start(f32[256,384]{1,0:T(8,128)S(1)} %get-tuple-element.98), channel_id=1, source_target_pairs={{0,1},{1,0},{2,3},{3,2},{4,5},{5,4},{6,7},{7,6},{8,9},{9,8},{10,11... | collective-permute-start | bytes 1179656 | tf_op jit(solution)/shard_map/ppermute | solution.py:332
  94.4 5.1 %collective-permute-done.23 = f32[256,384]{1,0:T(8,128)S(1)} collective-permute-done((f32[256,384]{1,0:T(8,128)S(1)}, f32[256,384]{1,0:T(8,128)S(1)}, u32[]{:S(2)}, u32[]{:S(2)}) %collective-permute-start.23) | collective-permute-done | bytes 393248 | tf_op jit(solution)/shard_map/ppermute | solution.py:332
  99.7 1.8 %collective-permute-start.21 = (f32[128,256]{1,0:T(8,128)S(1)}, f32[128,256]{1,0:T(8,128)S(1)}, u32[]{:S(2)}, u32[]{:S(2)}) collective-permute-start(f32[128,256]{1,0:T(8,128)S(1)} %add.101), channel_id=1, source_target_pairs={{0,16},{8,24},{16,0},{24,8},{1,17},{9,25},{17,1},{25,9},{2,18},{10... | collective-permute-start | bytes 393224 | tf_op jit(solution)/shard_map/ppermute | solution.py:332
  101.5 3.2 %collective-permute-done.21 = f32[128,256]{1,0:T(8,128)S(1)} collective-permute-done((f32[128,256]{1,0:T(8,128)S(1)}, f32[128,256]{1,0:T(8,128)S(1)}, u32[]{:S(2)}, u32[]{:S(2)}) %collective-permute-start.21) | collective-permute-done | bytes 131104 | tf_op jit(solution)/shard_map/ppermute | solution.py:332
  104.8 2.1 %collective-permute-start.22 = (f32[128,256]{1,0:T(8,128)S(1)}, f32[128,256]{1,0:T(8,128)S(1)}, u32[]{:S(2)}, u32[]{:S(2)}) collective-permute-start(f32[128,256]{1,0:T(8,128)S(1)} %add.102), channel_id=1, source_target_pairs={{0,2},{2,0},{4,6},{6,4},{1,3},{3,1},{5,7},{7,5},{8,10},{10,8},{12,... | collective-permute-start | bytes 393224 | tf_op jit(solution)/shard_map/ppermute | solution.py:332
  106.8 3.3 %far_slab_1.1 = (f32[256,384]{1,0:T(8,128)S(1)}, f32[256,384]{1,0:T(8,128)S(1)}) custom-call(s32[4]{0:T(128)S(1)} %pad_add_fusion.scalars, f32[256,384]{1,0:T(8,128)S(1)} %collective-permute-done.18.near.far, f32[256,384]{1,0:T(8,128)S(1)} %collective-permute-done.19.far.far_far, f32[3,256,768]{2,1,0:T(8,128)S(1)} %near_half.1.start, ...), custom_call_target="tpu_custom_call" | custom-call | flops 28311552 | bytes 86016 | tf_op jit(solution)/shard_map/far_slab_1/pallas_call | solution.py:119
  112.0 1.8 %collective-permute-start.24 = (f32[128,256]{1,0:T(8,128)S(1)}, f32[128,256]{1,0:T(8,128)S(1)}, u32[]{:S(2)}, u32[]{:S(2)}) collective-permute-start(f32[128,256]{1,0:T(8,128)S(1)} %add.104), channel_id=1, source_target_pairs={{0,4},{2,6},{4,0},{6,2},{1,5},{3,7},{5,1},{7,3},{8,12},{10,14},{12... | collective-permute-start | bytes 393224 | tf_op jit(solution)/shard_map/ppermute | solution.py:332
  113.8 5.3 %held_slab_0.1 = (f32[256,384]{1,0:T(8,128)S(1)}, f32[256,384]{1,0:T(8,128)S(1)}) custom-call(s32[4]{0:T(128)S(1)} %pad_add_fusion.scalars, f32[256,384]{1,0:T(8,128)S(1)} %get-tuple-element.121.near, f32[256,384]{1,0:T(8,128)S(1)} %collective-permute-done.17.far.near_far, f32[256,384]{1,0:T(8,128)S(1)} %collective-permute-done.18.near.far, ...), custom_call_target="tpu_custom_call" | custom-call | flops 56623104 | bytes 172032 | tf_op jit(solution)/shard_map/held_slab_0/pallas_call | solution.py:119
  120.6 2.2 %collective-permute-start.30 = (f32[256,384]{1,0:T(8,128)S(1)}, f32[256,384]{1,0:T(8,128)S(1)}, u32[]{:S(2)}, u32[]{:S(2)}) collective-permute-start(f32[256,384]{1,0:T(8,128)S(1)} %add.108), channel_id=1, source_target_pairs={{0,2},{2,0},{4,6},{6,4},{1,3},{3,1},{5,7},{7,5},{8,10},{10,8},{12,... | collective-permute-start | bytes 1179656 | tf_op jit(solution)/shard_map/ppermute | solution.py:332
  122.8 1.6 %spread.3 = (f32[256,384]{1,0:T(8,128)S(1)}, f32[256,384]{1,0:T(8,128)S(1)}) custom-call(s32[4]{0:T(128)S(1)} %pad_add_fusion.scalars, f32[128,256]{1,0:T(8,128)S(1)} %add.107.near, f32[128,256]{1,0:T(8,128)S(1)} %collective-permute-done.27.far, f32[1,256]{1,0:T(1,128)S(1)} %bitcast.6, f32[768,256]{1,0:T(8,128)S(1)} %copy-done, f32[768,256]{1,0:T(8,128)S(1)} %copy-done.1, ...), custom_call_target="tpu_custom_call" | custom-call | flops 9437184 | bytes 24576 | tf_op jit(solution)/shard_map/spread/pallas_call | solution.py:119
  124.7 13.3 %collective-permute-done.30.by_near = f32[256,384]{1,0:T(8,128)S(1)} collective-permute-done((f32[256,384]{1,0:T(8,128)S(1)}, f32[256,384]{1,0:T(8,128)S(1)}, u32[]{:S(2)}, u32[]{:S(2)}) %collective-permute-start.30) | collective-permute-done | bytes 393248 | tf_op jit(solution)/shard_map/ppermute | solution.py:332
  138.0 2.3 %collective-permute-done.31.by_far = f32[256,384]{1,0:T(8,128)S(1)} collective-permute-done((f32[256,384]{1,0:T(8,128)S(1)}, f32[256,384]{1,0:T(8,128)S(1)}, u32[]{:S(2)}, u32[]{:S(2)}) %collective-permute-start.31) | collective-permute-done | bytes 393248 | tf_op jit(solution)/shard_map/ppermute | solution.py:332
  (85 shorter events, 22.1 us)
Async XLA Ops:
  3.0 4.6 %collective-permute-start.1 = (f32[128,384]{1,0:T(8,128)S(1)}, f32[128,384]{1,0:T(8,128)S(1)}, u32[]{:S(2)}, u32[]{:S(2)}) collective-permute-start(f32[128,384]{1,0:T(8,128)S(1)} %get-tuple-element.60.near), channel_id=1, source_target_pairs={{0,8},{8,0},{16,24},{24,16},{1,9},{9,1},{17,25},{25,17},{2,10},{10... | collective-permute-start | bytes 589832 | tf_op jit(solution)/shard_map/ppermute | solution.py:332
  3.5 8.5 %collective-permute-start.2 = (f32[128,384]{1,0:T(8,128)S(1)}, f32[128,384]{1,0:T(8,128)S(1)}, u32[]{:S(2)}, u32[]{:S(2)}) collective-permute-start(f32[128,384]{1,0:T(8,128)S(1)} %get-tuple-element.60.near), channel_id=1, source_target_pairs={{0,16},{8,24},{16,0},{24,8},{1,17},{9,25},{17,1},{25,9},{2,18},{10... | collective-permute-start | bytes 589832 | tf_op jit(solution)/shard_map/ppermute | solution.py:332
  6.1 7.0 %collective-permute-start = (f32[128,384]{1,0:T(8,128)S(1)}, f32[128,384]{1,0:T(8,128)S(1)}, u32[]{:S(2)}, u32[]{:S(2)}) collective-permute-start(f32[128,384]{1,0:T(8,128)S(1)} %get-tuple-element.60.near), channel_id=1, source_target_pairs={{0,1},{1,0},{2,3},{3,2},{4,5},{5,4},{6,7},{7,6},{8,9},{9,8},{10,11... | collective-permute-start | bytes 589832 | tf_op jit(solution)/shard_map/ppermute | solution.py:332
  12.0 1.5 %collective-permute-start.3 = (f32[128,384]{1,0:T(8,128)S(1)}, f32[128,384]{1,0:T(8,128)S(1)}, u32[]{:S(2)}, u32[]{:S(2)}) collective-permute-start(f32[128,384]{1,0:T(8,128)S(1)} %collective-permute-done.2.near.far), channel_id=1, source_target_pairs={{0,8},{8,0},{16,24},{24,16},{1,9},{9,1},{17,25},{25,17},{2,10},{10... | collective-permute-start | bytes 589832 | tf_op jit(solution)/shard_map/ppermute | solution.py:332
  15.6 11.2 %collective-permute-start.7 = (f32[256,384]{1,0:T(8,128)S(1)}, f32[256,384]{1,0:T(8,128)S(1)}, u32[]{:S(2)}, u32[]{:S(2)}) collective-permute-start(f32[256,384]{1,0:T(8,128)S(1)} %get-tuple-element.68), channel_id=1, source_target_pairs={{0,1},{1,0},{2,3},{3,2},{4,5},{5,4},{6,7},{7,6},{8,9},{9,8},{10,11... | collective-permute-start | bytes 1179656 | tf_op jit(solution)/shard_map/ppermute | solution.py:332
  18.1 10.4 %collective-permute-start.4 = (f32[128,256]{1,0:T(8,128)S(1)}, f32[128,256]{1,0:T(8,128)S(1)}, u32[]{:S(2)}, u32[]{:S(2)}) collective-permute-start(f32[128,256]{1,0:T(8,128)S(1)} %get-tuple-element.69), channel_id=1, source_target_pairs={{0,8},{8,0},{16,24},{24,16},{1,9},{9,1},{17,25},{25,17},{2,10},{10... | collective-permute-start | bytes 393224 | tf_op jit(solution)/shard_map/ppermute | solution.py:332
  23.7 20.4 %collective-permute-start.9 = (f32[256,384]{1,0:T(8,128)S(1)}, f32[256,384]{1,0:T(8,128)S(1)}, u32[]{:S(2)}, u32[]{:S(2)}) collective-permute-start(f32[256,384]{1,0:T(8,128)S(1)} %get-tuple-element.71), channel_id=1, source_target_pairs={{0,1},{1,0},{2,3},{3,2},{4,5},{5,4},{6,7},{7,6},{8,9},{9,8},{10,11... | collective-permute-start | bytes 1179656 | tf_op jit(solution)/shard_map/ppermute | solution.py:332
  26.9 17.3 %collective-permute-start.10 = (f32[256,384]{1,0:T(8,128)S(1)}, f32[256,384]{1,0:T(8,128)S(1)}, u32[]{:S(2)}, u32[]{:S(2)}) collective-permute-start(f32[256,384]{1,0:T(8,128)S(1)} %add.87), channel_id=1, source_target_pairs={{0,2},{2,0},{4,6},{6,4},{1,3},{3,1},{5,7},{7,5},{8,10},{10,8},{12,... | collective-permute-start | bytes 1179656 | tf_op jit(solution)/shard_map/ppermute | solution.py:332
  28.5 5.0 %collective-permute-start.5 = (f32[128,256]{1,0:T(8,128)S(1)}, f32[128,256]{1,0:T(8,128)S(1)}, u32[]{:S(2)}, u32[]{:S(2)}) collective-permute-start(f32[128,256]{1,0:T(8,128)S(1)} %add.85), channel_id=1, source_target_pairs={{0,16},{8,24},{16,0},{24,8},{1,17},{9,25},{17,1},{25,9},{2,18},{10... | collective-permute-start | bytes 393224 | tf_op jit(solution)/shard_map/ppermute | solution.py:332
  33.6 8.0 %collective-permute-start.6 = (f32[128,256]{1,0:T(8,128)S(1)}, f32[128,256]{1,0:T(8,128)S(1)}, u32[]{:S(2)}, u32[]{:S(2)}) collective-permute-start(f32[128,256]{1,0:T(8,128)S(1)} %add.86), channel_id=1, source_target_pairs={{0,2},{2,0},{4,6},{6,4},{1,3},{3,1},{5,7},{7,5},{8,10},{10,8},{12,... | collective-permute-start | bytes 393224 | tf_op jit(solution)/shard_map/ppermute | solution.py:332
  39.7 10.7 %collective-permute-start.12 = (f32[256,384]{1,0:T(8,128)S(1)}, f32[256,384]{1,0:T(8,128)S(1)}, u32[]{:S(2)}, u32[]{:S(2)}) collective-permute-start(f32[256,384]{1,0:T(8,128)S(1)} %get-tuple-element.75), channel_id=1, source_target_pairs={{0,1},{1,0},{2,3},{3,2},{4,5},{5,4},{6,7},{7,6},{8,9},{9,8},{10,11... | collective-permute-start | bytes 1179656 | tf_op jit(solution)/shard_map/ppermute | solution.py:332
  41.5 8.3 %collective-permute-start.8 = (f32[128,256]{1,0:T(8,128)S(1)}, f32[128,256]{1,0:T(8,128)S(1)}, u32[]{:S(2)}, u32[]{:S(2)}) collective-permute-start(f32[128,256]{1,0:T(8,128)S(1)} %add.88), channel_id=1, source_target_pairs={{0,4},{2,6},{4,0},{6,2},{1,5},{3,7},{5,1},{7,3},{8,12},{10,14},{12... | collective-permute-start | bytes 393224 | tf_op jit(solution)/shard_map/ppermute | solution.py:332
  49.9 3.3 %collective-permute-start.11 = (f32[128,256]{1,0:T(8,128)S(1)}, f32[128,256]{1,0:T(8,128)S(1)}, u32[]{:S(2)}, u32[]{:S(2)}) collective-permute-start(f32[128,256]{1,0:T(8,128)S(1)} %add.91.near), channel_id=1, source_target_pairs={{0,8},{8,0},{16,24},{24,16},{1,9},{9,1},{17,25},{25,17},{2,10},{10... | collective-permute-start | bytes 393224 | tf_op jit(solution)/shard_map/ppermute | solution.py:332
  50.0 20.9 %collective-permute-start.15 = (f32[256,384]{1,0:T(8,128)S(1)}, f32[256,384]{1,0:T(8,128)S(1)}, u32[]{:S(2)}, u32[]{:S(2)}) collective-permute-start(f32[256,384]{1,0:T(8,128)S(1)} %add_add_fusion.1), channel_id=1, source_target_pairs={{0,4},{2,6},{4,0},{6,2},{1,5},{3,7},{5,1},{7,3},{8,12},{10,14},{12... | collective-permute-start | bytes 1179656 | tf_op jit(solution)/shard_map/ppermute | solution.py:332
  50.5 17.4 %collective-permute-start.14 = (f32[256,384]{1,0:T(8,128)S(1)}, f32[256,384]{1,0:T(8,128)S(1)}, u32[]{:S(2)}, u32[]{:S(2)}) collective-permute-start(f32[256,384]{1,0:T(8,128)S(1)} %add.92), channel_id=1, source_target_pairs={{0,2},{2,0},{4,6},{6,4},{1,3},{3,1},{5,7},{7,5},{8,10},{10,8},{12,... | collective-permute-start | bytes 1179656 | tf_op jit(solution)/shard_map/ppermute | solution.py:332
  54.7 16.1 %collective-permute-start.13 = (f32[256,384]{1,0:T(8,128)S(1)}, f32[256,384]{1,0:T(8,128)S(1)}, u32[]{:S(2)}, u32[]{:S(2)}) collective-permute-start(f32[256,384]{1,0:T(8,128)S(1)} %get-tuple-element.85), channel_id=1, source_target_pairs={{0,1},{1,0},{2,3},{3,2},{4,5},{5,4},{6,7},{7,6},{8,9},{9,8},{10,11... | collective-permute-start | bytes 1179656 | tf_op jit(solution)/shard_map/ppermute | solution.py:332
  71.0 2.0 %collective-permute-start.17 = (f32[256,384]{1,0:T(8,128)S(1)}, f32[256,384]{1,0:T(8,128)S(1)}, u32[]{:S(2)}, u32[]{:S(2)}) collective-permute-start(f32[256,384]{1,0:T(8,128)S(1)} %get-tuple-element.121.near), channel_id=1, source_target_pairs={{0,8},{8,0},{16,24},{24,16},{1,9},{9,1},{17,25},{25,17},{2,10},{10... | collective-permute-start | bytes 1179656 | tf_op jit(solution)/shard_map/ppermute | solution.py:332
  71.1 11.6 %collective-permute-start.18 = (f32[256,384]{1,0:T(8,128)S(1)}, f32[256,384]{1,0:T(8,128)S(1)}, u32[]{:S(2)}, u32[]{:S(2)}) collective-permute-start(f32[256,384]{1,0:T(8,128)S(1)} %get-tuple-element.121.near), channel_id=1, source_target_pairs={{0,16},{8,24},{16,0},{24,8},{1,17},{9,25},{17,1},{25,9},{2,18},{10... | collective-permute-start | bytes 1179656 | tf_op jit(solution)/shard_map/ppermute | solution.py:332
  73.0 11.2 %collective-permute-start.16 = (f32[256,384]{1,0:T(8,128)S(1)}, f32[256,384]{1,0:T(8,128)S(1)}, u32[]{:S(2)}, u32[]{:S(2)}) collective-permute-start(f32[256,384]{1,0:T(8,128)S(1)} %get-tuple-element.121.near), channel_id=1, source_target_pairs={{0,1},{1,0},{2,3},{3,2},{4,5},{5,4},{6,7},{7,6},{8,9},{9,8},{10,11... | collective-permute-start | bytes 1179656 | tf_op jit(solution)/shard_map/ppermute | solution.py:332
  82.7 1.7 %collective-permute-start.19 = (f32[256,384]{1,0:T(8,128)S(1)}, f32[256,384]{1,0:T(8,128)S(1)}, u32[]{:S(2)}, u32[]{:S(2)}) collective-permute-start(f32[256,384]{1,0:T(8,128)S(1)} %collective-permute-done.18.near.far), channel_id=1, source_target_pairs={{0,8},{8,0},{16,24},{24,16},{1,9},{9,1},{17,25},{25,17},{2,10},{10... | collective-permute-start | bytes 1179656 | tf_op jit(solution)/shard_map/ppermute | solution.py:332
  87.5 12.0 %collective-permute-start.23 = (f32[256,384]{1,0:T(8,128)S(1)}, f32[256,384]{1,0:T(8,128)S(1)}, u32[]{:S(2)}, u32[]{:S(2)}) collective-permute-start(f32[256,384]{1,0:T(8,128)S(1)} %get-tuple-element.91), channel_id=1, source_target_pairs={{0,1},{1,0},{2,3},{3,2},{4,5},{5,4},{6,7},{7,6},{8,9},{9,8},{10,11... | collective-permute-start | bytes 1179656 | tf_op jit(solution)/shard_map/ppermute | solution.py:332
  89.6 10.1 %collective-permute-start.20 = (f32[128,256]{1,0:T(8,128)S(1)}, f32[128,256]{1,0:T(8,128)S(1)}, u32[]{:S(2)}, u32[]{:S(2)}) collective-permute-start(f32[128,256]{1,0:T(8,128)S(1)} %get-tuple-element.95), channel_id=1, source_target_pairs={{0,8},{8,0},{16,24},{24,16},{1,9},{9,1},{17,25},{25,17},{2,10},{10... | collective-permute-start | bytes 393224 | tf_op jit(solution)/shard_map/ppermute | solution.py:332
  92.7 21.0 %collective-permute-start.25 = (f32[256,384]{1,0:T(8,128)S(1)}, f32[256,384]{1,0:T(8,128)S(1)}, u32[]{:S(2)}, u32[]{:S(2)}) collective-permute-start(f32[256,384]{1,0:T(8,128)S(1)} %get-tuple-element.98), channel_id=1, source_target_pairs={{0,1},{1,0},{2,3},{3,2},{4,5},{5,4},{6,7},{7,6},{8,9},{9,8},{10,11... | collective-permute-start | bytes 1179656 | tf_op jit(solution)/shard_map/ppermute | solution.py:332
  99.6 14.2 %collective-permute-start.26 = (f32[256,384]{1,0:T(8,128)S(1)}, f32[256,384]{1,0:T(8,128)S(1)}, u32[]{:S(2)}, u32[]{:S(2)}) collective-permute-start(f32[256,384]{1,0:T(8,128)S(1)} %add.103), channel_id=1, source_target_pairs={{0,2},{2,0},{4,6},{6,4},{1,3},{3,1},{5,7},{7,5},{8,10},{10,8},{12,... | collective-permute-start | bytes 1179656 | tf_op jit(solution)/shard_map/ppermute | solution.py:332
  99.7 5.0 %collective-permute-start.21 = (f32[128,256]{1,0:T(8,128)S(1)}, f32[128,256]{1,0:T(8,128)S(1)}, u32[]{:S(2)}, u32[]{:S(2)}) collective-permute-start(f32[128,256]{1,0:T(8,128)S(1)} %add.101), channel_id=1, source_target_pairs={{0,16},{8,24},{16,0},{24,8},{1,17},{9,25},{17,1},{25,9},{2,18},{10... | collective-permute-start | bytes 393224 | tf_op jit(solution)/shard_map/ppermute | solution.py:332
  104.8 7.2 %collective-permute-start.22 = (f32[128,256]{1,0:T(8,128)S(1)}, f32[128,256]{1,0:T(8,128)S(1)}, u32[]{:S(2)}, u32[]{:S(2)}) collective-permute-start(f32[128,256]{1,0:T(8,128)S(1)} %add.102), channel_id=1, source_target_pairs={{0,2},{2,0},{4,6},{6,4},{1,3},{3,1},{5,7},{7,5},{8,10},{10,8},{12,... | collective-permute-start | bytes 393224 | tf_op jit(solution)/shard_map/ppermute | solution.py:332
  110.1 10.4 %collective-permute-start.28 = (f32[256,384]{1,0:T(8,128)S(1)}, f32[256,384]{1,0:T(8,128)S(1)}, u32[]{:S(2)}, u32[]{:S(2)}) collective-permute-start(f32[256,384]{1,0:T(8,128)S(1)} %get-tuple-element.103), channel_id=1, source_target_pairs={{0,1},{1,0},{2,3},{3,2},{4,5},{5,4},{6,7},{7,6},{8,9},{9,8},{10,11... | collective-permute-start | bytes 1179656 | tf_op jit(solution)/shard_map/ppermute | solution.py:332
  112.0 7.3 %collective-permute-start.24 = (f32[128,256]{1,0:T(8,128)S(1)}, f32[128,256]{1,0:T(8,128)S(1)}, u32[]{:S(2)}, u32[]{:S(2)}) collective-permute-start(f32[128,256]{1,0:T(8,128)S(1)} %add.104), channel_id=1, source_target_pairs={{0,4},{2,6},{4,0},{6,2},{1,5},{3,7},{5,1},{7,3},{8,12},{10,14},{12... | collective-permute-start | bytes 393224 | tf_op jit(solution)/shard_map/ppermute | solution.py:332
  119.3 3.5 %collective-permute-start.27 = (f32[128,256]{1,0:T(8,128)S(1)}, f32[128,256]{1,0:T(8,128)S(1)}, u32[]{:S(2)}, u32[]{:S(2)}) collective-permute-start(f32[128,256]{1,0:T(8,128)S(1)} %add.107.near), channel_id=1, source_target_pairs={{0,8},{8,0},{16,24},{24,16},{1,9},{9,1},{17,25},{25,17},{2,10},{10... | collective-permute-start | bytes 393224 | tf_op jit(solution)/shard_map/ppermute | solution.py:332
  119.4 20.9 %collective-permute-start.31 = (f32[256,384]{1,0:T(8,128)S(1)}, f32[256,384]{1,0:T(8,128)S(1)}, u32[]{:S(2)}, u32[]{:S(2)}) collective-permute-start(f32[256,384]{1,0:T(8,128)S(1)} %add_add_fusion), channel_id=1, source_target_pairs={{0,4},{2,6},{4,0},{6,2},{1,5},{3,7},{5,1},{7,3},{8,12},{10,14},{12... | collective-permute-start | bytes 1179656 | tf_op jit(solution)/shard_map/ppermute | solution.py:332
  120.6 17.4 %collective-permute-start.30 = (f32[256,384]{1,0:T(8,128)S(1)}, f32[256,384]{1,0:T(8,128)S(1)}, u32[]{:S(2)}, u32[]{:S(2)}) collective-permute-start(f32[256,384]{1,0:T(8,128)S(1)} %add.108), channel_id=1, source_target_pairs={{0,2},{2,0},{4,6},{6,4},{1,3},{3,1},{5,7},{7,5},{8,10},{10,8},{12,... | collective-permute-start | bytes 1179656 | tf_op jit(solution)/shard_map/ppermute | solution.py:332
  124.3 15.9 %collective-permute-start.29 = (f32[256,384]{1,0:T(8,128)S(1)}, f32[256,384]{1,0:T(8,128)S(1)}, u32[]{:S(2)}, u32[]{:S(2)}) collective-permute-start(f32[256,384]{1,0:T(8,128)S(1)} %get-tuple-element.115), channel_id=1, source_target_pairs={{0,1},{1,0},{2,3},{3,2},{4,5},{5,4},{6,7},{7,6},{8,9},{9,8},{10,11... | collective-permute-start | bytes 1179656 | tf_op jit(solution)/shard_map/ppermute | solution.py:332
  (8 other events, 101.0 us)

commit v3 on v2

--- a/solution.py
+++ b/solution.py
@@ -15,7 +15,6 @@
 MIB = 1 << 20
 DEPTH = 4
 LIMIT = 8
-HURRY = 64
 AHEAD = 3
 
 
@@ -123,7 +122,7 @@
         out_specs=[vmem] * len(out_shape),
         out_shape=out_shape,
         scratch_shapes=scratch,
-        cost_estimate=pl.CostEstimate(flops=cost[0] // HURRY, bytes_accessed=cost[1] // HURRY, transcendentals=0),
+        cost_estimate=pl.CostEstimate(flops=cost[0], bytes_accessed=cost[1], transcendentals=0),
         compiler_params=pltpu.CompilerParams(vmem_limit_bytes=limit * MIB),
     )(scalars, *operands)
 
@@ -183,33 +182,7 @@
 def begin_kernel(scalars, source, coulomb, bare, scaled):
     turned = source[...].T
     bare[...] = turned
-    scaled[...] = turned * coulomb[...]
-
-
-def each_block(count, chi, buffers, sems, place, use):
-    slots, slab = buffers.shape[0], buffers.shape[-1]
-
-    def copy(t):
-        part, pair, row = place(t)
-        at = pl.ds(pl.multiple_of(row * slab, slab), slab)
-        slot = lax.rem(t, slots)
-        return pltpu.make_async_copy(chi.at[part, pl.ds(2 * pair, 2), 0, :, at], buffers.at[slot], sems.at[slot])
-
-    def step(t, carry):
-        copy(t).wait()
-
-        @pl.when((t == 0) & (count > 1))
-        def _():
-            copy(t + 1).start()
-
-        @pl.when(t + 2 < count)
-        def _():
-            copy(t + 2).start()
-
-        use(t, buffers[lax.rem(t, slots)].reshape(slab, slab))
-        return carry
-
-    return copy, step
+    scaled[...] = turned * coulomb[...][None, :]
 
 
 def first_kernel(width, jobs, scalars, near, far, chi, out, *rest):
@@ -313,8 +286,8 @@
         out[width:] = given[width:] - (by_re[width:] + by_im[:width])
 
 
-def end_kernel(width, scalars, own, by_dev, by_near, by_far, iterate, bare, coulomb, out_re, out_im):
-    image = coulomb[...] * (own[...] + by_dev[...] + by_near[...] + by_far[...])
+def end_kernel(width, scalars, own, by_dev, iterate, bare, coulomb, out_re, out_im):
+    image = coulomb[...] * (own[...] + by_dev[...])
     real_part = iterate[:width]
     imag_part = iterate[width:]
     real_part = real_part + damping * (bare[...] + image[:width] - real_part)
@@ -347,7 +320,7 @@
     scale = coulomb[None, :]
 
     bare, scaled = small(
-        begin_kernel, "begin", scalars, [shaped(width, half)] * 2, [], (0, 12 * half * width), source, scale
+        begin_kernel, "begin", scalars, [shaped(width, half)] * 2, [], (0, 12 * half * width), source, coulomb
     )
 
     def products(blocks, rows):
@@ -365,6 +338,7 @@
         panel = pltpu.VMEM(panel_shape, jnp.bfloat16)
         full = pltpu.VMEM((panel_rows, slab), jnp.float32)
         fresh = not blocks
+
 
         if fresh:
             jobs = [(last, False), (last, True)]
@@ -397,21 +371,20 @@
                 scaled, from_core, from_x, after(from_x_core, *earlier), blocks[j, False], blocks[j, True],
             )
 
-        def both_slabs(*slabs, earlier):
-            count = len(slabs)
-            jobs = [(j, far) for j in slabs for far in (False, True)]
-            outs = small(
-                functools.partial(both_kernel, width, jobs), f"both_slabs_{count}", scalars,
-                [shaped(panel_rows, half)] * (2 * count) + [shaped(*block_shape)] * (2 * count),
-                [pltpu.VMEM((2, *panel_shape), jnp.bfloat16), full, pltpu.SemaphoreType.DMA((4 * count,))],
-                products(2 * count, rows), scaled, from_core, from_x, after(from_x_core, *earlier), chi=chi_prev,
+        def both_slab(j, *earlier):
+            jobs = [(j, False), (j, True)]
+            *outs, near_block, far_block = small(
+                functools.partial(both_kernel, width, jobs), f"both_slabs_{j}", scalars,
+                [shaped(panel_rows, half)] * 2 + [shaped(*block_shape)] * 2,
+                [pltpu.VMEM((2, *panel_shape), jnp.bfloat16), full, pltpu.SemaphoreType.DMA((4,))],
+                products(2, rows), scaled, from_core, from_x, after(from_x_core, *earlier), chi=chi_prev,
             )
-            blocks.update(zip(jobs, outs[2 * count :]))
-            return outs[: 2 * count]
+            blocks.update(zip(jobs, (near_block, far_block)))
+            return outs
 
         def slab_of(j, *earlier):
             if fresh:
-                return both_slabs(j, earlier=earlier)
+                return both_slab(j, *earlier)
             return (far_slab if last - j < AHEAD else held_slab)(j, *earlier)
 
         send3, keep3 = far_slab(3, start, from_dev)
@@ -420,26 +393,23 @@
             functools.partial(project_kernel, width), "project", scalars, [shaped(width, pairs)] * 2,
             [pltpu.VMEM((panel_rows, pairs), jnp.float32)],
             (3 * 4 * rows * slab * pairs, 8 * slab * pairs),
-            scaled, after(from_dev, start, *(() if fresh else (send3,))), rho_re, rho_im,
+            scaled, after(from_dev, start, send3), rho_re, rho_im,
         )
-        total = keep + exchange(after(send, send3), "grp", 1)
-        from_z = exchange(total, "grp", 2)
-        send2, keep2 = slab_of(2, send3, keep)
+        total = keep + exchange(send, "grp", 1)
+        send2, keep2 = slab_of(2, send3, total)
         got2 = exchange(send2, "dev", 1)
-        total = total + after(from_z, send2)
-        from_z = exchange(total, "col", 1)
-        sum3 = keep3 + got3
+        total = total + exchange(total, "col", 1)
+        sum3 = keep3 + after(got3, total)
         across = exchange(sum3, "col", 1)
         send1, keep1 = slab_of(1, send2, total, sum3)
         got1 = exchange(send1, "dev", 1)
-        total = total + after(from_z, send1)
-        from_z = exchange(total, "col", 2)
+        total = total + after(exchange(total, "grp", 2), send1)
         sum2 = keep2 + got2 + across
         far = exchange(sum2, "col", 2)
-        send0, keep0 = slab_of(0, send1, total, sum2)
-        total = total + after(from_z, send0)
+        send0, keep0 = slab_of(0, send1, total)
+        total = total + after(exchange(total, "col", 2), send0)
         other = exchange(total, "grp", 1)
-        sum1 = keep1 + got1
+        sum1 = keep1 + after(got1, send0)
         near = exchange(sum1, "col", 1)
         send0, keep0 = small(
             functools.partial(spread_kernel, width), "spread", scalars, [shaped(panel_rows, half)] * 2,
@@ -448,20 +418,22 @@
             total, after(other, sum1), weight, rho_re, rho_im, send0, keep0,
         )
         got0 = exchange(send0, "dev", 1)
-        return keep0, got0, near, far
+        mine = keep0 + far
+        mine = mine + after(near, mine)
+        return mine, after(got0, mine)
 
     blocks = {}
-    own, by_dev, by_near, by_far = image(scaled, blocks)
-    pulled = scale * (own + by_dev + by_near + by_far)
+    mine, by_dev = image(scaled, blocks)
+    pulled = scale * (mine + by_dev)
     real_part = bare + damping * (bare + pulled[:width] - bare)
     imag_part = damping * pulled[width:]
     iterate = jnp.concatenate([real_part, imag_part], axis=0)
     for sweep in range(1, ITERS):
-        own, by_dev, by_near, by_far = image(scale * iterate, blocks)
+        mine, by_dev = image(scale * iterate, blocks)
     return small(
         functools.partial(end_kernel, width), "end", scalars, [shaped(half, width)] * 2,
         [], (0, 4 * 8 * half * panel_rows),
-        own, by_dev, by_near, by_far, iterate, bare, scale,
+        mine, by_dev, iterate, bare, scale,
     )
 
 

time: 142 us -> 130 us (0.915)
  waiting for transfers between devices: 52.8 us -> 43.6 us
  starting transfers between devices: 32.7 us -> 30.8 us
    ppermute x32, waiting for transfers between devices: 52.8 us -> 43.6 us  [exchange(): return lax.ppermute(value, axis, [(i, i ^ flip) for i in range(size)])]
    ppermute x32, starting transfers between devices: 32.7 us -> 30.8 us  [exchange(): return lax.ppermute(value, axis, [(i, i ^ flip) for i in range(size)])]
  transfers between devices with their start and end apart: 32 -> 32, of which waited for: 15 -> 16; matrix products, arithmetic and copies ran while one was open for 0% -> 1% of each run, Pallas kernels for 32% -> 34%
where the time goes in v3:
time: 130 us
  Pallas kernels  51.7 us (40%)
  waiting for transfers between devices  43.6 us (34%)
  starting transfers between devices  30.8 us (24%)
  local copies, waits for them, and re-layouts  1.66 us (1%)
    pallas_call x16, Pallas kernels, small(): pl.pallas_call(kernel, name=name, in_specs=in_specs, out_specs=[vmem] * l...  51.7 us
    ppermute x32, waiting for transfers between devices, exchange(): return lax.ppermute(value, axis, [(i, i ^ flip) for i in range(size)])  43.6 us
    ppermute x32, starting transfers between devices, exchange(): return lax.ppermute(value, axis, [(i, i ^ flip) for i in range(size)])  30.8 us
  transfers between devices with their start and end apart: 32, of which 16 were waited for; matrix products, arithmetic and copies ran while one was open for 1% of the time, Pallas kernels for 34%

profile of v3, /device:TPU:0, one launch (start us, length us, event | category | flops | bytes accessed | tf_op | source)
XLA Modules:
  0.0 129.9 jit_solution(16941377837376441917)
XLA Ops:
  3.5 2.6 %collective-permute-start.2 = (f32[128,384]{1,0:T(8,128)S(1)}, f32[128,384]{1,0:T(8,128)S(1)}, u32[]{:S(2)}, u32[]{:S(2)}) collective-permute-start(f32[128,384]{1,0:T(8,128)S(1)} %get-tuple-element.64.near), channel_id=1, source_target_pairs={{0,16},{8,24},{16,0},{24,8},{1,17},{9,25},{17,1},{25,9},{2,18},{10... | collective-permute-start | bytes 589832 | tf_op jit(solution)/shard_map/ppermute | solution.py:305
  6.1 1.5 %collective-permute-start = (f32[128,384]{1,0:T(8,128)S(1)}, f32[128,384]{1,0:T(8,128)S(1)}, u32[]{:S(2)}, u32[]{:S(2)}) collective-permute-start(f32[128,384]{1,0:T(8,128)S(1)} %get-tuple-element.64.near), channel_id=1, source_target_pairs={{0,1},{1,0},{2,3},{3,2},{4,5},{5,4},{6,7},{7,6},{8,9},{9,8},{10,11... | collective-permute-start | bytes 589832 | tf_op jit(solution)/shard_map/ppermute | solution.py:305
  7.6 4.4 %first_near.1 = (f32[1,256,768]{2,1,0:T(8,128)S(1)}, f32[2,2,384,768]{3,2,1,0:T(8,128)S(1)}, f32[2,2,384,768]{3,2,1,0:T(8,128)S(1)}) custom-call(s32[4]{0:T(128)S(1)} %pad_add_fusion.scalars, f32[128,384]{1,0:T(8,128)S(1)} %get-tuple-element.64.near, f32[128,384]{1,0:T(8,128)S(1)} %collective-permute-done.1.far.near_far, f32[2,4,1,384,3072]{4,3,2,1,0:T(8,128)} %chi.7), custom_call_target="tpu_custom_call" | custom-call | flops 905969664 | bytes 5505024 | tf_op jit(solution)/shard_map/first_near/pallas_call | solution.py:118
  13.6 2.0 %far_slab_3.2 = (f32[256,384]{1,0:T(8,128)S(1)}, f32[256,384]{1,0:T(8,128)S(1)}) custom-call(s32[4]{0:T(128)S(1)} %pad_add_fusion.scalars, f32[128,384]{1,0:T(8,128)S(1)} %collective-permute-done.2.near.far, f32[128,384]{1,0:T(8,128)S(1)} %collective-permute-done.3.far.far_far, f32[1,256,768]{2,1,0:T(8,128)S(1)} %get-tuple-element.65.start, ...), custom_call_target="tpu_custom_call" | custom-call | flops 905969664 | bytes 5505024 | tf_op jit(solution)/shard_map/far_slab_3/pallas_call | solution.py:118
  15.6 1.3 collective-permute-start.7
  19.5 1.7 %collective-permute-start.5 = (f32[128,256]{1,0:T(8,128)S(1)}, f32[128,256]{1,0:T(8,128)S(1)}, u32[]{:S(2)}, u32[]{:S(2)}) collective-permute-start(f32[128,256]{1,0:T(8,128)S(1)} %add.91), channel_id=1, source_target_pairs={{0,2},{2,0},{4,6},{6,4},{1,3},{3,1},{5,7},{7,5},{8,10},{10,8},{12,... | collective-permute-start | bytes 393224 | tf_op jit(solution)/shard_map/ppermute | solution.py:305
  21.2 5.4 %both_slabs_2.1 = (f32[256,384]{1,0:T(8,128)S(1)}, f32[256,384]{1,0:T(8,128)S(1)}, f32[2,2,384,768]{3,2,1,0:T(8,128)S(1)}, f32[2,2,384,768]{3,2,1,0:T(8,128)S(1)}) custom-call(s32[4]{0:T(128)S(1)} %pad_add_fusion.scalars, f32[128,384]{1,0:T(8,128)S(1)} %get-tuple-element.64.near, f32[128,384]{1,0:T(8,128)S(1)} %collective-permute-done.1.far.near_far, ...), custom_call_target="tpu_custom_call" | custom-call | flops 1811939328 | bytes 11010048 | tf_op jit(solution)/shard_map/both_slabs_2/pallas_call | solution.py:118
  29.8 5.5 %both_slabs_1.1 = (f32[256,384]{1,0:T(8,128)S(1)}, f32[256,384]{1,0:T(8,128)S(1)}, f32[2,2,384,768]{3,2,1,0:T(8,128)S(1)}, f32[2,2,384,768]{3,2,1,0:T(8,128)S(1)}) custom-call(s32[4]{0:T(128)S(1)} %pad_add_fusion.scalars, f32[128,384]{1,0:T(8,128)S(1)} %get-tuple-element.64.near, f32[128,384]{1,0:T(8,128)S(1)} %collective-permute-done.1.far.near_far, ...), custom_call_target="tpu_custom_call" | custom-call | flops 1811939328 | bytes 11010048 | tf_op jit(solution)/shard_map/both_slabs_1/pallas_call | solution.py:118
  35.2 1.6 %collective-permute-start.10 = (f32[256,384]{1,0:T(8,128)S(1)}, f32[256,384]{1,0:T(8,128)S(1)}, u32[]{:S(2)}, u32[]{:S(2)}) collective-permute-start(f32[256,384]{1,0:T(8,128)S(1)} %get-tuple-element.78), channel_id=1, source_target_pairs={{0,1},{1,0},{2,3},{3,2},{4,5},{5,4},{6,7},{7,6},{8,9},{9,8},{10,11... | collective-permute-start | bytes 1179656 | tf_op jit(solution)/shard_map/ppermute | solution.py:305
  36.8 2.7 %collective-permute-start.8 = (f32[128,256]{1,0:T(8,128)S(1)}, f32[128,256]{1,0:T(8,128)S(1)}, u32[]{:S(2)}, u32[]{:S(2)}) collective-permute-start(f32[128,256]{1,0:T(8,128)S(1)} %add.94), channel_id=1, source_target_pairs={{0,4},{2,6},{4,0},{6,2},{1,5},{3,7},{5,1},{7,3},{8,12},{10,14},{12... | collective-permute-start | bytes 393224 | tf_op jit(solution)/shard_map/ppermute | solution.py:305
  39.5 5.3 %both_slabs_0.1 = (f32[256,384]{1,0:T(8,128)S(1)}, f32[256,384]{1,0:T(8,128)S(1)}, f32[2,2,384,768]{3,2,1,0:T(8,128)S(1)}, f32[2,2,384,768]{3,2,1,0:T(8,128)S(1)}) custom-call(s32[4]{0:T(128)S(1)} %pad_add_fusion.scalars, f32[128,384]{1,0:T(8,128)S(1)} %get-tuple-element.64.near, f32[128,384]{1,0:T(8,128)S(1)} %collective-permute-done.1.far.near_far, ...), custom_call_target="tpu_custom_call" | custom-call | flops 1811939328 | bytes 11010048 | tf_op jit(solution)/shard_map/both_slabs_0/pallas_call | solution.py:118
  46.0 3.0 %collective-permute-start.14 = (f32[256,384]{1,0:T(8,128)S(1)}, f32[256,384]{1,0:T(8,128)S(1)}, u32[]{:S(2)}, u32[]{:S(2)}) collective-permute-start(f32[256,384]{1,0:T(8,128)S(1)} %add.96), channel_id=1, source_target_pairs={{0,2},{2,0},{4,6},{6,4},{1,3},{3,1},{5,7},{7,5},{8,10},{10,8},{12,... | collective-permute-start | bytes 1179656 | tf_op jit(solution)/shard_map/ppermute | solution.py:305
  49.0 1.6 %spread.2 = (f32[256,384]{1,0:T(8,128)S(1)}, f32[256,384]{1,0:T(8,128)S(1)}) custom-call(s32[4]{0:T(128)S(1)} %pad_add_fusion.scalars, f32[128,256]{1,0:T(8,128)S(1)} %add.95.near, f32[128,256]{1,0:T(8,128)S(1)} %collective-permute-done.9.far, f32[1,256]{1,0:T(1,128)S(1)} %bitcast.5, f32[768,256]{1,0:T(8,128)S(1)} %copy-done, f32[768,256]{1,0:T(8,128)S(1)} %copy-done.1, ...), custom_call_target="tpu_custom_call" | custom-call | flops 603979776 | bytes 1572864 | tf_op jit(solution)/shard_map/spread/pallas_call | solution.py:118
  51.1 15.0 %collective-permute-done.13 = f32[256,384]{1,0:T(8,128)S(1)} collective-permute-done((f32[256,384]{1,0:T(8,128)S(1)}, f32[256,384]{1,0:T(8,128)S(1)}, u32[]{:S(2)}, u32[]{:S(2)}) %collective-permute-start.13) | collective-permute-done | bytes 393248 | tf_op jit(solution)/shard_map/ppermute | solution.py:305
  68.3 6.8 %near_half.1.start = f32[3,256,768]{2,1,0:T(8,128)S(1)} custom-call(s32[4]{0:T(128)S(1)} %pad_add_fusion.scalars, f32[256,384]{1,0:T(8,128)S(1)} %get-tuple-element.129.near, f32[256,384]{1,0:T(8,128)S(1)} %collective-permute-done.17.far.near_far, f32[2,2,384,768]{3,2,1,0:T(8,128)S(1)} %get-tuple-element.92.rest_0_, ...), custom_call_target="tpu_custom_call" | custom-call | flops 5435817984 | bytes 16515072 | tf_op jit(solution)/shard_map/near_half/pallas_call | solution.py:118
  75.1 3.0 %collective-permute-done.18.near.far = f32[256,384]{1,0:T(8,128)S(1)} collective-permute-done((f32[256,384]{1,0:T(8,128)S(1)}, f32[256,384]{1,0:T(8,128)S(1)}, u32[]{:S(2)}, u32[]{:S(2)}) %collective-permute-start.18) | collective-permute-done | bytes 393248 | tf_op jit(solution)/shard_map/ppermute | solution.py:305
  78.3 1.6 %collective-permute-done.19.far.far_far = f32[256,384]{1,0:T(8,128)S(1)} collective-permute-done((f32[256,384]{1,0:T(8,128)S(1)}, f32[256,384]{1,0:T(8,128)S(1)}, u32[]{:S(2)}, u32[]{:S(2)}) %collective-permute-start.19) | collective-permute-done | bytes 393248 | tf_op jit(solution)/shard_map/ppermute | solution.py:305
  79.8 3.1 %far_slab_3.3 = (f32[256,384]{1,0:T(8,128)S(1)}, f32[256,384]{1,0:T(8,128)S(1)}) custom-call(s32[4]{0:T(128)S(1)} %pad_add_fusion.scalars, f32[256,384]{1,0:T(8,128)S(1)} %collective-permute-done.18.near.far, f32[256,384]{1,0:T(8,128)S(1)} %collective-permute-done.19.far.far_far, f32[3,256,768]{2,1,0:T(8,128)S(1)} %near_half.1.start, ...), custom_call_target="tpu_custom_call" | custom-call | flops 1811939328 | bytes 5505024 | tf_op jit(solution)/shard_map/far_slab_3/pallas_call | solution.py:118
  83.5 1.6 %project.3 = (f32[128,256]{1,0:T(8,128)S(1)}, f32[128,256]{1,0:T(8,128)S(1)}) custom-call(s32[4]{0:T(128)S(1)} %pad_add_fusion.scalars, f32[256,384]{1,0:T(8,128)S(1)} %get-tuple-element.129.near, f32[256,384]{1,0:T(8,128)S(1)} %collective-permute-done.16.far, f32[768,256]{1,0:T(8,128)S(1)} %copy-done, f32[768,256]{1,0:T(8,128)S(1)} %copy-done.1), custom_call_target="tpu_custom_call" | custom-call | flops 603979776 | bytes 1572864 | tf_op jit(solution)/shard_map/project/pallas_call | solution.py:118
  85.1 1.3 %collective-permute-done.20 = f32[128,256]{1,0:T(8,128)S(1)} collective-permute-done((f32[128,256]{1,0:T(8,128)S(1)}, f32[128,256]{1,0:T(8,128)S(1)}, u32[]{:S(2)}, u32[]{:S(2)}) %collective-permute-start.20) | collective-permute-done | bytes 131104 | tf_op jit(solution)/shard_map/ppermute | solution.py:305
  86.6 3.1 %far_slab_2.1 = (f32[256,384]{1,0:T(8,128)S(1)}, f32[256,384]{1,0:T(8,128)S(1)}) custom-call(s32[4]{0:T(128)S(1)} %pad_add_fusion.scalars, f32[256,384]{1,0:T(8,128)S(1)} %collective-permute-done.18.near.far, f32[256,384]{1,0:T(8,128)S(1)} %collective-permute-done.19.far.far_far, f32[3,256,768]{2,1,0:T(8,128)S(1)} %near_half.1.start, ...), custom_call_target="tpu_custom_call" | custom-call | flops 1811939328 | bytes 5505024 | tf_op jit(solution)/shard_map/far_slab_2/pallas_call | solution.py:118
  89.7 1.6 %collective-permute-start.27 = (f32[256,384]{1,0:T(8,128)S(1)}, f32[256,384]{1,0:T(8,128)S(1)}, u32[]{:S(2)}, u32[]{:S(2)}) collective-permute-start(f32[256,384]{1,0:T(8,128)S(1)} %get-tuple-element.103), channel_id=1, source_target_pairs={{0,1},{1,0},{2,3},{3,2},{4,5},{5,4},{6,7},{7,6},{8,9},{9,8},{10,11... | collective-permute-start | bytes 1179656 | tf_op jit(solution)/shard_map/ppermute | solution.py:305
  93.1 1.8 %collective-permute-done.23 = f32[256,384]{1,0:T(8,128)S(1)} collective-permute-done((f32[256,384]{1,0:T(8,128)S(1)}, f32[256,384]{1,0:T(8,128)S(1)}, u32[]{:S(2)}, u32[]{:S(2)}) %collective-permute-start.23) | collective-permute-done | bytes 393248 | tf_op jit(solution)/shard_map/ppermute | solution.py:305
  95.1 3.3 %far_slab_1.1 = (f32[256,384]{1,0:T(8,128)S(1)}, f32[256,384]{1,0:T(8,128)S(1)}) custom-call(s32[4]{0:T(128)S(1)} %pad_add_fusion.scalars, f32[256,384]{1,0:T(8,128)S(1)} %collective-permute-done.18.near.far, f32[256,384]{1,0:T(8,128)S(1)} %collective-permute-done.19.far.far_far, f32[3,256,768]{2,1,0:T(8,128)S(1)} %near_half.1.start, ...), custom_call_target="tpu_custom_call" | custom-call | flops 1811939328 | bytes 5505024 | tf_op jit(solution)/shard_map/far_slab_1/pallas_call | solution.py:118
  98.8 2.8 %collective-permute-start.24 = (f32[128,256]{1,0:T(8,128)S(1)}, f32[128,256]{1,0:T(8,128)S(1)}, u32[]{:S(2)}, u32[]{:S(2)}) collective-permute-start(f32[128,256]{1,0:T(8,128)S(1)} %add.110), channel_id=1, source_target_pairs={{0,4},{2,6},{4,0},{6,2},{1,5},{3,7},{5,1},{7,3},{8,12},{10,14},{12... | collective-permute-start | bytes 393224 | tf_op jit(solution)/shard_map/ppermute | solution.py:305
  101.6 5.0 %held_slab_0.1 = (f32[256,384]{1,0:T(8,128)S(1)}, f32[256,384]{1,0:T(8,128)S(1)}) custom-call(s32[4]{0:T(128)S(1)} %pad_add_fusion.scalars, f32[256,384]{1,0:T(8,128)S(1)} %get-tuple-element.129.near, f32[256,384]{1,0:T(8,128)S(1)} %collective-permute-done.17.far.near_far, f32[256,384]{1,0:T(8,128)S(1)} %collective-permute-done.18.near.far, ...), custom_call_target="tpu_custom_call" | custom-call | flops 3623878656 | bytes 11010048 | tf_op jit(solution)/shard_map/held_slab_0/pallas_call | solution.py:118
  107.4 1.4 %collective-permute-start.29 = (f32[256,384]{1,0:T(8,128)S(1)}, f32[256,384]{1,0:T(8,128)S(1)}, u32[]{:S(2)}, u32[]{:S(2)}) collective-permute-start(f32[256,384]{1,0:T(8,128)S(1)} %add_add_fusion), channel_id=1, source_target_pairs={{0,4},{2,6},{4,0},{6,2},{1,5},{3,7},{5,1},{7,3},{8,12},{10,14},{12... | collective-permute-start | bytes 1179656 | tf_op jit(solution)/shard_map/ppermute | solution.py:305
  108.8 2.2 %collective-permute-done.26 = f32[256,384]{1,0:T(8,128)S(1)} collective-permute-done((f32[256,384]{1,0:T(8,128)S(1)}, f32[256,384]{1,0:T(8,128)S(1)}, u32[]{:S(2)}, u32[]{:S(2)}) %collective-permute-start.26) | collective-permute-done | bytes 393248 | tf_op jit(solution)/shard_map/ppermute | solution.py:305
  111.2 1.6 %spread.3 = (f32[256,384]{1,0:T(8,128)S(1)}, f32[256,384]{1,0:T(8,128)S(1)}) custom-call(s32[4]{0:T(128)S(1)} %pad_add_fusion.scalars, f32[128,256]{1,0:T(8,128)S(1)} %add.111.near, f32[128,256]{1,0:T(8,128)S(1)} %collective-permute-done.25.far, f32[1,256]{1,0:T(1,128)S(1)} %bitcast.6, f32[768,256]{1,0:T(8,128)S(1)} %copy-done, f32[768,256]{1,0:T(8,128)S(1)} %copy-done.1, ...), custom_call_target="tpu_custom_call" | custom-call | flops 603979776 | bytes 1572864 | tf_op jit(solution)/shard_map/spread/pallas_call | solution.py:118
  112.7 1.6 %collective-permute-start.31 = (f32[256,384]{1,0:T(8,128)S(1)}, f32[256,384]{1,0:T(8,128)S(1)}, u32[]{:S(2)}, u32[]{:S(2)}) collective-permute-start(f32[256,384]{1,0:T(8,128)S(1)} %get-tuple-element.122), channel_id=1, source_target_pairs={{0,1},{1,0},{2,3},{3,2},{4,5},{5,4},{6,7},{7,6},{8,9},{9,8},{10,11... | collective-permute-start | bytes 1179656 | tf_op jit(solution)/shard_map/ppermute | solution.py:305
  114.3 13.4 %collective-permute-done.29 = f32[256,384]{1,0:T(8,128)S(1)} collective-permute-done((f32[256,384]{1,0:T(8,128)S(1)}, f32[256,384]{1,0:T(8,128)S(1)}, u32[]{:S(2)}, u32[]{:S(2)}) %collective-permute-start.29) | collective-permute-done | bytes 393248 | tf_op jit(solution)/shard_map/ppermute | solution.py:305
  128.5 1.4 %end.1 = (f32[384,128]{1,0:T(8,128)}, f32[384,128]{1,0:T(8,128)}) custom-call(s32[4]{0:T(128)S(1)} %pad_add_fusion.scalars, f32[256,384]{1,0:T(8,128)S(1)} %add.116.own, f32[256,384]{1,0:T(8,128)S(1)} %collective-permute-done.31.by_dev, f32[256,384]{1,0:T(8,128)S(1)} %get-tuple-element.128.iterate, f32[128,384]{1,0:T(8,128)S(1)} %get-tuple-element.63.bare, ...), custom_call_target="tpu_custom_call" | custom-call | bytes 3145728 | tf_op jit(solution)/shard_map/end/pallas_call | solution.py:118
  (91 shorter events, 19.0 us)
Async XLA Ops:
  3.0 4.6 %collective-permute-start.1 = (f32[128,384]{1,0:T(8,128)S(1)}, f32[128,384]{1,0:T(8,128)S(1)}, u32[]{:S(2)}, u32[]{:S(2)}) collective-permute-start(f32[128,384]{1,0:T(8,128)S(1)} %get-tuple-element.64.near), channel_id=1, source_target_pairs={{0,8},{8,0},{16,24},{24,16},{1,9},{9,1},{17,25},{25,17},{2,10},{10... | collective-permute-start | bytes 589832 | tf_op jit(solution)/shard_map/ppermute | solution.py:305
  3.5 8.5 %collective-permute-start.2 = (f32[128,384]{1,0:T(8,128)S(1)}, f32[128,384]{1,0:T(8,128)S(1)}, u32[]{:S(2)}, u32[]{:S(2)}) collective-permute-start(f32[128,384]{1,0:T(8,128)S(1)} %get-tuple-element.64.near), channel_id=1, source_target_pairs={{0,16},{8,24},{16,0},{24,8},{1,17},{9,25},{17,1},{25,9},{2,18},{10... | collective-permute-start | bytes 589832 | tf_op jit(solution)/shard_map/ppermute | solution.py:305
  6.1 7.0 %collective-permute-start = (f32[128,384]{1,0:T(8,128)S(1)}, f32[128,384]{1,0:T(8,128)S(1)}, u32[]{:S(2)}, u32[]{:S(2)}) collective-permute-start(f32[128,384]{1,0:T(8,128)S(1)} %get-tuple-element.64.near), channel_id=1, source_target_pairs={{0,1},{1,0},{2,3},{3,2},{4,5},{5,4},{6,7},{7,6},{8,9},{9,8},{10,11... | collective-permute-start | bytes 589832 | tf_op jit(solution)/shard_map/ppermute | solution.py:305
  12.1 1.5 %collective-permute-start.3 = (f32[128,384]{1,0:T(8,128)S(1)}, f32[128,384]{1,0:T(8,128)S(1)}, u32[]{:S(2)}, u32[]{:S(2)}) collective-permute-start(f32[128,384]{1,0:T(8,128)S(1)} %collective-permute-done.2.near.far), channel_id=1, source_target_pairs={{0,8},{8,0},{16,24},{24,16},{1,9},{9,1},{17,25},{25,17},{2,10},{10... | collective-permute-start | bytes 589832 | tf_op jit(solution)/shard_map/ppermute | solution.py:305
  15.6 11.9 %collective-permute-start.7 = (f32[256,384]{1,0:T(8,128)S(1)}, f32[256,384]{1,0:T(8,128)S(1)}, u32[]{:S(2)}, u32[]{:S(2)}) collective-permute-start(f32[256,384]{1,0:T(8,128)S(1)} %get-tuple-element.69), channel_id=1, source_target_pairs={{0,1},{1,0},{2,3},{3,2},{4,5},{5,4},{6,7},{7,6},{8,9},{9,8},{10,11... | collective-permute-start | bytes 1179656 | tf_op jit(solution)/shard_map/ppermute | solution.py:305
  18.1 1.4 %collective-permute-start.4 = (f32[128,256]{1,0:T(8,128)S(1)}, f32[128,256]{1,0:T(8,128)S(1)}, u32[]{:S(2)}, u32[]{:S(2)}) collective-permute-start(f32[128,256]{1,0:T(8,128)S(1)} %get-tuple-element.72), channel_id=1, source_target_pairs={{0,8},{8,0},{16,24},{24,16},{1,9},{9,1},{17,25},{25,17},{2,10},{10... | collective-permute-start | bytes 393224 | tf_op jit(solution)/shard_map/ppermute | solution.py:305
  19.5 7.9 %collective-permute-start.5 = (f32[128,256]{1,0:T(8,128)S(1)}, f32[128,256]{1,0:T(8,128)S(1)}, u32[]{:S(2)}, u32[]{:S(2)}) collective-permute-start(f32[128,256]{1,0:T(8,128)S(1)} %add.91), channel_id=1, source_target_pairs={{0,2},{2,0},{4,6},{6,4},{1,3},{3,1},{5,7},{7,5},{8,10},{10,8},{12,... | collective-permute-start | bytes 393224 | tf_op jit(solution)/shard_map/ppermute | solution.py:305
  26.6 18.5 %collective-permute-start.11 = (f32[256,384]{1,0:T(8,128)S(1)}, f32[256,384]{1,0:T(8,128)S(1)}, u32[]{:S(2)}, u32[]{:S(2)}) collective-permute-start(f32[256,384]{1,0:T(8,128)S(1)} %get-tuple-element.74), channel_id=1, source_target_pairs={{0,1},{1,0},{2,3},{3,2},{4,5},{5,4},{6,7},{7,6},{8,9},{9,8},{10,11... | collective-permute-start | bytes 1179656 | tf_op jit(solution)/shard_map/ppermute | solution.py:305
  27.6 17.6 %collective-permute-start.12 = (f32[256,384]{1,0:T(8,128)S(1)}, f32[256,384]{1,0:T(8,128)S(1)}, u32[]{:S(2)}, u32[]{:S(2)}) collective-permute-start(f32[256,384]{1,0:T(8,128)S(1)} %add.93), channel_id=1, source_target_pairs={{0,2},{2,0},{4,6},{6,4},{1,3},{3,1},{5,7},{7,5},{8,10},{10,8},{12,... | collective-permute-start | bytes 1179656 | tf_op jit(solution)/shard_map/ppermute | solution.py:305
  28.5 8.3 %collective-permute-start.6 = (f32[128,256]{1,0:T(8,128)S(1)}, f32[128,256]{1,0:T(8,128)S(1)}, u32[]{:S(2)}, u32[]{:S(2)}) collective-permute-start(f32[128,256]{1,0:T(8,128)S(1)} %add.92), channel_id=1, source_target_pairs={{0,16},{8,24},{16,0},{24,8},{1,17},{9,25},{17,1},{25,9},{2,18},{10... | collective-permute-start | bytes 393224 | tf_op jit(solution)/shard_map/ppermute | solution.py:305
  35.2 10.8 %collective-permute-start.10 = (f32[256,384]{1,0:T(8,128)S(1)}, f32[256,384]{1,0:T(8,128)S(1)}, u32[]{:S(2)}, u32[]{:S(2)}) collective-permute-start(f32[256,384]{1,0:T(8,128)S(1)} %get-tuple-element.78), channel_id=1, source_target_pairs={{0,1},{1,0},{2,3},{3,2},{4,5},{5,4},{6,7},{7,6},{8,9},{9,8},{10,11... | collective-permute-start | bytes 1179656 | tf_op jit(solution)/shard_map/ppermute | solution.py:305
  36.8 8.0 %collective-permute-start.8 = (f32[128,256]{1,0:T(8,128)S(1)}, f32[128,256]{1,0:T(8,128)S(1)}, u32[]{:S(2)}, u32[]{:S(2)}) collective-permute-start(f32[128,256]{1,0:T(8,128)S(1)} %add.94), channel_id=1, source_target_pairs={{0,4},{2,6},{4,0},{6,2},{1,5},{3,7},{5,1},{7,3},{8,12},{10,14},{12... | collective-permute-start | bytes 393224 | tf_op jit(solution)/shard_map/ppermute | solution.py:305
  44.8 4.2 %collective-permute-start.9 = (f32[128,256]{1,0:T(8,128)S(1)}, f32[128,256]{1,0:T(8,128)S(1)}, u32[]{:S(2)}, u32[]{:S(2)}) collective-permute-start(f32[128,256]{1,0:T(8,128)S(1)} %add.95.near), channel_id=1, source_target_pairs={{0,8},{8,0},{16,24},{24,16},{1,9},{9,1},{17,25},{25,17},{2,10},{10... | collective-permute-start | bytes 393224 | tf_op jit(solution)/shard_map/ppermute | solution.py:305
  45.2 21.0 %collective-permute-start.13 = (f32[256,384]{1,0:T(8,128)S(1)}, f32[256,384]{1,0:T(8,128)S(1)}, u32[]{:S(2)}, u32[]{:S(2)}) collective-permute-start(f32[256,384]{1,0:T(8,128)S(1)} %add_add_fusion.1), channel_id=1, source_target_pairs={{0,4},{2,6},{4,0},{6,2},{1,5},{3,7},{5,1},{7,3},{8,12},{10,14},{12... | collective-permute-start | bytes 1179656 | tf_op jit(solution)/shard_map/ppermute | solution.py:305
  46.0 20.2 %collective-permute-start.14 = (f32[256,384]{1,0:T(8,128)S(1)}, f32[256,384]{1,0:T(8,128)S(1)}, u32[]{:S(2)}, u32[]{:S(2)}) collective-permute-start(f32[256,384]{1,0:T(8,128)S(1)} %add.96), channel_id=1, source_target_pairs={{0,2},{2,0},{4,6},{6,4},{1,3},{3,1},{5,7},{7,5},{8,10},{10,8},{12,... | collective-permute-start | bytes 1179656 | tf_op jit(solution)/shard_map/ppermute | solution.py:305
  50.6 15.7 %collective-permute-start.15 = (f32[256,384]{1,0:T(8,128)S(1)}, f32[256,384]{1,0:T(8,128)S(1)}, u32[]{:S(2)}, u32[]{:S(2)}) collective-permute-start(f32[256,384]{1,0:T(8,128)S(1)} %get-tuple-element.90), channel_id=1, source_target_pairs={{0,1},{1,0},{2,3},{3,2},{4,5},{5,4},{6,7},{7,6},{8,9},{9,8},{10,11... | collective-permute-start | bytes 1179656 | tf_op jit(solution)/shard_map/ppermute | solution.py:305
  66.5 1.8 %collective-permute-start.17 = (f32[256,384]{1,0:T(8,128)S(1)}, f32[256,384]{1,0:T(8,128)S(1)}, u32[]{:S(2)}, u32[]{:S(2)}) collective-permute-start(f32[256,384]{1,0:T(8,128)S(1)} %get-tuple-element.129.near), channel_id=1, source_target_pairs={{0,8},{8,0},{16,24},{24,16},{1,9},{9,1},{17,25},{25,17},{2,10},{10... | collective-permute-start | bytes 1179656 | tf_op jit(solution)/shard_map/ppermute | solution.py:305
  66.6 11.5 %collective-permute-start.18 = (f32[256,384]{1,0:T(8,128)S(1)}, f32[256,384]{1,0:T(8,128)S(1)}, u32[]{:S(2)}, u32[]{:S(2)}) collective-permute-start(f32[256,384]{1,0:T(8,128)S(1)} %get-tuple-element.129.near), channel_id=1, source_target_pairs={{0,16},{8,24},{16,0},{24,8},{1,17},{9,25},{17,1},{25,9},{2,18},{10... | collective-permute-start | bytes 1179656 | tf_op jit(solution)/shard_map/ppermute | solution.py:305
  67.1 11.2 %collective-permute-start.16 = (f32[256,384]{1,0:T(8,128)S(1)}, f32[256,384]{1,0:T(8,128)S(1)}, u32[]{:S(2)}, u32[]{:S(2)}) collective-permute-start(f32[256,384]{1,0:T(8,128)S(1)} %get-tuple-element.129.near), channel_id=1, source_target_pairs={{0,1},{1,0},{2,3},{3,2},{4,5},{5,4},{6,7},{7,6},{8,9},{9,8},{10,11... | collective-permute-start | bytes 1179656 | tf_op jit(solution)/shard_map/ppermute | solution.py:305
  78.1 1.7 %collective-permute-start.19 = (f32[256,384]{1,0:T(8,128)S(1)}, f32[256,384]{1,0:T(8,128)S(1)}, u32[]{:S(2)}, u32[]{:S(2)}) collective-permute-start(f32[256,384]{1,0:T(8,128)S(1)} %collective-permute-done.18.near.far), channel_id=1, source_target_pairs={{0,8},{8,0},{16,24},{24,16},{1,9},{9,1},{17,25},{25,17},{2,10},{10... | collective-permute-start | bytes 1179656 | tf_op jit(solution)/shard_map/ppermute | solution.py:305
  82.9 12.0 %collective-permute-start.23 = (f32[256,384]{1,0:T(8,128)S(1)}, f32[256,384]{1,0:T(8,128)S(1)}, u32[]{:S(2)}, u32[]{:S(2)}) collective-permute-start(f32[256,384]{1,0:T(8,128)S(1)} %get-tuple-element.97), channel_id=1, source_target_pairs={{0,1},{1,0},{2,3},{3,2},{4,5},{5,4},{6,7},{7,6},{8,9},{9,8},{10,11... | collective-permute-start | bytes 1179656 | tf_op jit(solution)/shard_map/ppermute | solution.py:305
  85.1 1.4 %collective-permute-start.20 = (f32[128,256]{1,0:T(8,128)S(1)}, f32[128,256]{1,0:T(8,128)S(1)}, u32[]{:S(2)}, u32[]{:S(2)}) collective-permute-start(f32[128,256]{1,0:T(8,128)S(1)} %get-tuple-element.100), channel_id=1, source_target_pairs={{0,8},{8,0},{16,24},{24,16},{1,9},{9,1},{17,25},{25,17},{2,10},{10... | collective-permute-start | bytes 393224 | tf_op jit(solution)/shard_map/ppermute | solution.py:305
  86.5 5.6 %collective-permute-start.21 = (f32[128,256]{1,0:T(8,128)S(1)}, f32[128,256]{1,0:T(8,128)S(1)}, u32[]{:S(2)}, u32[]{:S(2)}) collective-permute-start(f32[128,256]{1,0:T(8,128)S(1)} %add.107), channel_id=1, source_target_pairs={{0,2},{2,0},{4,6},{6,4},{1,3},{3,1},{5,7},{7,5},{8,10},{10,8},{12,... | collective-permute-start | bytes 393224 | tf_op jit(solution)/shard_map/ppermute | solution.py:305
  89.7 17.0 %collective-permute-start.27 = (f32[256,384]{1,0:T(8,128)S(1)}, f32[256,384]{1,0:T(8,128)S(1)}, u32[]{:S(2)}, u32[]{:S(2)}) collective-permute-start(f32[256,384]{1,0:T(8,128)S(1)} %get-tuple-element.103), channel_id=1, source_target_pairs={{0,1},{1,0},{2,3},{3,2},{4,5},{5,4},{6,7},{7,6},{8,9},{9,8},{10,11... | collective-permute-start | bytes 1179656 | tf_op jit(solution)/shard_map/ppermute | solution.py:305
  92.1 6.6 %collective-permute-start.22 = (f32[128,256]{1,0:T(8,128)S(1)}, f32[128,256]{1,0:T(8,128)S(1)}, u32[]{:S(2)}, u32[]{:S(2)}) collective-permute-start(f32[128,256]{1,0:T(8,128)S(1)} %add.108), channel_id=1, source_target_pairs={{0,16},{8,24},{16,0},{24,8},{1,17},{9,25},{17,1},{25,9},{2,18},{10... | collective-permute-start | bytes 393224 | tf_op jit(solution)/shard_map/ppermute | solution.py:305
  95.0 12.4 %collective-permute-start.28 = (f32[256,384]{1,0:T(8,128)S(1)}, f32[256,384]{1,0:T(8,128)S(1)}, u32[]{:S(2)}, u32[]{:S(2)}) collective-permute-start(f32[256,384]{1,0:T(8,128)S(1)} %add.109), channel_id=1, source_target_pairs={{0,2},{2,0},{4,6},{6,4},{1,3},{3,1},{5,7},{7,5},{8,10},{10,8},{12,... | collective-permute-start | bytes 1179656 | tf_op jit(solution)/shard_map/ppermute | solution.py:305
  98.4 12.6 %collective-permute-start.26 = (f32[256,384]{1,0:T(8,128)S(1)}, f32[256,384]{1,0:T(8,128)S(1)}, u32[]{:S(2)}, u32[]{:S(2)}) collective-permute-start(f32[256,384]{1,0:T(8,128)S(1)} %get-tuple-element.108), channel_id=1, source_target_pairs={{0,1},{1,0},{2,3},{3,2},{4,5},{5,4},{6,7},{7,6},{8,9},{9,8},{10,11... | collective-permute-start | bytes 1179656 | tf_op jit(solution)/shard_map/ppermute | solution.py:305
  98.8 7.8 %collective-permute-start.24 = (f32[128,256]{1,0:T(8,128)S(1)}, f32[128,256]{1,0:T(8,128)S(1)}, u32[]{:S(2)}, u32[]{:S(2)}) collective-permute-start(f32[128,256]{1,0:T(8,128)S(1)} %add.110), channel_id=1, source_target_pairs={{0,4},{2,6},{4,0},{6,2},{1,5},{3,7},{5,1},{7,3},{8,12},{10,14},{12... | collective-permute-start | bytes 393224 | tf_op jit(solution)/shard_map/ppermute | solution.py:305
  106.6 4.6 %collective-permute-start.25 = (f32[128,256]{1,0:T(8,128)S(1)}, f32[128,256]{1,0:T(8,128)S(1)}, u32[]{:S(2)}, u32[]{:S(2)}) collective-permute-start(f32[128,256]{1,0:T(8,128)S(1)} %add.111.near), channel_id=1, source_target_pairs={{0,8},{8,0},{16,24},{24,16},{1,9},{9,1},{17,25},{25,17},{2,10},{10... | collective-permute-start | bytes 393224 | tf_op jit(solution)/shard_map/ppermute | solution.py:305
  107.4 20.3 %collective-permute-start.29 = (f32[256,384]{1,0:T(8,128)S(1)}, f32[256,384]{1,0:T(8,128)S(1)}, u32[]{:S(2)}, u32[]{:S(2)}) collective-permute-start(f32[256,384]{1,0:T(8,128)S(1)} %add_add_fusion), channel_id=1, source_target_pairs={{0,4},{2,6},{4,0},{6,2},{1,5},{3,7},{5,1},{7,3},{8,12},{10,14},{12... | collective-permute-start | bytes 1179656 | tf_op jit(solution)/shard_map/ppermute | solution.py:305
  111.0 17.4 %collective-permute-start.30 = (f32[256,384]{1,0:T(8,128)S(1)}, f32[256,384]{1,0:T(8,128)S(1)}, u32[]{:S(2)}, u32[]{:S(2)}) collective-permute-start(f32[256,384]{1,0:T(8,128)S(1)} %add.112), channel_id=1, source_target_pairs={{0,2},{2,0},{4,6},{6,4},{1,3},{3,1},{5,7},{7,5},{8,10},{10,8},{12,... | collective-permute-start | bytes 1179656 | tf_op jit(solution)/shard_map/ppermute | solution.py:305
  112.7 15.8 %collective-permute-start.31 = (f32[256,384]{1,0:T(8,128)S(1)}, f32[256,384]{1,0:T(8,128)S(1)}, u32[]{:S(2)}, u32[]{:S(2)}) collective-permute-start(f32[256,384]{1,0:T(8,128)S(1)} %get-tuple-element.122), channel_id=1, source_target_pairs={{0,1},{1,0},{2,3},{3,2},{4,5},{5,4},{6,7},{7,6},{8,9},{9,8},{10,11... | collective-permute-start | bytes 1179656 | tf_op jit(solution)/shard_map/ppermute | solution.py:305
  (9 other events, 57.7 us)

commit v4 on v3

--- a/solution.py
+++ b/solution.py
@@ -179,10 +179,18 @@
     return arrived
 
 
-def begin_kernel(scalars, source, coulomb, bare, scaled):
-    turned = source[...].T
+def begin_kernel(source, coulomb, bare, scaled, source_here, coulomb_here, sems):
+    copies = [
+        pltpu.make_async_copy(source, source_here, sems.at[0]),
+        pltpu.make_async_copy(coulomb, coulomb_here, sems.at[1]),
+    ]
+    for copy in copies:
+        copy.start()
+    for copy in copies:
+        copy.wait()
+    turned = source_here[...].T
     bare[...] = turned
-    scaled[...] = turned * coulomb[...][None, :]
+    scaled[...] = turned * coulomb_here[...][None, :]
 
 
 def first_kernel(width, jobs, scalars, near, far, chi, out, *rest):
@@ -319,9 +327,20 @@
     scalars = jnp.stack([grp // 2, grp % 2, lax.axis_index("col"), lax.axis_index("dev")]).astype(jnp.int32)
     scale = coulomb[None, :]
 
-    bare, scaled = small(
-        begin_kernel, "begin", scalars, [shaped(width, half)] * 2, [], (0, 12 * half * width), source, coulomb
-    )
+    bare, scaled = pl.pallas_call(
+        begin_kernel,
+        name="begin",
+        in_specs=[pl.BlockSpec(memory_space=pl.ANY)] * 2,
+        out_specs=[pl.BlockSpec(memory_space=pltpu.VMEM)] * 2,
+        out_shape=[shaped(width, half)] * 2,
+        scratch_shapes=[
+            pltpu.VMEM((half, width), jnp.float32),
+            pltpu.VMEM((half,), jnp.float32),
+            pltpu.SemaphoreType.DMA((2,)),
+        ],
+        cost_estimate=pl.CostEstimate(flops=0, bytes_accessed=12 * half * width, transcendentals=0),
+        compiler_params=pltpu.CompilerParams(vmem_limit_bytes=LIMIT * MIB),
+    )(source, coulomb)
 
     def products(blocks, rows):
         flops = 3 * 2 * 2 * blocks * rows * slab * slab

time: 130 us -> 130 us (level)
    pallas_call x16 -> x15, Pallas kernels: 51.7 us -> 51.1 us  [small(): pl.pallas_call(kernel, name=name, in_specs=in_specs, out_specs=[vmem] * l...]
where the time goes in v4:
time: 130 us
  Pallas kernels  51.4 us (40%)
  waiting for transfers between devices  43.5 us (33%)
  starting transfers between devices  30.8 us (24%)
  local copies, waits for them, and re-layouts  1.65 us (1%)
    pallas_call x15, Pallas kernels, small(): pl.pallas_call(kernel, name=name, in_specs=in_specs, out_specs=[vmem] * l...  51.1 us
    ppermute x32, waiting for transfers between devices, exchange(): return lax.ppermute(value, axis, [(i, i ^ flip) for i in range(size)])  43.5 us
    ppermute x32, starting transfers between devices, exchange(): return lax.ppermute(value, axis, [(i, i ^ flip) for i in range(size)])  30.8 us
  transfers between devices with their start and end apart: 32, of which 16 were waited for; matrix products, arithmetic and copies ran while one was open for 1% of the time, Pallas kernels for 34%

profile of v4, /device:TPU:0, one launch (start us, length us, event | category | flops | bytes accessed | tf_op | source)
XLA Modules:
  0.0 129.6 jit_solution(16707182273358813655)
XLA Ops:
  3.1 2.6 %collective-permute-start.2 = (f32[128,384]{1,0:T(8,128)S(1)}, f32[128,384]{1,0:T(8,128)S(1)}, u32[]{:S(2)}, u32[]{:S(2)}) collective-permute-start(f32[128,384]{1,0:T(8,128)S(1)} %get-tuple-element.64.near), channel_id=1, source_target_pairs={{0,16},{8,24},{16,0},{24,8},{1,17},{9,25},{17,1},{25,9},{2,18},{10... | collective-permute-start | bytes 589832 | tf_op jit(solution)/shard_map/ppermute | solution.py:313
  5.7 1.5 %collective-permute-start = (f32[128,384]{1,0:T(8,128)S(1)}, f32[128,384]{1,0:T(8,128)S(1)}, u32[]{:S(2)}, u32[]{:S(2)}) collective-permute-start(f32[128,384]{1,0:T(8,128)S(1)} %get-tuple-element.64.near), channel_id=1, source_target_pairs={{0,1},{1,0},{2,3},{3,2},{4,5},{5,4},{6,7},{7,6},{8,9},{9,8},{10,11... | collective-permute-start | bytes 589832 | tf_op jit(solution)/shard_map/ppermute | solution.py:313
  7.3 4.4 %first_near.1 = (f32[1,256,768]{2,1,0:T(8,128)S(1)}, f32[2,2,384,768]{3,2,1,0:T(8,128)S(1)}, f32[2,2,384,768]{3,2,1,0:T(8,128)S(1)}) custom-call(s32[4]{0:T(128)S(1)} %pad_add_fusion.scalars, f32[128,384]{1,0:T(8,128)S(1)} %get-tuple-element.64.near, f32[128,384]{1,0:T(8,128)S(1)} %collective-permute-done.1.far.near_far, f32[2,4,1,384,3072]{4,3,2,1,0:T(8,128)} %chi.7), custom_call_target="tpu_custom_call" | custom-call | flops 905969664 | bytes 5505024 | tf_op jit(solution)/shard_map/first_near/pallas_call | solution.py:118
  13.3 2.0 %far_slab_3.2 = (f32[256,384]{1,0:T(8,128)S(1)}, f32[256,384]{1,0:T(8,128)S(1)}) custom-call(s32[4]{0:T(128)S(1)} %pad_add_fusion.scalars, f32[128,384]{1,0:T(8,128)S(1)} %collective-permute-done.2.near.far, f32[128,384]{1,0:T(8,128)S(1)} %collective-permute-done.3.far.far_far, f32[1,256,768]{2,1,0:T(8,128)S(1)} %get-tuple-element.65.start, ...), custom_call_target="tpu_custom_call" | custom-call | flops 905969664 | bytes 5505024 | tf_op jit(solution)/shard_map/far_slab_3/pallas_call | solution.py:118
  15.3 1.2 collective-permute-start.7
  19.2 1.6 %collective-permute-start.5 = (f32[128,256]{1,0:T(8,128)S(1)}, f32[128,256]{1,0:T(8,128)S(1)}, u32[]{:S(2)}, u32[]{:S(2)}) collective-permute-start(f32[128,256]{1,0:T(8,128)S(1)} %add.91), channel_id=1, source_target_pairs={{0,2},{2,0},{4,6},{6,4},{1,3},{3,1},{5,7},{7,5},{8,10},{10,8},{12,... | collective-permute-start | bytes 393224 | tf_op jit(solution)/shard_map/ppermute | solution.py:313
  20.8 5.4 %both_slabs_2.1 = (f32[256,384]{1,0:T(8,128)S(1)}, f32[256,384]{1,0:T(8,128)S(1)}, f32[2,2,384,768]{3,2,1,0:T(8,128)S(1)}, f32[2,2,384,768]{3,2,1,0:T(8,128)S(1)}) custom-call(s32[4]{0:T(128)S(1)} %pad_add_fusion.scalars, f32[128,384]{1,0:T(8,128)S(1)} %get-tuple-element.64.near, f32[128,384]{1,0:T(8,128)S(1)} %collective-permute-done.1.far.near_far, ...), custom_call_target="tpu_custom_call" | custom-call | flops 1811939328 | bytes 11010048 | tf_op jit(solution)/shard_map/both_slabs_2/pallas_call | solution.py:118
  29.4 5.5 %both_slabs_1.1 = (f32[256,384]{1,0:T(8,128)S(1)}, f32[256,384]{1,0:T(8,128)S(1)}, f32[2,2,384,768]{3,2,1,0:T(8,128)S(1)}, f32[2,2,384,768]{3,2,1,0:T(8,128)S(1)}) custom-call(s32[4]{0:T(128)S(1)} %pad_add_fusion.scalars, f32[128,384]{1,0:T(8,128)S(1)} %get-tuple-element.64.near, f32[128,384]{1,0:T(8,128)S(1)} %collective-permute-done.1.far.near_far, ...), custom_call_target="tpu_custom_call" | custom-call | flops 1811939328 | bytes 11010048 | tf_op jit(solution)/shard_map/both_slabs_1/pallas_call | solution.py:118
  34.8 1.6 %collective-permute-start.10 = (f32[256,384]{1,0:T(8,128)S(1)}, f32[256,384]{1,0:T(8,128)S(1)}, u32[]{:S(2)}, u32[]{:S(2)}) collective-permute-start(f32[256,384]{1,0:T(8,128)S(1)} %get-tuple-element.78), channel_id=1, source_target_pairs={{0,1},{1,0},{2,3},{3,2},{4,5},{5,4},{6,7},{7,6},{8,9},{9,8},{10,11... | collective-permute-start | bytes 1179656 | tf_op jit(solution)/shard_map/ppermute | solution.py:313
  36.5 2.7 %collective-permute-start.8 = (f32[128,256]{1,0:T(8,128)S(1)}, f32[128,256]{1,0:T(8,128)S(1)}, u32[]{:S(2)}, u32[]{:S(2)}) collective-permute-start(f32[128,256]{1,0:T(8,128)S(1)} %add.94), channel_id=1, source_target_pairs={{0,4},{2,6},{4,0},{6,2},{1,5},{3,7},{5,1},{7,3},{8,12},{10,14},{12... | collective-permute-start | bytes 393224 | tf_op jit(solution)/shard_map/ppermute | solution.py:313
  39.1 5.3 %both_slabs_0.1 = (f32[256,384]{1,0:T(8,128)S(1)}, f32[256,384]{1,0:T(8,128)S(1)}, f32[2,2,384,768]{3,2,1,0:T(8,128)S(1)}, f32[2,2,384,768]{3,2,1,0:T(8,128)S(1)}) custom-call(s32[4]{0:T(128)S(1)} %pad_add_fusion.scalars, f32[128,384]{1,0:T(8,128)S(1)} %get-tuple-element.64.near, f32[128,384]{1,0:T(8,128)S(1)} %collective-permute-done.1.far.near_far, ...), custom_call_target="tpu_custom_call" | custom-call | flops 1811939328 | bytes 11010048 | tf_op jit(solution)/shard_map/both_slabs_0/pallas_call | solution.py:118
  45.7 3.0 %collective-permute-start.14 = (f32[256,384]{1,0:T(8,128)S(1)}, f32[256,384]{1,0:T(8,128)S(1)}, u32[]{:S(2)}, u32[]{:S(2)}) collective-permute-start(f32[256,384]{1,0:T(8,128)S(1)} %add.96), channel_id=1, source_target_pairs={{0,2},{2,0},{4,6},{6,4},{1,3},{3,1},{5,7},{7,5},{8,10},{10,8},{12,... | collective-permute-start | bytes 1179656 | tf_op jit(solution)/shard_map/ppermute | solution.py:313
  48.6 1.6 %spread.2 = (f32[256,384]{1,0:T(8,128)S(1)}, f32[256,384]{1,0:T(8,128)S(1)}) custom-call(s32[4]{0:T(128)S(1)} %pad_add_fusion.scalars, f32[128,256]{1,0:T(8,128)S(1)} %add.95.near, f32[128,256]{1,0:T(8,128)S(1)} %collective-permute-done.9.far, f32[1,256]{1,0:T(1,128)S(1)} %bitcast.5, f32[768,256]{1,0:T(8,128)S(1)} %copy-done, f32[768,256]{1,0:T(8,128)S(1)} %copy-done.1, ...), custom_call_target="tpu_custom_call" | custom-call | flops 603979776 | bytes 1572864 | tf_op jit(solution)/shard_map/spread/pallas_call | solution.py:118
  50.8 15.0 %collective-permute-done.13 = f32[256,384]{1,0:T(8,128)S(1)} collective-permute-done((f32[256,384]{1,0:T(8,128)S(1)}, f32[256,384]{1,0:T(8,128)S(1)}, u32[]{:S(2)}, u32[]{:S(2)}) %collective-permute-start.13) | collective-permute-done | bytes 393248 | tf_op jit(solution)/shard_map/ppermute | solution.py:313
  67.9 6.8 %near_half.1.start = f32[3,256,768]{2,1,0:T(8,128)S(1)} custom-call(s32[4]{0:T(128)S(1)} %pad_add_fusion.scalars, f32[256,384]{1,0:T(8,128)S(1)} %get-tuple-element.129.near, f32[256,384]{1,0:T(8,128)S(1)} %collective-permute-done.17.far.near_far, f32[2,2,384,768]{3,2,1,0:T(8,128)S(1)} %get-tuple-element.92.rest_0_, ...), custom_call_target="tpu_custom_call" | custom-call | flops 5435817984 | bytes 16515072 | tf_op jit(solution)/shard_map/near_half/pallas_call | solution.py:118
  74.7 3.0 %collective-permute-done.18.near.far = f32[256,384]{1,0:T(8,128)S(1)} collective-permute-done((f32[256,384]{1,0:T(8,128)S(1)}, f32[256,384]{1,0:T(8,128)S(1)}, u32[]{:S(2)}, u32[]{:S(2)}) %collective-permute-start.18) | collective-permute-done | bytes 393248 | tf_op jit(solution)/shard_map/ppermute | solution.py:313
  77.9 1.5 %collective-permute-done.19.far.far_far = f32[256,384]{1,0:T(8,128)S(1)} collective-permute-done((f32[256,384]{1,0:T(8,128)S(1)}, f32[256,384]{1,0:T(8,128)S(1)}, u32[]{:S(2)}, u32[]{:S(2)}) %collective-permute-start.19) | collective-permute-done | bytes 393248 | tf_op jit(solution)/shard_map/ppermute | solution.py:313
  79.4 3.1 %far_slab_3.3 = (f32[256,384]{1,0:T(8,128)S(1)}, f32[256,384]{1,0:T(8,128)S(1)}) custom-call(s32[4]{0:T(128)S(1)} %pad_add_fusion.scalars, f32[256,384]{1,0:T(8,128)S(1)} %collective-permute-done.18.near.far, f32[256,384]{1,0:T(8,128)S(1)} %collective-permute-done.19.far.far_far, f32[3,256,768]{2,1,0:T(8,128)S(1)} %near_half.1.start, ...), custom_call_target="tpu_custom_call" | custom-call | flops 1811939328 | bytes 5505024 | tf_op jit(solution)/shard_map/far_slab_3/pallas_call | solution.py:118
  83.1 1.6 %project.3 = (f32[128,256]{1,0:T(8,128)S(1)}, f32[128,256]{1,0:T(8,128)S(1)}) custom-call(s32[4]{0:T(128)S(1)} %pad_add_fusion.scalars, f32[256,384]{1,0:T(8,128)S(1)} %get-tuple-element.129.near, f32[256,384]{1,0:T(8,128)S(1)} %collective-permute-done.16.far, f32[768,256]{1,0:T(8,128)S(1)} %copy-done, f32[768,256]{1,0:T(8,128)S(1)} %copy-done.1), custom_call_target="tpu_custom_call" | custom-call | flops 603979776 | bytes 1572864 | tf_op jit(solution)/shard_map/project/pallas_call | solution.py:118
  84.7 1.3 %collective-permute-done.20 = f32[128,256]{1,0:T(8,128)S(1)} collective-permute-done((f32[128,256]{1,0:T(8,128)S(1)}, f32[128,256]{1,0:T(8,128)S(1)}, u32[]{:S(2)}, u32[]{:S(2)}) %collective-permute-start.20) | collective-permute-done | bytes 131104 | tf_op jit(solution)/shard_map/ppermute | solution.py:313
  86.2 3.1 %far_slab_2.1 = (f32[256,384]{1,0:T(8,128)S(1)}, f32[256,384]{1,0:T(8,128)S(1)}) custom-call(s32[4]{0:T(128)S(1)} %pad_add_fusion.scalars, f32[256,384]{1,0:T(8,128)S(1)} %collective-permute-done.18.near.far, f32[256,384]{1,0:T(8,128)S(1)} %collective-permute-done.19.far.far_far, f32[3,256,768]{2,1,0:T(8,128)S(1)} %near_half.1.start, ...), custom_call_target="tpu_custom_call" | custom-call | flops 1811939328 | bytes 5505024 | tf_op jit(solution)/shard_map/far_slab_2/pallas_call | solution.py:118
  89.3 1.6 %collective-permute-start.27 = (f32[256,384]{1,0:T(8,128)S(1)}, f32[256,384]{1,0:T(8,128)S(1)}, u32[]{:S(2)}, u32[]{:S(2)}) collective-permute-start(f32[256,384]{1,0:T(8,128)S(1)} %get-tuple-element.103), channel_id=1, source_target_pairs={{0,1},{1,0},{2,3},{3,2},{4,5},{5,4},{6,7},{7,6},{8,9},{9,8},{10,11... | collective-permute-start | bytes 1179656 | tf_op jit(solution)/shard_map/ppermute | solution.py:313
  92.8 1.7 %collective-permute-done.23 = f32[256,384]{1,0:T(8,128)S(1)} collective-permute-done((f32[256,384]{1,0:T(8,128)S(1)}, f32[256,384]{1,0:T(8,128)S(1)}, u32[]{:S(2)}, u32[]{:S(2)}) %collective-permute-start.23) | collective-permute-done | bytes 393248 | tf_op jit(solution)/shard_map/ppermute | solution.py:313
  94.7 3.3 %far_slab_1.1 = (f32[256,384]{1,0:T(8,128)S(1)}, f32[256,384]{1,0:T(8,128)S(1)}) custom-call(s32[4]{0:T(128)S(1)} %pad_add_fusion.scalars, f32[256,384]{1,0:T(8,128)S(1)} %collective-permute-done.18.near.far, f32[256,384]{1,0:T(8,128)S(1)} %collective-permute-done.19.far.far_far, f32[3,256,768]{2,1,0:T(8,128)S(1)} %near_half.1.start, ...), custom_call_target="tpu_custom_call" | custom-call | flops 1811939328 | bytes 5505024 | tf_op jit(solution)/shard_map/far_slab_1/pallas_call | solution.py:118
  98.4 2.9 %collective-permute-start.24 = (f32[128,256]{1,0:T(8,128)S(1)}, f32[128,256]{1,0:T(8,128)S(1)}, u32[]{:S(2)}, u32[]{:S(2)}) collective-permute-start(f32[128,256]{1,0:T(8,128)S(1)} %add.110), channel_id=1, source_target_pairs={{0,4},{2,6},{4,0},{6,2},{1,5},{3,7},{5,1},{7,3},{8,12},{10,14},{12... | collective-permute-start | bytes 393224 | tf_op jit(solution)/shard_map/ppermute | solution.py:313
  101.2 5.0 %held_slab_0.1 = (f32[256,384]{1,0:T(8,128)S(1)}, f32[256,384]{1,0:T(8,128)S(1)}) custom-call(s32[4]{0:T(128)S(1)} %pad_add_fusion.scalars, f32[256,384]{1,0:T(8,128)S(1)} %get-tuple-element.129.near, f32[256,384]{1,0:T(8,128)S(1)} %collective-permute-done.17.far.near_far, f32[256,384]{1,0:T(8,128)S(1)} %collective-permute-done.18.near.far, ...), custom_call_target="tpu_custom_call" | custom-call | flops 3623878656 | bytes 11010048 | tf_op jit(solution)/shard_map/held_slab_0/pallas_call | solution.py:118
  107.1 1.4 %collective-permute-start.29 = (f32[256,384]{1,0:T(8,128)S(1)}, f32[256,384]{1,0:T(8,128)S(1)}, u32[]{:S(2)}, u32[]{:S(2)}) collective-permute-start(f32[256,384]{1,0:T(8,128)S(1)} %add_add_fusion), channel_id=1, source_target_pairs={{0,4},{2,6},{4,0},{6,2},{1,5},{3,7},{5,1},{7,3},{8,12},{10,14},{12... | collective-permute-start | bytes 1179656 | tf_op jit(solution)/shard_map/ppermute | solution.py:313
  108.4 2.2 %collective-permute-done.26 = f32[256,384]{1,0:T(8,128)S(1)} collective-permute-done((f32[256,384]{1,0:T(8,128)S(1)}, f32[256,384]{1,0:T(8,128)S(1)}, u32[]{:S(2)}, u32[]{:S(2)}) %collective-permute-start.26) | collective-permute-done | bytes 393248 | tf_op jit(solution)/shard_map/ppermute | solution.py:313
  110.8 1.6 %spread.3 = (f32[256,384]{1,0:T(8,128)S(1)}, f32[256,384]{1,0:T(8,128)S(1)}) custom-call(s32[4]{0:T(128)S(1)} %pad_add_fusion.scalars, f32[128,256]{1,0:T(8,128)S(1)} %add.111.near, f32[128,256]{1,0:T(8,128)S(1)} %collective-permute-done.25.far, f32[1,256]{1,0:T(1,128)S(1)} %bitcast.6, f32[768,256]{1,0:T(8,128)S(1)} %copy-done, f32[768,256]{1,0:T(8,128)S(1)} %copy-done.1, ...), custom_call_target="tpu_custom_call" | custom-call | flops 603979776 | bytes 1572864 | tf_op jit(solution)/shard_map/spread/pallas_call | solution.py:118
  112.3 1.6 %collective-permute-start.31 = (f32[256,384]{1,0:T(8,128)S(1)}, f32[256,384]{1,0:T(8,128)S(1)}, u32[]{:S(2)}, u32[]{:S(2)}) collective-permute-start(f32[256,384]{1,0:T(8,128)S(1)} %get-tuple-element.122), channel_id=1, source_target_pairs={{0,1},{1,0},{2,3},{3,2},{4,5},{5,4},{6,7},{7,6},{8,9},{9,8},{10,11... | collective-permute-start | bytes 1179656 | tf_op jit(solution)/shard_map/ppermute | solution.py:313
  113.9 13.5 %collective-permute-done.29 = f32[256,384]{1,0:T(8,128)S(1)} collective-permute-done((f32[256,384]{1,0:T(8,128)S(1)}, f32[256,384]{1,0:T(8,128)S(1)}, u32[]{:S(2)}, u32[]{:S(2)}) %collective-permute-start.29) | collective-permute-done | bytes 393248 | tf_op jit(solution)/shard_map/ppermute | solution.py:313
  128.1 1.4 %end.1 = (f32[384,128]{1,0:T(8,128)}, f32[384,128]{1,0:T(8,128)}) custom-call(s32[4]{0:T(128)S(1)} %pad_add_fusion.scalars, f32[256,384]{1,0:T(8,128)S(1)} %add.116.own, f32[256,384]{1,0:T(8,128)S(1)} %collective-permute-done.31.by_dev, f32[256,384]{1,0:T(8,128)S(1)} %get-tuple-element.128.iterate, f32[128,384]{1,0:T(8,128)S(1)} %get-tuple-element.63.bare, ...), custom_call_target="tpu_custom_call" | custom-call | bytes 3145728 | tf_op jit(solution)/shard_map/end/pallas_call | solution.py:118
  (91 shorter events, 18.7 us)
Async XLA Ops:
  2.6 4.7 %collective-permute-start.1 = (f32[128,384]{1,0:T(8,128)S(1)}, f32[128,384]{1,0:T(8,128)S(1)}, u32[]{:S(2)}, u32[]{:S(2)}) collective-permute-start(f32[128,384]{1,0:T(8,128)S(1)} %get-tuple-element.64.near), channel_id=1, source_target_pairs={{0,8},{8,0},{16,24},{24,16},{1,9},{9,1},{17,25},{25,17},{2,10},{10... | collective-permute-start | bytes 589832 | tf_op jit(solution)/shard_map/ppermute | solution.py:313
  3.1 8.6 %collective-permute-start.2 = (f32[128,384]{1,0:T(8,128)S(1)}, f32[128,384]{1,0:T(8,128)S(1)}, u32[]{:S(2)}, u32[]{:S(2)}) collective-permute-start(f32[128,384]{1,0:T(8,128)S(1)} %get-tuple-element.64.near), channel_id=1, source_target_pairs={{0,16},{8,24},{16,0},{24,8},{1,17},{9,25},{17,1},{25,9},{2,18},{10... | collective-permute-start | bytes 589832 | tf_op jit(solution)/shard_map/ppermute | solution.py:313
  5.7 7.0 %collective-permute-start = (f32[128,384]{1,0:T(8,128)S(1)}, f32[128,384]{1,0:T(8,128)S(1)}, u32[]{:S(2)}, u32[]{:S(2)}) collective-permute-start(f32[128,384]{1,0:T(8,128)S(1)} %get-tuple-element.64.near), channel_id=1, source_target_pairs={{0,1},{1,0},{2,3},{3,2},{4,5},{5,4},{6,7},{7,6},{8,9},{9,8},{10,11... | collective-permute-start | bytes 589832 | tf_op jit(solution)/shard_map/ppermute | solution.py:313
  11.8 1.5 %collective-permute-start.3 = (f32[128,384]{1,0:T(8,128)S(1)}, f32[128,384]{1,0:T(8,128)S(1)}, u32[]{:S(2)}, u32[]{:S(2)}) collective-permute-start(f32[128,384]{1,0:T(8,128)S(1)} %collective-permute-done.2.near.far), channel_id=1, source_target_pairs={{0,8},{8,0},{16,24},{24,16},{1,9},{9,1},{17,25},{25,17},{2,10},{10... | collective-permute-start | bytes 589832 | tf_op jit(solution)/shard_map/ppermute | solution.py:313
  15.3 11.9 %collective-permute-start.7 = (f32[256,384]{1,0:T(8,128)S(1)}, f32[256,384]{1,0:T(8,128)S(1)}, u32[]{:S(2)}, u32[]{:S(2)}) collective-permute-start(f32[256,384]{1,0:T(8,128)S(1)} %get-tuple-element.69), channel_id=1, source_target_pairs={{0,1},{1,0},{2,3},{3,2},{4,5},{5,4},{6,7},{7,6},{8,9},{9,8},{10,11... | collective-permute-start | bytes 1179656 | tf_op jit(solution)/shard_map/ppermute | solution.py:313
  17.7 1.4 %collective-permute-start.4 = (f32[128,256]{1,0:T(8,128)S(1)}, f32[128,256]{1,0:T(8,128)S(1)}, u32[]{:S(2)}, u32[]{:S(2)}) collective-permute-start(f32[128,256]{1,0:T(8,128)S(1)} %get-tuple-element.72), channel_id=1, source_target_pairs={{0,8},{8,0},{16,24},{24,16},{1,9},{9,1},{17,25},{25,17},{2,10},{10... | collective-permute-start | bytes 393224 | tf_op jit(solution)/shard_map/ppermute | solution.py:313
  19.2 8.0 %collective-permute-start.5 = (f32[128,256]{1,0:T(8,128)S(1)}, f32[128,256]{1,0:T(8,128)S(1)}, u32[]{:S(2)}, u32[]{:S(2)}) collective-permute-start(f32[128,256]{1,0:T(8,128)S(1)} %add.91), channel_id=1, source_target_pairs={{0,2},{2,0},{4,6},{6,4},{1,3},{3,1},{5,7},{7,5},{8,10},{10,8},{12,... | collective-permute-start | bytes 393224 | tf_op jit(solution)/shard_map/ppermute | solution.py:313
  26.2 18.5 %collective-permute-start.11 = (f32[256,384]{1,0:T(8,128)S(1)}, f32[256,384]{1,0:T(8,128)S(1)}, u32[]{:S(2)}, u32[]{:S(2)}) collective-permute-start(f32[256,384]{1,0:T(8,128)S(1)} %get-tuple-element.74), channel_id=1, source_target_pairs={{0,1},{1,0},{2,3},{3,2},{4,5},{5,4},{6,7},{7,6},{8,9},{9,8},{10,11... | collective-permute-start | bytes 1179656 | tf_op jit(solution)/shard_map/ppermute | solution.py:313
  27.2 17.5 %collective-permute-start.12 = (f32[256,384]{1,0:T(8,128)S(1)}, f32[256,384]{1,0:T(8,128)S(1)}, u32[]{:S(2)}, u32[]{:S(2)}) collective-permute-start(f32[256,384]{1,0:T(8,128)S(1)} %add.93), channel_id=1, source_target_pairs={{0,2},{2,0},{4,6},{6,4},{1,3},{3,1},{5,7},{7,5},{8,10},{10,8},{12,... | collective-permute-start | bytes 1179656 | tf_op jit(solution)/shard_map/ppermute | solution.py:313
  28.2 8.2 %collective-permute-start.6 = (f32[128,256]{1,0:T(8,128)S(1)}, f32[128,256]{1,0:T(8,128)S(1)}, u32[]{:S(2)}, u32[]{:S(2)}) collective-permute-start(f32[128,256]{1,0:T(8,128)S(1)} %add.92), channel_id=1, source_target_pairs={{0,16},{8,24},{16,0},{24,8},{1,17},{9,25},{17,1},{25,9},{2,18},{10... | collective-permute-start | bytes 393224 | tf_op jit(solution)/shard_map/ppermute | solution.py:313
  34.8 10.8 %collective-permute-start.10 = (f32[256,384]{1,0:T(8,128)S(1)}, f32[256,384]{1,0:T(8,128)S(1)}, u32[]{:S(2)}, u32[]{:S(2)}) collective-permute-start(f32[256,384]{1,0:T(8,128)S(1)} %get-tuple-element.78), channel_id=1, source_target_pairs={{0,1},{1,0},{2,3},{3,2},{4,5},{5,4},{6,7},{7,6},{8,9},{9,8},{10,11... | collective-permute-start | bytes 1179656 | tf_op jit(solution)/shard_map/ppermute | solution.py:313
  36.5 8.0 %collective-permute-start.8 = (f32[128,256]{1,0:T(8,128)S(1)}, f32[128,256]{1,0:T(8,128)S(1)}, u32[]{:S(2)}, u32[]{:S(2)}) collective-permute-start(f32[128,256]{1,0:T(8,128)S(1)} %add.94), channel_id=1, source_target_pairs={{0,4},{2,6},{4,0},{6,2},{1,5},{3,7},{5,1},{7,3},{8,12},{10,14},{12... | collective-permute-start | bytes 393224 | tf_op jit(solution)/shard_map/ppermute | solution.py:313
  44.4 4.2 %collective-permute-start.9 = (f32[128,256]{1,0:T(8,128)S(1)}, f32[128,256]{1,0:T(8,128)S(1)}, u32[]{:S(2)}, u32[]{:S(2)}) collective-permute-start(f32[128,256]{1,0:T(8,128)S(1)} %add.95.near), channel_id=1, source_target_pairs={{0,8},{8,0},{16,24},{24,16},{1,9},{9,1},{17,25},{25,17},{2,10},{10... | collective-permute-start | bytes 393224 | tf_op jit(solution)/shard_map/ppermute | solution.py:313
  44.8 21.0 %collective-permute-start.13 = (f32[256,384]{1,0:T(8,128)S(1)}, f32[256,384]{1,0:T(8,128)S(1)}, u32[]{:S(2)}, u32[]{:S(2)}) collective-permute-start(f32[256,384]{1,0:T(8,128)S(1)} %add_add_fusion.1), channel_id=1, source_target_pairs={{0,4},{2,6},{4,0},{6,2},{1,5},{3,7},{5,1},{7,3},{8,12},{10,14},{12... | collective-permute-start | bytes 1179656 | tf_op jit(solution)/shard_map/ppermute | solution.py:313
  45.7 20.2 %collective-permute-start.14 = (f32[256,384]{1,0:T(8,128)S(1)}, f32[256,384]{1,0:T(8,128)S(1)}, u32[]{:S(2)}, u32[]{:S(2)}) collective-permute-start(f32[256,384]{1,0:T(8,128)S(1)} %add.96), channel_id=1, source_target_pairs={{0,2},{2,0},{4,6},{6,4},{1,3},{3,1},{5,7},{7,5},{8,10},{10,8},{12,... | collective-permute-start | bytes 1179656 | tf_op jit(solution)/shard_map/ppermute | solution.py:313
  50.2 15.7 %collective-permute-start.15 = (f32[256,384]{1,0:T(8,128)S(1)}, f32[256,384]{1,0:T(8,128)S(1)}, u32[]{:S(2)}, u32[]{:S(2)}) collective-permute-start(f32[256,384]{1,0:T(8,128)S(1)} %get-tuple-element.90), channel_id=1, source_target_pairs={{0,1},{1,0},{2,3},{3,2},{4,5},{5,4},{6,7},{7,6},{8,9},{9,8},{10,11... | collective-permute-start | bytes 1179656 | tf_op jit(solution)/shard_map/ppermute | solution.py:313
  66.1 1.8 %collective-permute-start.17 = (f32[256,384]{1,0:T(8,128)S(1)}, f32[256,384]{1,0:T(8,128)S(1)}, u32[]{:S(2)}, u32[]{:S(2)}) collective-permute-start(f32[256,384]{1,0:T(8,128)S(1)} %get-tuple-element.129.near), channel_id=1, source_target_pairs={{0,8},{8,0},{16,24},{24,16},{1,9},{9,1},{17,25},{25,17},{2,10},{10... | collective-permute-start | bytes 1179656 | tf_op jit(solution)/shard_map/ppermute | solution.py:313
  66.2 11.5 %collective-permute-start.18 = (f32[256,384]{1,0:T(8,128)S(1)}, f32[256,384]{1,0:T(8,128)S(1)}, u32[]{:S(2)}, u32[]{:S(2)}) collective-permute-start(f32[256,384]{1,0:T(8,128)S(1)} %get-tuple-element.129.near), channel_id=1, source_target_pairs={{0,16},{8,24},{16,0},{24,8},{1,17},{9,25},{17,1},{25,9},{2,18},{10... | collective-permute-start | bytes 1179656 | tf_op jit(solution)/shard_map/ppermute | solution.py:313
  66.7 11.2 %collective-permute-start.16 = (f32[256,384]{1,0:T(8,128)S(1)}, f32[256,384]{1,0:T(8,128)S(1)}, u32[]{:S(2)}, u32[]{:S(2)}) collective-permute-start(f32[256,384]{1,0:T(8,128)S(1)} %get-tuple-element.129.near), channel_id=1, source_target_pairs={{0,1},{1,0},{2,3},{3,2},{4,5},{5,4},{6,7},{7,6},{8,9},{9,8},{10,11... | collective-permute-start | bytes 1179656 | tf_op jit(solution)/shard_map/ppermute | solution.py:313
  77.7 1.7 %collective-permute-start.19 = (f32[256,384]{1,0:T(8,128)S(1)}, f32[256,384]{1,0:T(8,128)S(1)}, u32[]{:S(2)}, u32[]{:S(2)}) collective-permute-start(f32[256,384]{1,0:T(8,128)S(1)} %collective-permute-done.18.near.far), channel_id=1, source_target_pairs={{0,8},{8,0},{16,24},{24,16},{1,9},{9,1},{17,25},{25,17},{2,10},{10... | collective-permute-start | bytes 1179656 | tf_op jit(solution)/shard_map/ppermute | solution.py:313
  82.5 12.0 %collective-permute-start.23 = (f32[256,384]{1,0:T(8,128)S(1)}, f32[256,384]{1,0:T(8,128)S(1)}, u32[]{:S(2)}, u32[]{:S(2)}) collective-permute-start(f32[256,384]{1,0:T(8,128)S(1)} %get-tuple-element.97), channel_id=1, source_target_pairs={{0,1},{1,0},{2,3},{3,2},{4,5},{5,4},{6,7},{7,6},{8,9},{9,8},{10,11... | collective-permute-start | bytes 1179656 | tf_op jit(solution)/shard_map/ppermute | solution.py:313
  84.7 1.4 %collective-permute-start.20 = (f32[128,256]{1,0:T(8,128)S(1)}, f32[128,256]{1,0:T(8,128)S(1)}, u32[]{:S(2)}, u32[]{:S(2)}) collective-permute-start(f32[128,256]{1,0:T(8,128)S(1)} %get-tuple-element.100), channel_id=1, source_target_pairs={{0,8},{8,0},{16,24},{24,16},{1,9},{9,1},{17,25},{25,17},{2,10},{10... | collective-permute-start | bytes 393224 | tf_op jit(solution)/shard_map/ppermute | solution.py:313
  86.1 5.6 %collective-permute-start.21 = (f32[128,256]{1,0:T(8,128)S(1)}, f32[128,256]{1,0:T(8,128)S(1)}, u32[]{:S(2)}, u32[]{:S(2)}) collective-permute-start(f32[128,256]{1,0:T(8,128)S(1)} %add.107), channel_id=1, source_target_pairs={{0,2},{2,0},{4,6},{6,4},{1,3},{3,1},{5,7},{7,5},{8,10},{10,8},{12,... | collective-permute-start | bytes 393224 | tf_op jit(solution)/shard_map/ppermute | solution.py:313
  89.3 17.0 %collective-permute-start.27 = (f32[256,384]{1,0:T(8,128)S(1)}, f32[256,384]{1,0:T(8,128)S(1)}, u32[]{:S(2)}, u32[]{:S(2)}) collective-permute-start(f32[256,384]{1,0:T(8,128)S(1)} %get-tuple-element.103), channel_id=1, source_target_pairs={{0,1},{1,0},{2,3},{3,2},{4,5},{5,4},{6,7},{7,6},{8,9},{9,8},{10,11... | collective-permute-start | bytes 1179656 | tf_op jit(solution)/shard_map/ppermute | solution.py:313
  91.7 6.6 %collective-permute-start.22 = (f32[128,256]{1,0:T(8,128)S(1)}, f32[128,256]{1,0:T(8,128)S(1)}, u32[]{:S(2)}, u32[]{:S(2)}) collective-permute-start(f32[128,256]{1,0:T(8,128)S(1)} %add.108), channel_id=1, source_target_pairs={{0,16},{8,24},{16,0},{24,8},{1,17},{9,25},{17,1},{25,9},{2,18},{10... | collective-permute-start | bytes 393224 | tf_op jit(solution)/shard_map/ppermute | solution.py:313
  94.6 12.4 %collective-permute-start.28 = (f32[256,384]{1,0:T(8,128)S(1)}, f32[256,384]{1,0:T(8,128)S(1)}, u32[]{:S(2)}, u32[]{:S(2)}) collective-permute-start(f32[256,384]{1,0:T(8,128)S(1)} %add.109), channel_id=1, source_target_pairs={{0,2},{2,0},{4,6},{6,4},{1,3},{3,1},{5,7},{7,5},{8,10},{10,8},{12,... | collective-permute-start | bytes 1179656 | tf_op jit(solution)/shard_map/ppermute | solution.py:313
  98.0 12.6 %collective-permute-start.26 = (f32[256,384]{1,0:T(8,128)S(1)}, f32[256,384]{1,0:T(8,128)S(1)}, u32[]{:S(2)}, u32[]{:S(2)}) collective-permute-start(f32[256,384]{1,0:T(8,128)S(1)} %get-tuple-element.108), channel_id=1, source_target_pairs={{0,1},{1,0},{2,3},{3,2},{4,5},{5,4},{6,7},{7,6},{8,9},{9,8},{10,11... | collective-permute-start | bytes 1179656 | tf_op jit(solution)/shard_map/ppermute | solution.py:313
  98.4 7.8 %collective-permute-start.24 = (f32[128,256]{1,0:T(8,128)S(1)}, f32[128,256]{1,0:T(8,128)S(1)}, u32[]{:S(2)}, u32[]{:S(2)}) collective-permute-start(f32[128,256]{1,0:T(8,128)S(1)} %add.110), channel_id=1, source_target_pairs={{0,4},{2,6},{4,0},{6,2},{1,5},{3,7},{5,1},{7,3},{8,12},{10,14},{12... | collective-permute-start | bytes 393224 | tf_op jit(solution)/shard_map/ppermute | solution.py:313
  106.2 4.5 %collective-permute-start.25 = (f32[128,256]{1,0:T(8,128)S(1)}, f32[128,256]{1,0:T(8,128)S(1)}, u32[]{:S(2)}, u32[]{:S(2)}) collective-permute-start(f32[128,256]{1,0:T(8,128)S(1)} %add.111.near), channel_id=1, source_target_pairs={{0,8},{8,0},{16,24},{24,16},{1,9},{9,1},{17,25},{25,17},{2,10},{10... | collective-permute-start | bytes 393224 | tf_op jit(solution)/shard_map/ppermute | solution.py:313
  107.1 20.3 %collective-permute-start.29 = (f32[256,384]{1,0:T(8,128)S(1)}, f32[256,384]{1,0:T(8,128)S(1)}, u32[]{:S(2)}, u32[]{:S(2)}) collective-permute-start(f32[256,384]{1,0:T(8,128)S(1)} %add_add_fusion), channel_id=1, source_target_pairs={{0,4},{2,6},{4,0},{6,2},{1,5},{3,7},{5,1},{7,3},{8,12},{10,14},{12... | collective-permute-start | bytes 1179656 | tf_op jit(solution)/shard_map/ppermute | solution.py:313
  110.7 17.4 %collective-permute-start.30 = (f32[256,384]{1,0:T(8,128)S(1)}, f32[256,384]{1,0:T(8,128)S(1)}, u32[]{:S(2)}, u32[]{:S(2)}) collective-permute-start(f32[256,384]{1,0:T(8,128)S(1)} %add.112), channel_id=1, source_target_pairs={{0,2},{2,0},{4,6},{6,4},{1,3},{3,1},{5,7},{7,5},{8,10},{10,8},{12,... | collective-permute-start | bytes 1179656 | tf_op jit(solution)/shard_map/ppermute | solution.py:313
  112.3 15.8 %collective-permute-start.31 = (f32[256,384]{1,0:T(8,128)S(1)}, f32[256,384]{1,0:T(8,128)S(1)}, u32[]{:S(2)}, u32[]{:S(2)}) collective-permute-start(f32[256,384]{1,0:T(8,128)S(1)} %get-tuple-element.122), channel_id=1, source_target_pairs={{0,1},{1,0},{2,3},{3,2},{4,5},{5,4},{6,7},{7,6},{8,9},{9,8},{10,11... | collective-permute-start | bytes 1179656 | tf_op jit(solution)/shard_map/ppermute | solution.py:313
  (9 other events, 57.3 us)

commit v5 on v4

--- a/solution.py
+++ b/solution.py
@@ -406,14 +406,21 @@
                 return both_slab(j, *earlier)
             return (far_slab if last - j < AHEAD else held_slab)(j, *earlier)
 
-        send3, keep3 = far_slab(3, start, from_dev)
+        def project(*earlier):
+            return small(
+                functools.partial(project_kernel, width), "project", scalars, [shaped(width, pairs)] * 2,
+                [pltpu.VMEM((panel_rows, pairs), jnp.float32)],
+                (3 * 4 * rows * slab * pairs, 8 * slab * pairs),
+                scaled, after(from_dev, start, *earlier), rho_re, rho_im,
+            )
+
+        if fresh:
+            send3, keep3 = far_slab(3, start, from_dev)
+            keep, send = project(send3)
+        else:
+            keep, send = project()
+            send3, keep3 = far_slab(3, start, keep)
         got3 = exchange(send3, "dev", 1)
-        keep, send = small(
-            functools.partial(project_kernel, width), "project", scalars, [shaped(width, pairs)] * 2,
-            [pltpu.VMEM((panel_rows, pairs), jnp.float32)],
-            (3 * 4 * rows * slab * pairs, 8 * slab * pairs),
-            scaled, after(from_dev, start, send3), rho_re, rho_im,
-        )
         total = keep + exchange(send, "grp", 1)
         send2, keep2 = slab_of(2, send3, total)
         got2 = exchange(send2, "dev", 1)

time: 130 us -> 130 us (level)
  starting transfers between devices: 30.8 us -> 32.5 us
    ppermute x32, starting transfers between devices: 30.8 us -> 32.5 us  [exchange(): return lax.ppermute(value, axis, [(i, i ^ flip) for i in range(size)])]
  transfers between devices with their start and end apart: 32 -> 32, of which waited for: 16 -> 13; matrix products, arithmetic and copies ran while one was open for 1% -> 1% of each run, Pallas kernels for 34% -> 37%
where the time goes in v5:
time: 130 us
  Pallas kernels  51.4 us (40%)
  waiting for transfers between devices  42.3 us (33%)
  starting transfers between devices  32.5 us (25%)
  local copies, waits for them, and re-layouts  1.65 us (1%)
    pallas_call x15, Pallas kernels, small(): pl.pallas_call(kernel, name=name, in_specs=in_specs, out_specs=[vmem] * l...  51.1 us
    ppermute x32, waiting for transfers between devices, exchange(): return lax.ppermute(value, axis, [(i, i ^ flip) for i in range(size)])  42.3 us
    ppermute x32, starting transfers between devices, exchange(): return lax.ppermute(value, axis, [(i, i ^ flip) for i in range(size)])  32.5 us
  transfers between devices with their start and end apart: 32, of which 13 were waited for; matrix products, arithmetic and copies ran while one was open for 1% of the time, Pallas kernels for 37%

profile of v5, /device:TPU:0, one launch (start us, length us, event | category | flops | bytes accessed | tf_op | source)
XLA Modules:
  0.0 129.9 jit_solution(18024548192385132462)
XLA Ops:
  3.1 2.6 %collective-permute-start.2 = (f32[128,384]{1,0:T(8,128)S(1)}, f32[128,384]{1,0:T(8,128)S(1)}, u32[]{:S(2)}, u32[]{:S(2)}) collective-permute-start(f32[128,384]{1,0:T(8,128)S(1)} %get-tuple-element.64.near), channel_id=1, source_target_pairs={{0,16},{8,24},{16,0},{24,8},{1,17},{9,25},{17,1},{25,9},{2,18},{10... | collective-permute-start | bytes 589832 | tf_op jit(solution)/shard_map/ppermute | solution.py:313
  5.7 1.5 %collective-permute-start = (f32[128,384]{1,0:T(8,128)S(1)}, f32[128,384]{1,0:T(8,128)S(1)}, u32[]{:S(2)}, u32[]{:S(2)}) collective-permute-start(f32[128,384]{1,0:T(8,128)S(1)} %get-tuple-element.64.near), channel_id=1, source_target_pairs={{0,1},{1,0},{2,3},{3,2},{4,5},{5,4},{6,7},{7,6},{8,9},{9,8},{10,11... | collective-permute-start | bytes 589832 | tf_op jit(solution)/shard_map/ppermute | solution.py:313
  7.3 4.4 %first_near.1 = (f32[1,256,768]{2,1,0:T(8,128)S(1)}, f32[2,2,384,768]{3,2,1,0:T(8,128)S(1)}, f32[2,2,384,768]{3,2,1,0:T(8,128)S(1)}) custom-call(s32[4]{0:T(128)S(1)} %pad_add_fusion.scalars, f32[128,384]{1,0:T(8,128)S(1)} %get-tuple-element.64.near, f32[128,384]{1,0:T(8,128)S(1)} %collective-permute-done.1.far.near_far, f32[2,4,1,384,3072]{4,3,2,1,0:T(8,128)} %chi.7), custom_call_target="tpu_custom_call" | custom-call | flops 905969664 | bytes 5505024 | tf_op jit(solution)/shard_map/first_near/pallas_call | solution.py:118
  13.3 2.0 %far_slab_3.2 = (f32[256,384]{1,0:T(8,128)S(1)}, f32[256,384]{1,0:T(8,128)S(1)}) custom-call(s32[4]{0:T(128)S(1)} %pad_add_fusion.scalars, f32[128,384]{1,0:T(8,128)S(1)} %collective-permute-done.2.near.far, f32[128,384]{1,0:T(8,128)S(1)} %collective-permute-done.3.far.far_far, f32[1,256,768]{2,1,0:T(8,128)S(1)} %get-tuple-element.65.start, ...), custom_call_target="tpu_custom_call" | custom-call | flops 905969664 | bytes 5505024 | tf_op jit(solution)/shard_map/far_slab_3/pallas_call | solution.py:118
  15.3 1.2 collective-permute-start.7
  16.6 1.2 project.2
  19.2 1.6 %collective-permute-start.5 = (f32[128,256]{1,0:T(8,128)S(1)}, f32[128,256]{1,0:T(8,128)S(1)}, u32[]{:S(2)}, u32[]{:S(2)}) collective-permute-start(f32[128,256]{1,0:T(8,128)S(1)} %add.91), channel_id=1, source_target_pairs={{0,2},{2,0},{4,6},{6,4},{1,3},{3,1},{5,7},{7,5},{8,10},{10,8},{12,... | collective-permute-start | bytes 393224 | tf_op jit(solution)/shard_map/ppermute | solution.py:313
  20.8 5.4 %both_slabs_2.1 = (f32[256,384]{1,0:T(8,128)S(1)}, f32[256,384]{1,0:T(8,128)S(1)}, f32[2,2,384,768]{3,2,1,0:T(8,128)S(1)}, f32[2,2,384,768]{3,2,1,0:T(8,128)S(1)}) custom-call(s32[4]{0:T(128)S(1)} %pad_add_fusion.scalars, f32[128,384]{1,0:T(8,128)S(1)} %get-tuple-element.64.near, f32[128,384]{1,0:T(8,128)S(1)} %collective-permute-done.1.far.near_far, ...), custom_call_target="tpu_custom_call" | custom-call | flops 1811939328 | bytes 11010048 | tf_op jit(solution)/shard_map/both_slabs_2/pallas_call | solution.py:118
  28.2 1.1 collective-permute-start.6
  29.4 5.5 %both_slabs_1.1 = (f32[256,384]{1,0:T(8,128)S(1)}, f32[256,384]{1,0:T(8,128)S(1)}, f32[2,2,384,768]{3,2,1,0:T(8,128)S(1)}, f32[2,2,384,768]{3,2,1,0:T(8,128)S(1)}) custom-call(s32[4]{0:T(128)S(1)} %pad_add_fusion.scalars, f32[128,384]{1,0:T(8,128)S(1)} %get-tuple-element.64.near, f32[128,384]{1,0:T(8,128)S(1)} %collective-permute-done.1.far.near_far, ...), custom_call_target="tpu_custom_call" | custom-call | flops 1811939328 | bytes 11010048 | tf_op jit(solution)/shard_map/both_slabs_1/pallas_call | solution.py:118
  34.8 1.6 %collective-permute-start.10 = (f32[256,384]{1,0:T(8,128)S(1)}, f32[256,384]{1,0:T(8,128)S(1)}, u32[]{:S(2)}, u32[]{:S(2)}) collective-permute-start(f32[256,384]{1,0:T(8,128)S(1)} %get-tuple-element.78), channel_id=1, source_target_pairs={{0,1},{1,0},{2,3},{3,2},{4,5},{5,4},{6,7},{7,6},{8,9},{9,8},{10,11... | collective-permute-start | bytes 1179656 | tf_op jit(solution)/shard_map/ppermute | solution.py:313
  36.5 2.7 %collective-permute-start.8 = (f32[128,256]{1,0:T(8,128)S(1)}, f32[128,256]{1,0:T(8,128)S(1)}, u32[]{:S(2)}, u32[]{:S(2)}) collective-permute-start(f32[128,256]{1,0:T(8,128)S(1)} %add.94), channel_id=1, source_target_pairs={{0,4},{2,6},{4,0},{6,2},{1,5},{3,7},{5,1},{7,3},{8,12},{10,14},{12... | collective-permute-start | bytes 393224 | tf_op jit(solution)/shard_map/ppermute | solution.py:313
  39.1 5.3 %both_slabs_0.1 = (f32[256,384]{1,0:T(8,128)S(1)}, f32[256,384]{1,0:T(8,128)S(1)}, f32[2,2,384,768]{3,2,1,0:T(8,128)S(1)}, f32[2,2,384,768]{3,2,1,0:T(8,128)S(1)}) custom-call(s32[4]{0:T(128)S(1)} %pad_add_fusion.scalars, f32[128,384]{1,0:T(8,128)S(1)} %get-tuple-element.64.near, f32[128,384]{1,0:T(8,128)S(1)} %collective-permute-done.1.far.near_far, ...), custom_call_target="tpu_custom_call" | custom-call | flops 1811939328 | bytes 11010048 | tf_op jit(solution)/shard_map/both_slabs_0/pallas_call | solution.py:118
  45.7 3.0 %collective-permute-start.14 = (f32[256,384]{1,0:T(8,128)S(1)}, f32[256,384]{1,0:T(8,128)S(1)}, u32[]{:S(2)}, u32[]{:S(2)}) collective-permute-start(f32[256,384]{1,0:T(8,128)S(1)} %add.96), channel_id=1, source_target_pairs={{0,2},{2,0},{4,6},{6,4},{1,3},{3,1},{5,7},{7,5},{8,10},{10,8},{12,... | collective-permute-start | bytes 1179656 | tf_op jit(solution)/shard_map/ppermute | solution.py:313
  48.6 1.6 %spread.2 = (f32[256,384]{1,0:T(8,128)S(1)}, f32[256,384]{1,0:T(8,128)S(1)}) custom-call(s32[4]{0:T(128)S(1)} %pad_add_fusion.scalars, f32[128,256]{1,0:T(8,128)S(1)} %add.95.near, f32[128,256]{1,0:T(8,128)S(1)} %collective-permute-done.9.far, f32[1,256]{1,0:T(1,128)S(1)} %bitcast.5, f32[768,256]{1,0:T(8,128)S(1)} %copy-done, f32[768,256]{1,0:T(8,128)S(1)} %copy-done.1, ...), custom_call_target="tpu_custom_call" | custom-call | flops 603979776 | bytes 1572864 | tf_op jit(solution)/shard_map/spread/pallas_call | solution.py:118
  50.8 15.0 %collective-permute-done.13 = f32[256,384]{1,0:T(8,128)S(1)} collective-permute-done((f32[256,384]{1,0:T(8,128)S(1)}, f32[256,384]{1,0:T(8,128)S(1)}, u32[]{:S(2)}, u32[]{:S(2)}) %collective-permute-start.13) | collective-permute-done | bytes 393248 | tf_op jit(solution)/shard_map/ppermute | solution.py:313
  67.9 6.8 %near_half.1.start = f32[3,256,768]{2,1,0:T(8,128)S(1)} custom-call(s32[4]{0:T(128)S(1)} %pad_add_fusion.scalars, f32[256,384]{1,0:T(8,128)S(1)} %get-tuple-element.129.near, f32[256,384]{1,0:T(8,128)S(1)} %collective-permute-done.17.far.near_far, f32[2,2,384,768]{3,2,1,0:T(8,128)S(1)} %get-tuple-element.92.rest_0_, ...), custom_call_target="tpu_custom_call" | custom-call | flops 5435817984 | bytes 16515072 | tf_op jit(solution)/shard_map/near_half/pallas_call | solution.py:118
  74.7 3.0 %collective-permute-done.21.near.far = f32[256,384]{1,0:T(8,128)S(1)} collective-permute-done((f32[256,384]{1,0:T(8,128)S(1)}, f32[256,384]{1,0:T(8,128)S(1)}, u32[]{:S(2)}, u32[]{:S(2)}) %collective-permute-start.21) | collective-permute-done | bytes 393248 | tf_op jit(solution)/shard_map/ppermute | solution.py:313
  77.9 1.6 %project.3 = (f32[128,256]{1,0:T(8,128)S(1)}, f32[128,256]{1,0:T(8,128)S(1)}) custom-call(s32[4]{0:T(128)S(1)} %pad_add_fusion.scalars, f32[256,384]{1,0:T(8,128)S(1)} %get-tuple-element.129.near, f32[256,384]{1,0:T(8,128)S(1)} %collective-permute-done.16.far, f32[768,256]{1,0:T(8,128)S(1)} %copy-done, f32[768,256]{1,0:T(8,128)S(1)} %copy-done.1), custom_call_target="tpu_custom_call" | custom-call | flops 603979776 | bytes 1572864 | tf_op jit(solution)/shard_map/project/pallas_call | solution.py:118
  79.9 3.1 %far_slab_3.3 = (f32[256,384]{1,0:T(8,128)S(1)}, f32[256,384]{1,0:T(8,128)S(1)}) custom-call(s32[4]{0:T(128)S(1)} %pad_add_fusion.scalars, f32[256,384]{1,0:T(8,128)S(1)} %collective-permute-done.21.near.far, f32[256,384]{1,0:T(8,128)S(1)} %collective-permute-done.22.far.far_far, f32[3,256,768]{2,1,0:T(8,128)S(1)} %near_half.1.start, ...), custom_call_target="tpu_custom_call" | custom-call | flops 1811939328 | bytes 5505024 | tf_op jit(solution)/shard_map/far_slab_3/pallas_call | solution.py:118
  83.9 5.6 %collective-permute-done.19 = f32[128,256]{1,0:T(8,128)S(1)} collective-permute-done((f32[128,256]{1,0:T(8,128)S(1)}, f32[128,256]{1,0:T(8,128)S(1)}, u32[]{:S(2)}, u32[]{:S(2)}) %collective-permute-start.19) | collective-permute-done | bytes 131104 | tf_op jit(solution)/shard_map/ppermute | solution.py:313
  90.6 3.1 %far_slab_2.1 = (f32[256,384]{1,0:T(8,128)S(1)}, f32[256,384]{1,0:T(8,128)S(1)}) custom-call(s32[4]{0:T(128)S(1)} %pad_add_fusion.scalars, f32[256,384]{1,0:T(8,128)S(1)} %collective-permute-done.21.near.far, f32[256,384]{1,0:T(8,128)S(1)} %collective-permute-done.22.far.far_far, f32[3,256,768]{2,1,0:T(8,128)S(1)} %near_half.1.start, ...), custom_call_target="tpu_custom_call" | custom-call | flops 1811939328 | bytes 5505024 | tf_op jit(solution)/shard_map/far_slab_2/pallas_call | solution.py:118
  93.7 1.6 %collective-permute-start.27 = (f32[256,384]{1,0:T(8,128)S(1)}, f32[256,384]{1,0:T(8,128)S(1)}, u32[]{:S(2)}, u32[]{:S(2)}) collective-permute-start(f32[256,384]{1,0:T(8,128)S(1)} %get-tuple-element.103), channel_id=1, source_target_pairs={{0,1},{1,0},{2,3},{3,2},{4,5},{5,4},{6,7},{7,6},{8,9},{9,8},{10,11... | collective-permute-start | bytes 1179656 | tf_op jit(solution)/shard_map/ppermute | solution.py:313
  95.6 3.3 %far_slab_1.1 = (f32[256,384]{1,0:T(8,128)S(1)}, f32[256,384]{1,0:T(8,128)S(1)}) custom-call(s32[4]{0:T(128)S(1)} %pad_add_fusion.scalars, f32[256,384]{1,0:T(8,128)S(1)} %collective-permute-done.21.near.far, f32[256,384]{1,0:T(8,128)S(1)} %collective-permute-done.22.far.far_far, f32[3,256,768]{2,1,0:T(8,128)S(1)} %near_half.1.start, ...), custom_call_target="tpu_custom_call" | custom-call | flops 1811939328 | bytes 5505024 | tf_op jit(solution)/shard_map/far_slab_1/pallas_call | solution.py:118
  99.6 2.6 %collective-permute-start.24 = (f32[128,256]{1,0:T(8,128)S(1)}, f32[128,256]{1,0:T(8,128)S(1)}, u32[]{:S(2)}, u32[]{:S(2)}) collective-permute-start(f32[128,256]{1,0:T(8,128)S(1)} %add.110), channel_id=1, source_target_pairs={{0,4},{2,6},{4,0},{6,2},{1,5},{3,7},{5,1},{7,3},{8,12},{10,14},{12... | collective-permute-start | bytes 393224 | tf_op jit(solution)/shard_map/ppermute | solution.py:313
  102.1 5.0 %held_slab_0.1 = (f32[256,384]{1,0:T(8,128)S(1)}, f32[256,384]{1,0:T(8,128)S(1)}) custom-call(s32[4]{0:T(128)S(1)} %pad_add_fusion.scalars, f32[256,384]{1,0:T(8,128)S(1)} %get-tuple-element.129.near, f32[256,384]{1,0:T(8,128)S(1)} %collective-permute-done.17.far.near_far, f32[256,384]{1,0:T(8,128)S(1)} %collective-permute-done.21.near.far, ...), custom_call_target="tpu_custom_call" | custom-call | flops 3623878656 | bytes 11010048 | tf_op jit(solution)/shard_map/held_slab_0/pallas_call | solution.py:118
  108.1 1.7 %collective-permute-start.29 = (f32[256,384]{1,0:T(8,128)S(1)}, f32[256,384]{1,0:T(8,128)S(1)}, u32[]{:S(2)}, u32[]{:S(2)}) collective-permute-start(f32[256,384]{1,0:T(8,128)S(1)} %add_add_fusion), channel_id=1, source_target_pairs={{0,4},{2,6},{4,0},{6,2},{1,5},{3,7},{5,1},{7,3},{8,12},{10,14},{12... | collective-permute-start | bytes 1179656 | tf_op jit(solution)/shard_map/ppermute | solution.py:313
  109.8 2.5 %collective-permute-done.26 = f32[256,384]{1,0:T(8,128)S(1)} collective-permute-done((f32[256,384]{1,0:T(8,128)S(1)}, f32[256,384]{1,0:T(8,128)S(1)}, u32[]{:S(2)}, u32[]{:S(2)}) %collective-permute-start.26) | collective-permute-done | bytes 393248 | tf_op jit(solution)/shard_map/ppermute | solution.py:313
  113.0 1.6 %spread.3 = (f32[256,384]{1,0:T(8,128)S(1)}, f32[256,384]{1,0:T(8,128)S(1)}) custom-call(s32[4]{0:T(128)S(1)} %pad_add_fusion.scalars, f32[128,256]{1,0:T(8,128)S(1)} %add.111.near, f32[128,256]{1,0:T(8,128)S(1)} %collective-permute-done.25.far, f32[1,256]{1,0:T(1,128)S(1)} %bitcast.6, f32[768,256]{1,0:T(8,128)S(1)} %copy-done, f32[768,256]{1,0:T(8,128)S(1)} %copy-done.1, ...), custom_call_target="tpu_custom_call" | custom-call | flops 603979776 | bytes 1572864 | tf_op jit(solution)/shard_map/spread/pallas_call | solution.py:118
  114.6 1.6 %collective-permute-start.31 = (f32[256,384]{1,0:T(8,128)S(1)}, f32[256,384]{1,0:T(8,128)S(1)}, u32[]{:S(2)}, u32[]{:S(2)}) collective-permute-start(f32[256,384]{1,0:T(8,128)S(1)} %get-tuple-element.122), channel_id=1, source_target_pairs={{0,1},{1,0},{2,3},{3,2},{4,5},{5,4},{6,7},{7,6},{8,9},{9,8},{10,11... | collective-permute-start | bytes 1179656 | tf_op jit(solution)/shard_map/ppermute | solution.py:313
  116.1 12.2 %collective-permute-done.29 = f32[256,384]{1,0:T(8,128)S(1)} collective-permute-done((f32[256,384]{1,0:T(8,128)S(1)}, f32[256,384]{1,0:T(8,128)S(1)}, u32[]{:S(2)}, u32[]{:S(2)}) %collective-permute-start.29) | collective-permute-done | bytes 393248 | tf_op jit(solution)/shard_map/ppermute | solution.py:313
  128.5 1.4 %end.1 = (f32[384,128]{1,0:T(8,128)}, f32[384,128]{1,0:T(8,128)}) custom-call(s32[4]{0:T(128)S(1)} %pad_add_fusion.scalars, f32[256,384]{1,0:T(8,128)S(1)} %add.116.own, f32[256,384]{1,0:T(8,128)S(1)} %collective-permute-done.31.by_dev, f32[256,384]{1,0:T(8,128)S(1)} %get-tuple-element.128.iterate, f32[128,384]{1,0:T(8,128)S(1)} %get-tuple-element.63.bare, ...), custom_call_target="tpu_custom_call" | custom-call | bytes 3145728 | tf_op jit(solution)/shard_map/end/pallas_call | solution.py:118
  (91 shorter events, 16.8 us)
Async XLA Ops:
  2.6 4.7 %collective-permute-start.1 = (f32[128,384]{1,0:T(8,128)S(1)}, f32[128,384]{1,0:T(8,128)S(1)}, u32[]{:S(2)}, u32[]{:S(2)}) collective-permute-start(f32[128,384]{1,0:T(8,128)S(1)} %get-tuple-element.64.near), channel_id=1, source_target_pairs={{0,8},{8,0},{16,24},{24,16},{1,9},{9,1},{17,25},{25,17},{2,10},{10... | collective-permute-start | bytes 589832 | tf_op jit(solution)/shard_map/ppermute | solution.py:313
  3.1 8.6 %collective-permute-start.2 = (f32[128,384]{1,0:T(8,128)S(1)}, f32[128,384]{1,0:T(8,128)S(1)}, u32[]{:S(2)}, u32[]{:S(2)}) collective-permute-start(f32[128,384]{1,0:T(8,128)S(1)} %get-tuple-element.64.near), channel_id=1, source_target_pairs={{0,16},{8,24},{16,0},{24,8},{1,17},{9,25},{17,1},{25,9},{2,18},{10... | collective-permute-start | bytes 589832 | tf_op jit(solution)/shard_map/ppermute | solution.py:313
  5.7 7.0 %collective-permute-start = (f32[128,384]{1,0:T(8,128)S(1)}, f32[128,384]{1,0:T(8,128)S(1)}, u32[]{:S(2)}, u32[]{:S(2)}) collective-permute-start(f32[128,384]{1,0:T(8,128)S(1)} %get-tuple-element.64.near), channel_id=1, source_target_pairs={{0,1},{1,0},{2,3},{3,2},{4,5},{5,4},{6,7},{7,6},{8,9},{9,8},{10,11... | collective-permute-start | bytes 589832 | tf_op jit(solution)/shard_map/ppermute | solution.py:313
  11.8 1.5 %collective-permute-start.3 = (f32[128,384]{1,0:T(8,128)S(1)}, f32[128,384]{1,0:T(8,128)S(1)}, u32[]{:S(2)}, u32[]{:S(2)}) collective-permute-start(f32[128,384]{1,0:T(8,128)S(1)} %collective-permute-done.2.near.far), channel_id=1, source_target_pairs={{0,8},{8,0},{16,24},{24,16},{1,9},{9,1},{17,25},{25,17},{2,10},{10... | collective-permute-start | bytes 589832 | tf_op jit(solution)/shard_map/ppermute | solution.py:313
  15.3 11.9 %collective-permute-start.7 = (f32[256,384]{1,0:T(8,128)S(1)}, f32[256,384]{1,0:T(8,128)S(1)}, u32[]{:S(2)}, u32[]{:S(2)}) collective-permute-start(f32[256,384]{1,0:T(8,128)S(1)} %get-tuple-element.69), channel_id=1, source_target_pairs={{0,1},{1,0},{2,3},{3,2},{4,5},{5,4},{6,7},{7,6},{8,9},{9,8},{10,11... | collective-permute-start | bytes 1179656 | tf_op jit(solution)/shard_map/ppermute | solution.py:313
  17.7 1.4 %collective-permute-start.4 = (f32[128,256]{1,0:T(8,128)S(1)}, f32[128,256]{1,0:T(8,128)S(1)}, u32[]{:S(2)}, u32[]{:S(2)}) collective-permute-start(f32[128,256]{1,0:T(8,128)S(1)} %get-tuple-element.72), channel_id=1, source_target_pairs={{0,8},{8,0},{16,24},{24,16},{1,9},{9,1},{17,25},{25,17},{2,10},{10... | collective-permute-start | bytes 393224 | tf_op jit(solution)/shard_map/ppermute | solution.py:313
  19.2 8.0 %collective-permute-start.5 = (f32[128,256]{1,0:T(8,128)S(1)}, f32[128,256]{1,0:T(8,128)S(1)}, u32[]{:S(2)}, u32[]{:S(2)}) collective-permute-start(f32[128,256]{1,0:T(8,128)S(1)} %add.91), channel_id=1, source_target_pairs={{0,2},{2,0},{4,6},{6,4},{1,3},{3,1},{5,7},{7,5},{8,10},{10,8},{12,... | collective-permute-start | bytes 393224 | tf_op jit(solution)/shard_map/ppermute | solution.py:313
  26.2 18.5 %collective-permute-start.11 = (f32[256,384]{1,0:T(8,128)S(1)}, f32[256,384]{1,0:T(8,128)S(1)}, u32[]{:S(2)}, u32[]{:S(2)}) collective-permute-start(f32[256,384]{1,0:T(8,128)S(1)} %get-tuple-element.74), channel_id=1, source_target_pairs={{0,1},{1,0},{2,3},{3,2},{4,5},{5,4},{6,7},{7,6},{8,9},{9,8},{10,11... | collective-permute-start | bytes 1179656 | tf_op jit(solution)/shard_map/ppermute | solution.py:313
  27.2 17.5 %collective-permute-start.12 = (f32[256,384]{1,0:T(8,128)S(1)}, f32[256,384]{1,0:T(8,128)S(1)}, u32[]{:S(2)}, u32[]{:S(2)}) collective-permute-start(f32[256,384]{1,0:T(8,128)S(1)} %add.93), channel_id=1, source_target_pairs={{0,2},{2,0},{4,6},{6,4},{1,3},{3,1},{5,7},{7,5},{8,10},{10,8},{12,... | collective-permute-start | bytes 1179656 | tf_op jit(solution)/shard_map/ppermute | solution.py:313
  28.2 8.2 %collective-permute-start.6 = (f32[128,256]{1,0:T(8,128)S(1)}, f32[128,256]{1,0:T(8,128)S(1)}, u32[]{:S(2)}, u32[]{:S(2)}) collective-permute-start(f32[128,256]{1,0:T(8,128)S(1)} %add.92), channel_id=1, source_target_pairs={{0,16},{8,24},{16,0},{24,8},{1,17},{9,25},{17,1},{25,9},{2,18},{10... | collective-permute-start | bytes 393224 | tf_op jit(solution)/shard_map/ppermute | solution.py:313
  34.8 10.8 %collective-permute-start.10 = (f32[256,384]{1,0:T(8,128)S(1)}, f32[256,384]{1,0:T(8,128)S(1)}, u32[]{:S(2)}, u32[]{:S(2)}) collective-permute-start(f32[256,384]{1,0:T(8,128)S(1)} %get-tuple-element.78), channel_id=1, source_target_pairs={{0,1},{1,0},{2,3},{3,2},{4,5},{5,4},{6,7},{7,6},{8,9},{9,8},{10,11... | collective-permute-start | bytes 1179656 | tf_op jit(solution)/shard_map/ppermute | solution.py:313
  36.5 8.0 %collective-permute-start.8 = (f32[128,256]{1,0:T(8,128)S(1)}, f32[128,256]{1,0:T(8,128)S(1)}, u32[]{:S(2)}, u32[]{:S(2)}) collective-permute-start(f32[128,256]{1,0:T(8,128)S(1)} %add.94), channel_id=1, source_target_pairs={{0,4},{2,6},{4,0},{6,2},{1,5},{3,7},{5,1},{7,3},{8,12},{10,14},{12... | collective-permute-start | bytes 393224 | tf_op jit(solution)/shard_map/ppermute | solution.py:313
  44.4 4.2 %collective-permute-start.9 = (f32[128,256]{1,0:T(8,128)S(1)}, f32[128,256]{1,0:T(8,128)S(1)}, u32[]{:S(2)}, u32[]{:S(2)}) collective-permute-start(f32[128,256]{1,0:T(8,128)S(1)} %add.95.near), channel_id=1, source_target_pairs={{0,8},{8,0},{16,24},{24,16},{1,9},{9,1},{17,25},{25,17},{2,10},{10... | collective-permute-start | bytes 393224 | tf_op jit(solution)/shard_map/ppermute | solution.py:313
  44.8 21.0 %collective-permute-start.13 = (f32[256,384]{1,0:T(8,128)S(1)}, f32[256,384]{1,0:T(8,128)S(1)}, u32[]{:S(2)}, u32[]{:S(2)}) collective-permute-start(f32[256,384]{1,0:T(8,128)S(1)} %add_add_fusion.1), channel_id=1, source_target_pairs={{0,4},{2,6},{4,0},{6,2},{1,5},{3,7},{5,1},{7,3},{8,12},{10,14},{12... | collective-permute-start | bytes 1179656 | tf_op jit(solution)/shard_map/ppermute | solution.py:313
  45.7 20.2 %collective-permute-start.14 = (f32[256,384]{1,0:T(8,128)S(1)}, f32[256,384]{1,0:T(8,128)S(1)}, u32[]{:S(2)}, u32[]{:S(2)}) collective-permute-start(f32[256,384]{1,0:T(8,128)S(1)} %add.96), channel_id=1, source_target_pairs={{0,2},{2,0},{4,6},{6,4},{1,3},{3,1},{5,7},{7,5},{8,10},{10,8},{12,... | collective-permute-start | bytes 1179656 | tf_op jit(solution)/shard_map/ppermute | solution.py:313
  50.2 15.7 %collective-permute-start.15 = (f32[256,384]{1,0:T(8,128)S(1)}, f32[256,384]{1,0:T(8,128)S(1)}, u32[]{:S(2)}, u32[]{:S(2)}) collective-permute-start(f32[256,384]{1,0:T(8,128)S(1)} %get-tuple-element.90), channel_id=1, source_target_pairs={{0,1},{1,0},{2,3},{3,2},{4,5},{5,4},{6,7},{7,6},{8,9},{9,8},{10,11... | collective-permute-start | bytes 1179656 | tf_op jit(solution)/shard_map/ppermute | solution.py:313
  66.1 1.8 %collective-permute-start.17 = (f32[256,384]{1,0:T(8,128)S(1)}, f32[256,384]{1,0:T(8,128)S(1)}, u32[]{:S(2)}, u32[]{:S(2)}) collective-permute-start(f32[256,384]{1,0:T(8,128)S(1)} %get-tuple-element.129.near), channel_id=1, source_target_pairs={{0,8},{8,0},{16,24},{24,16},{1,9},{9,1},{17,25},{25,17},{2,10},{10... | collective-permute-start | bytes 1179656 | tf_op jit(solution)/shard_map/ppermute | solution.py:313
  66.2 11.5 %collective-permute-start.21 = (f32[256,384]{1,0:T(8,128)S(1)}, f32[256,384]{1,0:T(8,128)S(1)}, u32[]{:S(2)}, u32[]{:S(2)}) collective-permute-start(f32[256,384]{1,0:T(8,128)S(1)} %get-tuple-element.129.near), channel_id=1, source_target_pairs={{0,16},{8,24},{16,0},{24,8},{1,17},{9,25},{17,1},{25,9},{2,18},{10... | collective-permute-start | bytes 1179656 | tf_op jit(solution)/shard_map/ppermute | solution.py:313
  66.7 11.2 %collective-permute-start.16 = (f32[256,384]{1,0:T(8,128)S(1)}, f32[256,384]{1,0:T(8,128)S(1)}, u32[]{:S(2)}, u32[]{:S(2)}) collective-permute-start(f32[256,384]{1,0:T(8,128)S(1)} %get-tuple-element.129.near), channel_id=1, source_target_pairs={{0,1},{1,0},{2,3},{3,2},{4,5},{5,4},{6,7},{7,6},{8,9},{9,8},{10,11... | collective-permute-start | bytes 1179656 | tf_op jit(solution)/shard_map/ppermute | solution.py:313
  77.7 2.2 %collective-permute-start.22 = (f32[256,384]{1,0:T(8,128)S(1)}, f32[256,384]{1,0:T(8,128)S(1)}, u32[]{:S(2)}, u32[]{:S(2)}) collective-permute-start(f32[256,384]{1,0:T(8,128)S(1)} %collective-permute-done.21.near.far), channel_id=1, source_target_pairs={{0,8},{8,0},{16,24},{24,16},{1,9},{9,1},{17,25},{25,17},{2,10},{10... | collective-permute-start | bytes 1179656 | tf_op jit(solution)/shard_map/ppermute | solution.py:313
  79.5 4.3 %collective-permute-start.18 = (f32[128,256]{1,0:T(8,128)S(1)}, f32[128,256]{1,0:T(8,128)S(1)}, u32[]{:S(2)}, u32[]{:S(2)}) collective-permute-start(f32[128,256]{1,0:T(8,128)S(1)} %get-tuple-element.97), channel_id=1, source_target_pairs={{0,8},{8,0},{16,24},{24,16},{1,9},{9,1},{17,25},{25,17},{2,10},{10... | collective-permute-start | bytes 393224 | tf_op jit(solution)/shard_map/ppermute | solution.py:313
  83.0 12.3 %collective-permute-start.23 = (f32[256,384]{1,0:T(8,128)S(1)}, f32[256,384]{1,0:T(8,128)S(1)}, u32[]{:S(2)}, u32[]{:S(2)}) collective-permute-start(f32[256,384]{1,0:T(8,128)S(1)} %get-tuple-element.100), channel_id=1, source_target_pairs={{0,1},{1,0},{2,3},{3,2},{4,5},{5,4},{6,7},{7,6},{8,9},{9,8},{10,11... | collective-permute-start | bytes 1179656 | tf_op jit(solution)/shard_map/ppermute | solution.py:313
  83.8 5.7 %collective-permute-start.19 = (f32[128,256]{1,0:T(8,128)S(1)}, f32[128,256]{1,0:T(8,128)S(1)}, u32[]{:S(2)}, u32[]{:S(2)}) collective-permute-start(f32[128,256]{1,0:T(8,128)S(1)} %add.107), channel_id=1, source_target_pairs={{0,2},{2,0},{4,6},{6,4},{1,3},{3,1},{5,7},{7,5},{8,10},{10,8},{12,... | collective-permute-start | bytes 393224 | tf_op jit(solution)/shard_map/ppermute | solution.py:313
  89.5 10.0 %collective-permute-start.20 = (f32[128,256]{1,0:T(8,128)S(1)}, f32[128,256]{1,0:T(8,128)S(1)}, u32[]{:S(2)}, u32[]{:S(2)}) collective-permute-start(f32[128,256]{1,0:T(8,128)S(1)} %add.108), channel_id=1, source_target_pairs={{0,16},{8,24},{16,0},{24,8},{1,17},{9,25},{17,1},{25,9},{2,18},{10... | collective-permute-start | bytes 393224 | tf_op jit(solution)/shard_map/ppermute | solution.py:313
  93.7 13.6 %collective-permute-start.27 = (f32[256,384]{1,0:T(8,128)S(1)}, f32[256,384]{1,0:T(8,128)S(1)}, u32[]{:S(2)}, u32[]{:S(2)}) collective-permute-start(f32[256,384]{1,0:T(8,128)S(1)} %get-tuple-element.103), channel_id=1, source_target_pairs={{0,1},{1,0},{2,3},{3,2},{4,5},{5,4},{6,7},{7,6},{8,9},{9,8},{10,11... | collective-permute-start | bytes 1179656 | tf_op jit(solution)/shard_map/ppermute | solution.py:313
  95.3 12.7 %collective-permute-start.28 = (f32[256,384]{1,0:T(8,128)S(1)}, f32[256,384]{1,0:T(8,128)S(1)}, u32[]{:S(2)}, u32[]{:S(2)}) collective-permute-start(f32[256,384]{1,0:T(8,128)S(1)} %add.109), channel_id=1, source_target_pairs={{0,2},{2,0},{4,6},{6,4},{1,3},{3,1},{5,7},{7,5},{8,10},{10,8},{12,... | collective-permute-start | bytes 1179656 | tf_op jit(solution)/shard_map/ppermute | solution.py:313
  99.0 13.3 %collective-permute-start.26 = (f32[256,384]{1,0:T(8,128)S(1)}, f32[256,384]{1,0:T(8,128)S(1)}, u32[]{:S(2)}, u32[]{:S(2)}) collective-permute-start(f32[256,384]{1,0:T(8,128)S(1)} %get-tuple-element.108), channel_id=1, source_target_pairs={{0,1},{1,0},{2,3},{3,2},{4,5},{5,4},{6,7},{7,6},{8,9},{9,8},{10,11... | collective-permute-start | bytes 1179656 | tf_op jit(solution)/shard_map/ppermute | solution.py:313
  99.6 7.5 %collective-permute-start.24 = (f32[128,256]{1,0:T(8,128)S(1)}, f32[128,256]{1,0:T(8,128)S(1)}, u32[]{:S(2)}, u32[]{:S(2)}) collective-permute-start(f32[128,256]{1,0:T(8,128)S(1)} %add.110), channel_id=1, source_target_pairs={{0,4},{2,6},{4,0},{6,2},{1,5},{3,7},{5,1},{7,3},{8,12},{10,14},{12... | collective-permute-start | bytes 393224 | tf_op jit(solution)/shard_map/ppermute | solution.py:313
  107.1 5.9 %collective-permute-start.25 = (f32[128,256]{1,0:T(8,128)S(1)}, f32[128,256]{1,0:T(8,128)S(1)}, u32[]{:S(2)}, u32[]{:S(2)}) collective-permute-start(f32[128,256]{1,0:T(8,128)S(1)} %add.111.near), channel_id=1, source_target_pairs={{0,8},{8,0},{16,24},{24,16},{1,9},{9,1},{17,25},{25,17},{2,10},{10... | collective-permute-start | bytes 393224 | tf_op jit(solution)/shard_map/ppermute | solution.py:313
  108.1 20.2 %collective-permute-start.29 = (f32[256,384]{1,0:T(8,128)S(1)}, f32[256,384]{1,0:T(8,128)S(1)}, u32[]{:S(2)}, u32[]{:S(2)}) collective-permute-start(f32[256,384]{1,0:T(8,128)S(1)} %add_add_fusion), channel_id=1, source_target_pairs={{0,4},{2,6},{4,0},{6,2},{1,5},{3,7},{5,1},{7,3},{8,12},{10,14},{12... | collective-permute-start | bytes 1179656 | tf_op jit(solution)/shard_map/ppermute | solution.py:313
  112.3 16.1 %collective-permute-start.30 = (f32[256,384]{1,0:T(8,128)S(1)}, f32[256,384]{1,0:T(8,128)S(1)}, u32[]{:S(2)}, u32[]{:S(2)}) collective-permute-start(f32[256,384]{1,0:T(8,128)S(1)} %add.112), channel_id=1, source_target_pairs={{0,2},{2,0},{4,6},{6,4},{1,3},{3,1},{5,7},{7,5},{8,10},{10,8},{12,... | collective-permute-start | bytes 1179656 | tf_op jit(solution)/shard_map/ppermute | solution.py:313
  114.6 13.9 %collective-permute-start.31 = (f32[256,384]{1,0:T(8,128)S(1)}, f32[256,384]{1,0:T(8,128)S(1)}, u32[]{:S(2)}, u32[]{:S(2)}) collective-permute-start(f32[256,384]{1,0:T(8,128)S(1)} %get-tuple-element.122), channel_id=1, source_target_pairs={{0,1},{1,0},{2,3},{3,2},{4,5},{5,4},{6,7},{7,6},{8,9},{9,8},{10,11... | collective-permute-start | bytes 1179656 | tf_op jit(solution)/shard_map/ppermute | solution.py:313
  (9 other events, 57.3 us)
